TPU v7x, 32 devices: a whole 2x2x4 slice. The times are simulated.
32 devices in a mesh: dp: 4 (over x, core), fsdp: 8 (over z, y).
Axes of the slice: x: 2, y: 2, z: 4, core: 2. Of those that a mesh axis runs over, the one named last changes fastest.
Arguments:
- frames: bfloat16 [51200, 640], P(('dp', 'fsdp')), may hold values from -6 to 6
- cotangent: bfloat16 [51200, 640], P(('dp', 'fsdp')), may hold values from -6 to 6
- span_starts: int32 [128, 32], P(('dp', 'fsdp')), may hold values from 0 to 390
- query_weight: bfloat16 [768, 768], P('fsdp'), may hold values from -0.25 to 0.25
- key_weight: bfloat16 [768, 768], P('fsdp'), may hold values from -0.25 to 0.25
- value_weight: bfloat16 [768, 768], P('fsdp'), may hold values from -0.25 to 0.25
- out_weight: bfloat16 [768, 768], P('fsdp'), may hold values from -3 to 3
- query_bias: bfloat16 [768], P('fsdp'), may hold values from -2.390625 to 2.390625
- value_bias: bfloat16 [768], P('fsdp'), may hold values from -2.390625 to 2.390625
- out_bias: bfloat16 [768], P('fsdp'), may hold values from -2.390625 to 2.390625
- first_gain: bfloat16 [768], P('fsdp'), may hold values from 0.3984375 to 1.59375
- first_shift: bfloat16 [768], P('fsdp'), may hold values from -2.390625 to 2.390625
- up_weight: bfloat16 [768, 3072], P('fsdp'), may hold values from -0.25 to 0.25
- up_bias: bfloat16 [3072], P('fsdp'), may hold values from -2.390625 to 2.390625
- down_weight: bfloat16 [3072, 768], P('fsdp'), may hold values from -0.15625 to 0.15625
- down_bias: bfloat16 [768], P('fsdp'), may hold values from -2.390625 to 2.390625
- second_gain: bfloat16 [768], P('fsdp'), may hold values from 0.3984375 to 1.59375
- second_shift: bfloat16 [768], P('fsdp'), may hold values from -2.390625 to 2.390625
- mask_vector: bfloat16 [768], P('fsdp'), may hold values from -5 to 5
Outputs:
- output: bfloat16 [51200, 640], P(('dp', 'fsdp'))
- frames_grad: bfloat16 [51200, 640], P(('dp', 'fsdp'))
- query_weight_grad: float32 [768, 768], P('fsdp')
- key_weight_grad: float32 [768, 768], P('fsdp')
- value_weight_grad: float32 [768, 768], P('fsdp')
- out_weight_grad: float32 [768, 768], P('fsdp')
- query_bias_grad: float32 [768], P('fsdp')
- value_bias_grad: float32 [768], P('fsdp')
- out_bias_grad: float32 [768], P('fsdp')
- first_gain_grad: float32 [768], P('fsdp')
- first_shift_grad: float32 [768], P('fsdp')
- up_weight_grad: float32 [768, 3072], P('fsdp')
- up_bias_grad: float32 [3072], P('fsdp')
- down_weight_grad: float32 [3072, 768], P('fsdp')
- down_bias_grad: float32 [768], P('fsdp')
- second_gain_grad: float32 [768], P('fsdp')
- second_shift_grad: float32 [768], P('fsdp')
- mask_vector_grad: float32 [768], P('fsdp')
Inputs may be any that keep to these rules, and one draw needn't show every extreme that they name: `span_starts`: first frame of a masked span of 10 frames within its utterance; spans may intersect.
All inputs are finite; a program needn't handle non-finite values.
Results may differ from a plain program's by a relative error of at most 0.015.
Values may be sent and summed in bfloat16 or wider, within the bound.
No kernel may reach another device: no remote copies, remote signals or barrier semaphores. Data moves between devices by JAX's collectives and lax.ppermute only.
A program may use at most 256 MiB of HBM per device.

v0:
```python
import jax
import jax.numpy as jnp
from jax import lax
from jax.sharding import PartitionSpec as P

HEADS = 10
HEAD_DIM = 64
FF = 2560
D = 640
FRAMES = 400
SPAN = 10


epsilon = 1e-05


def matmul(left, right):
    return jnp.dot(left, right, preferred_element_type=jnp.float32)


def matmul_nt(left, right):
    return lax.dot_general(
        left, right, (((1,), (1,)), ((), ())), preferred_element_type=jnp.float32
    )


def matmul_tn(left, right):
    return lax.dot_general(
        left, right, (((0,), (0,)), ((), ())), preferred_element_type=jnp.float32
    )


def layer_norm(value, gain, shift):
    center = value - jnp.mean(value, axis=-1, keepdims=True)
    spread = jnp.mean(center * center, axis=-1, keepdims=True)
    return center * lax.rsqrt(spread + epsilon) * gain + shift


def gelu_exact(value):
    return jax.nn.gelu(value, approximate=False)


def span_mask(starts):
    places = jnp.arange(FRAMES, dtype=jnp.int32)[None, :, None]
    inside = (places >= starts[:, None, :]) & (places < starts[:, None, :] + SPAN)
    return jnp.any(inside, axis=2)


def widen(grad, full_shape):
    return jnp.pad(grad, [(0, whole - part) for whole, part in zip(full_shape, grad.shape)])


def column_sum(value):
    return jnp.sum(value, axis=0, dtype=jnp.float32)


def cut_attn(gathered):
    query_w, key_w, value_w, out_w, query_b, value_b, out_b, gain_one, shift_one, mask_vec = (
        gathered
    )
    return (
        query_w[:D, :D],
        key_w[:D, :D],
        value_w[:D, :D],
        out_w[:D, :D],
        query_b[:D].astype(jnp.float32),
        value_b[:D].astype(jnp.float32),
        out_b[:D].astype(jnp.float32),
        gain_one[:D].astype(jnp.float32),
        shift_one[:D].astype(jnp.float32),
        mask_vec[:D].astype(jnp.float32),
    )


def cut_ffn(gathered):
    up_w, up_b, down_w, down_b, gain_two, shift_two = gathered
    return (
        up_w[:D, :FF],
        up_b[:FF].astype(jnp.float32),
        down_w[:FF, :D],
        down_b[:D].astype(jnp.float32),
        gain_two[:D].astype(jnp.float32),
        shift_two[:D].astype(jnp.float32),
    )


def on_device(
    frames,
    cotangent,
    span_starts,
    query_weight,
    key_weight,
    value_weight,
    out_weight,
    query_bias,
    value_bias,
    out_bias,
    first_gain,
    first_shift,
    up_weight,
    up_bias,
    down_weight,
    down_bias,
    second_gain,
    second_shift,
    mask_vector,
):
    attn_full = (
        lax.all_gather(query_weight, "fsdp", axis=0, tiled=True),
        lax.all_gather(key_weight, "fsdp", axis=0, tiled=True),
        lax.all_gather(value_weight, "fsdp", axis=0, tiled=True),
        lax.all_gather(out_weight, "fsdp", axis=0, tiled=True),
        lax.all_gather(query_bias, "fsdp", axis=0, tiled=True),
        lax.all_gather(value_bias, "fsdp", axis=0, tiled=True),
        lax.all_gather(out_bias, "fsdp", axis=0, tiled=True),
        lax.all_gather(first_gain, "fsdp", axis=0, tiled=True),
        lax.all_gather(first_shift, "fsdp", axis=0, tiled=True),
        lax.all_gather(mask_vector, "fsdp", axis=0, tiled=True),
    )
    attn_shapes = [piece.shape for piece in attn_full]
    query_w, key_w, value_w, out_w, query_b, value_b, out_b, gain_one, shift_one, mask_vec = (
        cut_attn(attn_full)
    )
    total_rows = frames.shape[0]
    utters = total_rows // FRAMES
    scale = HEAD_DIM ** (-0.5)
    masked = span_mask(span_starts).reshape(total_rows, 1)
    start_rows = jnp.where(masked, mask_vec[None, :], frames.astype(jnp.float32))
    start_low = start_rows.astype(jnp.bfloat16)
    query_rows = (matmul(start_low, query_w) + query_b).astype(jnp.bfloat16)
    key_rows = matmul(start_low, key_w).astype(jnp.bfloat16)
    value_rows = (matmul(start_low, value_w) + value_b).astype(jnp.bfloat16)
    query_heads = query_rows.reshape(utters, FRAMES, HEADS, HEAD_DIM)
    key_heads = key_rows.reshape(utters, FRAMES, HEADS, HEAD_DIM)
    value_heads = value_rows.reshape(utters, FRAMES, HEADS, HEAD_DIM)
    scores = (
        jnp.einsum("bqhd,bkhd->bhqk", query_heads, key_heads, preferred_element_type=jnp.float32)
        * scale
    )
    top = jnp.max(scores, axis=-1, keepdims=True)
    expo = jnp.exp(scores - top)
    total = jnp.sum(expo, axis=-1, keepdims=True)
    log_total = top + jnp.log(total)
    attn_prob = (expo / total).astype(jnp.bfloat16)
    mixed = jnp.einsum(
        "bhqk,bkhd->bqhd", attn_prob, value_heads, preferred_element_type=jnp.float32
    )
    mixed = mixed.reshape(total_rows, D).astype(jnp.bfloat16)
    branch_one = matmul(mixed, out_w) + out_b
    first_out, first_pull = jax.vjp(layer_norm, start_rows + branch_one, gain_one, shift_one)
    ffn_full = (
        lax.all_gather(up_weight, "fsdp", axis=0, tiled=True),
        lax.all_gather(up_bias, "fsdp", axis=0, tiled=True),
        lax.all_gather(down_weight, "fsdp", axis=0, tiled=True),
        lax.all_gather(down_bias, "fsdp", axis=0, tiled=True),
        lax.all_gather(second_gain, "fsdp", axis=0, tiled=True),
        lax.all_gather(second_shift, "fsdp", axis=0, tiled=True),
    )
    ffn_shapes = [piece.shape for piece in ffn_full]
    up_w, up_b, down_w, down_b, gain_two, shift_two = cut_ffn(ffn_full)
    first_low = first_out.astype(jnp.bfloat16)
    hidden_pre = matmul(first_low, up_w) + up_b
    hidden_act, gelu_pull = jax.vjp(gelu_exact, hidden_pre)
    hidden_low = hidden_act.astype(jnp.bfloat16)
    branch_two = matmul(hidden_low, down_w) + down_b
    result, second_pull = jax.vjp(layer_norm, first_out + branch_two, gain_two, shift_two)
    grad_two, grad_gain_two, grad_shift_two = second_pull(cotangent.astype(jnp.float32))
    grad_branch = grad_two.astype(jnp.bfloat16)
    ffn_back = cut_ffn(
        (
            lax.all_gather(up_weight, "fsdp", axis=0, tiled=True),
            lax.all_gather(up_bias, "fsdp", axis=0, tiled=True),
            lax.all_gather(down_weight, "fsdp", axis=0, tiled=True),
            lax.all_gather(down_bias, "fsdp", axis=0, tiled=True),
            lax.all_gather(second_gain, "fsdp", axis=0, tiled=True),
            lax.all_gather(second_shift, "fsdp", axis=0, tiled=True),
        )
    )
    up_w = ffn_back[0]
    down_w = ffn_back[2]
    grad_hidden = matmul_nt(grad_branch, down_w)
    (grad_pre,) = gelu_pull(grad_hidden)
    grad_pre_low = grad_pre.astype(jnp.bfloat16)
    grad_first = matmul_nt(grad_pre_low, up_w) + grad_two
    ffn_grads = (
        widen(matmul_tn(first_low, grad_pre_low), ffn_shapes[0]),
        widen(column_sum(grad_pre_low), ffn_shapes[1]),
        widen(matmul_tn(hidden_low, grad_branch), ffn_shapes[2]),
        widen(column_sum(grad_branch), ffn_shapes[3]),
        widen(grad_gain_two, ffn_shapes[4]),
        widen(grad_shift_two, ffn_shapes[5]),
    )
    grad_res, grad_gain_one, grad_shift_one = first_pull(grad_first)
    grad_attn_out = grad_res.astype(jnp.bfloat16)
    attn_back = cut_attn(
        (
            lax.all_gather(query_weight, "fsdp", axis=0, tiled=True),
            lax.all_gather(key_weight, "fsdp", axis=0, tiled=True),
            lax.all_gather(value_weight, "fsdp", axis=0, tiled=True),
            lax.all_gather(out_weight, "fsdp", axis=0, tiled=True),
            lax.all_gather(query_bias, "fsdp", axis=0, tiled=True),
            lax.all_gather(value_bias, "fsdp", axis=0, tiled=True),
            lax.all_gather(out_bias, "fsdp", axis=0, tiled=True),
            lax.all_gather(first_gain, "fsdp", axis=0, tiled=True),
            lax.all_gather(first_shift, "fsdp", axis=0, tiled=True),
            lax.all_gather(mask_vector, "fsdp", axis=0, tiled=True),
        )
    )
    query_w = attn_back[0]
    key_w = attn_back[1]
    value_w = attn_back[2]
    out_w = attn_back[3]
    grad_mixed = matmul_nt(grad_attn_out, out_w).astype(jnp.bfloat16)
    grad_mixed_heads = grad_mixed.reshape(utters, FRAMES, HEADS, HEAD_DIM)
    scores_again = (
        jnp.einsum("bqhd,bkhd->bhqk", query_heads, key_heads, preferred_element_type=jnp.float32)
        * scale
    )
    prob_again = jnp.exp(scores_again - log_total)
    grad_prob = jnp.einsum(
        "bqhd,bkhd->bhqk", grad_mixed_heads, value_heads, preferred_element_type=jnp.float32
    )
    grad_value = jnp.einsum(
        "bhqk,bqhd->bkhd",
        prob_again.astype(jnp.bfloat16),
        grad_mixed_heads,
        preferred_element_type=jnp.float32,
    )
    grad_value = grad_value.reshape(total_rows, D).astype(jnp.bfloat16)
    grad_scores = (
        prob_again * (grad_prob - jnp.sum(grad_prob * prob_again, axis=-1, keepdims=True))
    ).astype(jnp.bfloat16)
    grad_query = (
        jnp.einsum("bhqk,bkhd->bqhd", grad_scores, key_heads, preferred_element_type=jnp.float32)
        * scale
    )
    grad_query = grad_query.reshape(total_rows, D).astype(jnp.bfloat16)
    grad_key = (
        jnp.einsum("bhqk,bqhd->bkhd", grad_scores, query_heads, preferred_element_type=jnp.float32)
        * scale
    )
    grad_key = grad_key.reshape(total_rows, D).astype(jnp.bfloat16)
    grad_start = (
        matmul_nt(grad_query, query_w)
        + matmul_nt(grad_key, key_w)
        + matmul_nt(grad_value, value_w)
        + grad_res
    )
    frames_grad = jnp.where(masked, 0.0, grad_start).astype(jnp.bfloat16)
    grad_mask = jnp.sum(jnp.where(masked, grad_start, 0.0), axis=0)
    attn_grads = (
        widen(matmul_tn(start_low, grad_query), attn_shapes[0]),
        widen(matmul_tn(start_low, grad_key), attn_shapes[1]),
        widen(matmul_tn(start_low, grad_value), attn_shapes[2]),
        widen(matmul_tn(mixed, grad_attn_out), attn_shapes[3]),
        widen(column_sum(grad_query), attn_shapes[4]),
        widen(column_sum(grad_value), attn_shapes[5]),
        widen(column_sum(grad_attn_out), attn_shapes[6]),
        widen(grad_gain_one, attn_shapes[7]),
        widen(grad_shift_one, attn_shapes[8]),
        widen(grad_mask, attn_shapes[9]),
    )
    summed = lax.psum(
        (
            lax.psum_scatter(attn_grads[0], "fsdp", scatter_dimension=0, tiled=True),
            lax.psum_scatter(attn_grads[1], "fsdp", scatter_dimension=0, tiled=True),
            lax.psum_scatter(attn_grads[2], "fsdp", scatter_dimension=0, tiled=True),
            lax.psum_scatter(attn_grads[3], "fsdp", scatter_dimension=0, tiled=True),
            lax.psum_scatter(attn_grads[4], "fsdp", scatter_dimension=0, tiled=True),
            lax.psum_scatter(attn_grads[5], "fsdp", scatter_dimension=0, tiled=True),
            lax.psum_scatter(attn_grads[6], "fsdp", scatter_dimension=0, tiled=True),
            lax.psum_scatter(attn_grads[7], "fsdp", scatter_dimension=0, tiled=True),
            lax.psum_scatter(attn_grads[8], "fsdp", scatter_dimension=0, tiled=True),
            lax.psum_scatter(attn_grads[9], "fsdp", scatter_dimension=0, tiled=True),
            lax.psum_scatter(ffn_grads[0], "fsdp", scatter_dimension=0, tiled=True),
            lax.psum_scatter(ffn_grads[1], "fsdp", scatter_dimension=0, tiled=True),
            lax.psum_scatter(ffn_grads[2], "fsdp", scatter_dimension=0, tiled=True),
            lax.psum_scatter(ffn_grads[3], "fsdp", scatter_dimension=0, tiled=True),
            lax.psum_scatter(ffn_grads[4], "fsdp", scatter_dimension=0, tiled=True),
            lax.psum_scatter(ffn_grads[5], "fsdp", scatter_dimension=0, tiled=True),
        ),
        "dp",
    )
    attn_sums = summed[:10]
    ffn_sums = summed[10:]
    attn_sums = [piece for piece in attn_sums]
    ffn_sums = [piece for piece in ffn_sums]
    return (
        result.astype(jnp.bfloat16),
        frames_grad,
        attn_sums[0],
        attn_sums[1],
        attn_sums[2],
        attn_sums[3],
        attn_sums[4],
        attn_sums[5],
        attn_sums[6],
        attn_sums[7],
        attn_sums[8],
        ffn_sums[0],
        ffn_sums[1],
        ffn_sums[2],
        ffn_sums[3],
        ffn_sums[4],
        ffn_sums[5],
        attn_sums[9],
    )


def solution(mesh):
    return jax.shard_map(
        on_device,
        mesh=mesh,
        in_specs=(
            P(("dp", "fsdp"), None),
            P(("dp", "fsdp"), None),
            P(("dp", "fsdp"), None),
            P("fsdp", None),
            P("fsdp", None),
            P("fsdp", None),
            P("fsdp", None),
            P("fsdp"),
            P("fsdp"),
            P("fsdp"),
            P("fsdp"),
            P("fsdp"),
            P("fsdp", None),
            P("fsdp"),
            P("fsdp", None),
            P("fsdp"),
            P("fsdp"),
            P("fsdp"),
            P("fsdp"),
        ),
        out_specs=(
            P(("dp", "fsdp"), None),
            P(("dp", "fsdp"), None),
            P("fsdp", None),
            P("fsdp", None),
            P("fsdp", None),
            P("fsdp", None),
            P("fsdp"),
            P("fsdp"),
            P("fsdp"),
            P("fsdp"),
            P("fsdp"),
            P("fsdp", None),
            P("fsdp"),
            P("fsdp", None),
            P("fsdp"),
            P("fsdp"),
            P("fsdp"),
            P("fsdp"),
        ),
        check_vma=False,
    )
```

profile of v0, /device:TPU:0, one launch (start us, length us, event | category | flops | bytes accessed | tf_op | source)
XLA Modules:
  0.0 1117.4 jit_solution(11925511347061986627)
XLA Ops:
  23.0 39.2 %all-reduce.38 = (bf16[768]{0:T(1024)(128)(2,1)S(1)}, bf16[768]{0:T(1024)(128)(2,1)S(1)}, bf16[768]{0:T(1024)(128)(2,1)S(1)}, bf16[768]{0:T(1024)(128)(2,1)S(1)}...) all-reduce(bf16[768]{0:T(1024)(128)(2,1)S(1)} %dynamic-update-slice, ...), channel_id=1, replica_groups=mesh['dp'=4,'fsdp'=8] {'fsdp'}, use_global_device_ids=true, to_apply=%add.16 | all-reduce | flops 6912 | bytes 27648
  62.2 25.9 %all-gather = bf16[8,1,384]{2,1,0:T(2,128)(2,1)S(1)} all-gather(bf16[1,1,384]{2,1,0:T(2,128)(2,1)S(1)} %reshape.175), channel_id=1, replica_groups=mesh['dp'=4,'fsdp'=8] {'fsdp'}, dimensions={0}, use_global_device_ids=true | all-gather | bytes 6912 | tf_op jit(solution)/shard_map/all_gather | solution.py:153
  89.5 5.1 add_convert_fusion.3
  94.6 3.3 copy.89
  97.8 4.8 reshape.144
  102.6 5.1 add_convert_fusion.2
  107.8 3.1 copy.90
  110.9 4.8 reshape.145
  115.7 22.4 %all-gather.12.cloned.1.call-done = bf16[768,768]{1,0:T(8,128)(2,1)} async-done(((bf16[96,768]{1,0:T(8,128)(2,1)}), bf16[768,768]{1,0:T(8,128)(2,1)}) %all-gather.12.cloned.1.call-update) | async-done | bytes 1179664 | tf_op jit(solution)/shard_map/all_gather | solution.py:110
  138.1 3.8 convolution_convert_fusion.1
  141.9 2.6 copy.91
  144.5 7.9 reshape.146
  152.4 15.5 %multiply_reduce_fusion.1 = (f32[4,10,400]{2,1,0:T(8,128)S(1)}, f32[4,10,400,400]{2,3,1,0:T(8,128)}) fusion(bf16[4,400,10,64]{1,0,3,2:T(4,128)(2,1)S(1)} %reshape.146, bf16[4,400,10,64]{1,0,3,2:T(4,128)(2,1)} %reshape.145), kind=kOutput, calls=%fused_computation.6 | convolution fusion | flops 831984000 | bytes 29760000 | tf_op jit(solution)/shard_map/bqhd,bkhd->bhqk/dot_general | solution.py:137
  167.9 14.1 %fusion = f32[4,10,400]{2,1,0:T(8,128)S(1)} fusion(f32[4,10,400,400]{2,3,1,0:T(8,128)} %get-tuple-element.73, f32[4,10,400]{2,1,0:T(8,128)S(1)} %get-tuple-element.72), kind=kLoop, calls=%fused_computation.5 | loop fusion | flops 19184000 | bytes 25728000 | tf_op jit(solution)/shard_map/reduce_sum | solution.py:142
  182.0 16.0 %convert_bitcast_fusion = bf16[4,400,10,64]{1,3,2,0:T(8,128)(2,1)} fusion(f32[4,10,400,400]{2,3,1,0:T(8,128)} %get-tuple-element.73, f32[4,10,400]{2,1,0:T(8,128)S(1)} %fusion, f32[4,10,400]{2,1,0:T(8,128)S(1)} %get-tuple-element.72, bf16[4,400,10,64]{1,0,3,2:T(4,128)(2,1)S(1)} %copy-done.8), kind=kOutput, calls=%fused_computation.72 | convolution fusion | flops 845824000 | bytes 29824000 | tf_op jit(solution)/shard_map/bhqk,bkhd->bqhd/dot_general | solution.py:145
  198.0 3.8 copy.96
  201.8 3.5 convert_element_type.172
  205.3 5.1 fusion.80
  210.4 1.9 copy-done.5
  213.6 47.1 %all-gather.16.cloned.1.call-done = bf16[768,3072]{1,0:T(8,128)(2,1)} async-done(((bf16[96,3072]{1,0:T(8,128)(2,1)}), bf16[768,3072]{1,0:T(8,128)(2,1)}) %all-gather.16.cloned.1.call-update) | async-done | bytes 4718608 | tf_op jit(solution)/shard_map/all_gather | solution.py:152
  260.7 46.6 %multiply_convert_fusion.1 = (bf16[1600,2560]{1,0:T(8,128)(2,1)}, f32[1600,2560]{1,0:T(8,128)}, f32[1600,2560]{1,0:T(8,128)}) fusion(f32[2560]{0:T(1024)S(1)} %slice_convert_fusion, bf16[768,3072]{1,0:T(8,128)(2,1)} %all-gather.16.cloned.1.call-done, f32[1600,640]{1,0:T(8,128)} %copy-done.5, f32[640]{0:T(1024)S(1)} %get-tuple-element.93, ...), kind=kOutput, calls=%fused_computation.14 | convolution fusion | flops 5518336000 | bytes 48360960 | tf_op jit(solution)/shard_map/dot_general | solution.py:18
  307.3 33.5 %all-gather.18.cloned.1.call-done = bf16[3072,768]{1,0:T(8,128)(2,1)} async-done(((bf16[384,768]{1,0:T(8,128)(2,1)}), bf16[3072,768]{1,0:T(8,128)(2,1)}) %all-gather.18.cloned.1.call-update) | async-done | bytes 4718608 | tf_op jit(solution)/shard_map/all_gather | solution.py:154
  340.8 12.8 %fusion.81 = (f32[1600]{0:T(1024)S(1)}, f32[1600,640]{1,0:T(8,128)S(1)}) fusion(f32[640]{0:T(1024)S(1)} %copy-done.34, bf16[1600,2560]{1,0:T(8,128)(2,1)} %get-tuple-element.67, bf16[3072,768]{1,0:T(8,128)(2,1)} %all-gather.18.cloned.1.call-done, f32[640]{0:T(1024)S(1)} %get-tuple-element.93, f32[640]{0:T(1024)S(1)} %slice_convert_fusion.5, ...), kind=kOutput, calls=%fused_computation.132 | convolution fusion | flops 5250046464 | bytes 19687680 | tf_op jit(solution)/shard_map/dot_general | solution.py:18
  355.2 2.1 fusion.16
  357.3 3.1 fusion.77
  360.5 1.9 copy-done.7
  363.4 21.9 %convert_reduce_fusion = (f32[2560]{0:T(1024)}, bf16[1600,2560]{1,0:T(8,128)(2,1)}) fusion(f32[1600,2560]{1,0:T(8,128)} %get-tuple-element.68, bf16[1600,640]{1,0:T(8,128)(2,1)S(1)} %get-tuple-element.60, bf16[3072,768]{1,0:T(8,128)(2,1)} %all-gather.18.cloned.1.call-done, f32[1600,2560]{1,0:T(8,128)} %get-tuple-element.76, f32[2560]{0:T(1024)S(1)} %slice_convert_fusion), kind=kOutput, calls=%fused_computation.11 | convolution fusion | flops 5312509440 | bytes 46305280 | tf_op jit(solution)/shard_map/dot_general | solution.py:22
  385.4 14.5 %multiply_reduce_fusion.2 = (f32[640]{0:T(1024)S(1)}, f32[1600]{0:T(1024)S(1)}, f32[640]{0:T(1024)S(1)}, f32[1600,640]{1,0:T(8,128)S(1)}) fusion(f32[1600,640]{1,0:T(8,128)} %copy-done.5, f32[1600]{0:T(1024)S(1)} %fusion.60, f32[1600]{0:T(1024)S(1)} %broadcast_multiply_fusion.1, f32[640]{0:T(1024)S(1)} %slice_convert_fusion.5, f32[1600,640]{1,0:T(8,128)} %copy-done.7, ...), kind=kOutput, calls=%fused_computation.45 | convolution fusion | flops 5253117440 | bytes 23790080 | tf_op jit(solution)/shard_map/dot_general | solution.py:22
  402.1 2.7 copy-done.12
  404.8 1.9 fusion.82
  408.5 3.7 convolution_convert_fusion
  412.2 2.8 copy.97
  415.0 7.9 reshape.147
  422.9 15.7 %convert_reduce_fusion.2 = (f32[10,64]{1,0:T(8,128)S(1)}, bf16[4,10,64,400]{3,2,1,0:T(8,128)(2,1)}) fusion(f32[4,10,400,400]{2,3,1,0:T(8,128)} %get-tuple-element.73, f32[4,10,400]{2,1,0:T(8,128)S(1)} %log_add_fusion, bf16[4,400,10,64]{1,0,3,2:T(4,128)(2,1)S(1)} %reshape.147), kind=kOutput, calls=%fused_computation.35 | convolution fusion | flops 841471360 | bytes 29762560 | tf_op jit(solution)/shard_map/bhqk,bqhd->bkhd/dot_general | solution.py:223
  438.6 5.4 copy.108
  443.9 6.0 convert_element_type.198
  449.9 4.6 fusion.67
  456.1 25.4 %multiply_reduce_fusion = (f32[4,10,400]{2,1,0:T(8,128)S(1)}, f32[4,10,400,400]{2,3,1,0:T(8,128)}) fusion(f32[4,10,400,400]{2,3,1,0:T(8,128)} %get-tuple-element.73, f32[4,10,400]{2,1,0:T(8,128)S(1)} %log_add_fusion, bf16[4,400,10,64]{1,0,3,2:T(4,128)(2,1)} %reshape.144, bf16[4,400,10,64]{1,0,3,2:T(4,128)(2,1)S(1)} %reshape.147), kind=kOutput, calls=%fused_computation.1 | convolution fusion | flops 844784000 | bytes 55424000 | tf_op jit(solution)/shard_map/bqhd,bkhd->bhqk/dot_general | solution.py:220
  481.6 28.0 %multiply_convert_fusion = bf16[4,10,400,400]{2,3,1,0:T(8,128)(2,1)} fusion(f32[4,10,400,400]{2,3,1,0:T(8,128)} %get-tuple-element.81, f32[4,10,400,400]{2,3,1,0:T(8,128)} %get-tuple-element.73, f32[4,10,400]{2,1,0:T(8,128)S(1)} %get-tuple-element.80, f32[4,10,400]{2,1,0:T(8,128)S(1)} %log_add_fusion), kind=kLoop, calls=%fused_computation | loop fusion | flops 32000000 | bytes 64128000 | tf_op jit(solution)/shard_map/convert_element_type | solution.py:232
  509.6 8.7 fusion.24
  518.3 2.0 copy.105
  520.4 3.5 convert_element_type.194
  523.8 4.6 fusion.69
  531.1 9.0 convert_reduce_fusion.3
  540.1 2.0 copy.102
  542.1 3.5 convert_element_type.191
  545.6 4.6 fusion.71
  551.9 10.6 fusion.64
  562.5 4.8 pad.62
  568.9 9.9 fusion.83
  578.8 4.4 pad.64
  584.5 34.3 %reduce-scatter.9.cloned.1.call-done = f32[96,768]{1,0:T(8,128)} async-done(((f32[768,768]{1,0:T(8,128)}), f32[96,768]{1,0:T(8,128)}) %reduce-scatter.9.cloned.1.call-update) | async-done | bytes 294928 | tf_op jit(solution)/shard_map/reduce_scatter | solution.py:266
  618.9 71.3 %reduce-scatter.7.cloned.1.call-done = f32[96,768]{1,0:T(8,128)} async-done(((f32[768,768]{1,0:T(8,128)}), f32[96,768]{1,0:T(8,128)}) %reduce-scatter.7.cloned.1.call-update) | async-done | bytes 294928 | tf_op jit(solution)/shard_map/reduce_scatter | solution.py:265
  690.2 166.1 %reduce-scatter.15.cloned.1.call-done = f32[96,3072]{1,0:T(8,128)} async-done(((f32[768,3072]{1,0:T(8,128)}), f32[96,3072]{1,0:T(8,128)}) %reduce-scatter.15.cloned.1.call-update) | async-done | bytes 1179664 | tf_op jit(solution)/shard_map/reduce_scatter | solution.py:275
  856.4 166.1 %reduce-scatter.17.cloned.1.call-done = f32[384,768]{1,0:T(8,128)} async-done(((f32[3072,768]{1,0:T(8,128)}), f32[384,768]{1,0:T(8,128)}) %reduce-scatter.17.cloned.1.call-update) | async-done | bytes 1179664 | tf_op jit(solution)/shard_map/reduce_scatter | solution.py:277
  1022.5 5.9 fusion.50
  1028.7 3.5 fusion.53
  1032.7 6.7 select_convert_fusion
  1039.8 35.2 %all-reduce.35 = (f32[768]{0:T(1024)S(1)}, f32[768]{0:T(1024)S(1)}, f32[768]{0:T(1024)S(1)}, f32[768]{0:T(1024)S(1)}, f32[768]{0:T(1024)S(1)}, /*index=5*/f32[30...) all-reduce(f32[768]{0:T(1024)S(1)} %pad.57, ...), channel_id=6, replica_groups=mesh['dp'=4,'fsdp'=8] {'fsdp'}, use_global_device_ids=true, to_apply=%region_21.22.clone | all-reduce | flops 9984 | bytes 79872
  1075.8 7.0 all-reduce.36
  1082.8 17.6 %all-reduce.41.cloned.1.call-done = (f32[96,768]{1,0:T(8,128)}, f32[96,768]{1,0:T(8,128)}, f32[96,768]{1,0:T(8,128)}, f32[96,768]{1,0:T(8,128)}, f32[96,3072]{1,0:T(8,128)}, /*index=5*/f32[384,768]{1,0:T(8,128)}) async-done(((f32[96,768]{1,0:T(8,128)}, f32[96,768]{1,0:T(8,128)}, f32[96,768]{1,0:T(8,128)}, f32[96,768]{1,0:T(8,128)}, f32[96,3072]{1,0:T(8,128)}, /*index=5*/f32[384,768]{1,0:T(8,128)}), ...) | async-done | bytes 3538960 | tf_op jit(solution)/shard_map/psum | solution.py:263
  1100.4 1.8 copy.164
  1102.2 1.7 copy.165
  1107.3 2.4 copy.168
  (179 shorter events, 37.8 us)
Async XLA Ops:
  7.2 82.3 %all-gather.8.cloned.1.call-start = ((), (), s32[]{:S(2)}) async-start(), calls=%async_computation.6 | async-start | bytes 1327104 | tf_op jit(solution)/shard_map/all_gather | solution.py:111
  7.9 94.7 %all-gather.10.cloned.1.call-start = ((), (), s32[]{:S(2)}) async-start(), calls=%async_computation.7 | async-start | bytes 1327104 | tf_op jit(solution)/shard_map/all_gather | solution.py:109
  8.7 129.4 %all-gather.12.cloned.1.call-start = ((), (), s32[]{:S(2)}) async-start(), calls=%async_computation.8 | async-start | bytes 1327104 | tf_op jit(solution)/shard_map/all_gather | solution.py:110
  9.4 195.8 %all-gather.14.cloned.1.call-start = ((), (), s32[]{:S(2)}) async-start(), calls=%async_computation.9 | async-start | bytes 1327104 | tf_op jit(solution)/shard_map/all_gather | solution.py:112
  10.0 250.7 %all-gather.16.cloned.1.call-start = ((), (), s32[]{:S(2)}) async-start(), calls=%async_computation.10 | async-start | bytes 5308416 | tf_op jit(solution)/shard_map/all_gather | solution.py:152
  10.6 330.2 %all-gather.18.cloned.1.call-start = ((), (), s32[]{:S(2)}) async-start(), calls=%async_computation.11 | async-start | bytes 5308416 | tf_op jit(solution)/shard_map/all_gather | solution.py:154
  11.1 573.4 %reduce-scatter.13.cloned.1.call-start = ((), (), s32[]{:S(2)}) async-start(), calls=%async_computation.15 | async-start | bytes 2654208 | tf_op jit(solution)/shard_map/reduce_scatter | solution.py:268
  13.5 191.8 %copy-start.25 = (pred[1600]{0:T(1024)(128)(4,1)}, pred[1600]{0:T(1024)(128)(4,1)S(1)}, u32[]{:S(2)}) copy-start(pred[1600]{0:T(1024)(128)(4,1)S(1)} %broadcast_in_dim.36) | copy-start | bytes 4804
  62.2 143.0 %copy-start.35 = (f32[640]{0:T(1024)}, f32[640]{0:T(1024)S(1)}, u32[]{:S(2)}) copy-start(f32[640]{0:T(1024)S(1)} %slice_convert_fusion.9) | copy-start | bytes 7684
  88.8 252.0 %copy-start.32 = (f32[640]{0:T(1024)}, f32[640]{0:T(1024)S(1)}, u32[]{:S(2)}) copy-start(f32[640]{0:T(1024)S(1)} %get-tuple-element.93) | copy-start | bytes 7684
  152.4 15.5 %copy-start.2 = (bf16[4,400,10,64]{1,0,3,2:T(4,128)(2,1)}, bf16[4,400,10,64]{1,0,3,2:T(4,128)(2,1)S(1)}, u32[]{:S(2)}) copy-start(bf16[4,400,10,64]{1,0,3,2:T(4,128)(2,1)S(1)} %reshape.146) | copy-start | bytes 6144004
  167.9 14.1 %copy-start.16 = (f32[4,10,400]{2,1,0:T(8,128)}, f32[4,10,400]{2,1,0:T(8,128)S(1)}, u32[]{:S(2)}) copy-start(f32[4,10,400]{2,1,0:T(8,128)S(1)} %get-tuple-element.72) | copy-start | bytes 192004
  167.9 14.1 %copy-start.8 = (bf16[4,400,10,64]{1,0,3,2:T(4,128)(2,1)S(1)}, bf16[4,400,10,64]{1,0,3,2:T(4,128)(2,1)}, u32[]{:S(2)}) copy-start(bf16[4,400,10,64]{1,0,3,2:T(4,128)(2,1)} %reshape.144) | copy-start | bytes 6144004
  182.0 16.0 %copy-start.20 = (f32[4,10,400]{2,1,0:T(8,128)}, f32[4,10,400]{2,1,0:T(8,128)S(1)}, u32[]{:S(2)}) copy-start(f32[4,10,400]{2,1,0:T(8,128)S(1)} %fusion) | copy-start | bytes 192004
  210.4 1.9 copy-start.5
  213.0 0.6 copy-start.22
  260.7 80.1 %copy-start.34 = (f32[640]{0:T(1024)S(1)}, f32[640]{0:T(1024)}, u32[]{:S(2)}) copy-start(f32[640]{0:T(1024)} %get-tuple-element.92) | copy-start | bytes 7684
  353.6 1.6 copy-start.10
  353.7 1.6 copy-start.24
  354.4 3.0 copy-start.27
  360.5 1.9 copy-start.7
  363.4 21.9 %copy-start.13 = (bf16[1600,640]{1,0:T(8,128)(2,1)}, bf16[1600,640]{1,0:T(8,128)(2,1)S(1)}, u32[]{:S(2)}) copy-start(bf16[1600,640]{1,0:T(8,128)(2,1)S(1)} %get-tuple-element.60) | copy-start | bytes 6144004
  385.4 14.5 %copy-start.23 = (f32[1600]{0:T(1024)S(1)}, f32[1600]{0:T(1024)}, u32[]{:S(2)}) copy-start(f32[1600]{0:T(1024)} %copy-done.22) | copy-start | bytes 19204
  385.4 14.6 %copy-start.6 = (f32[1600,640]{1,0:T(8,128)S(1)}, f32[1600,640]{1,0:T(8,128)}, u32[]{:S(2)}) copy-start(f32[1600,640]{1,0:T(8,128)} %copy-done.5) | copy-start | bytes 12288004
  401.6 5.1 copy-start
  401.6 3.2 copy-start.12
  402.1 4.6 copy-start.15
  406.7 1.7 copy-start.17
  406.7 1.7 copy-start.21
  408.4 176.2 %reduce-scatter.11.cloned.1.call-start = ((), (), s32[]{:S(2)}) async-start(), calls=%async_computation.14 | async-start | bytes 2654208 | tf_op jit(solution)/shard_map/reduce_scatter | solution.py:267
  438.6 11.3 %copy-start.26 = (pred[1600]{0:T(1024)(128)(4,1)S(1)}, pred[1600]{0:T(1024)(128)(4,1)}, u32[]{:S(2)}) copy-start(pred[1600]{0:T(1024)(128)(4,1)} %copy-done.25) | copy-start | bytes 4804
  438.6 11.3 %copy-start.36 = (f32[640]{0:T(1024)S(1)}, f32[640]{0:T(1024)}, u32[]{:S(2)}) copy-start(f32[640]{0:T(1024)} %copy-done.35) | copy-start | bytes 7684
  456.1 162.8 %reduce-scatter.9.cloned.1.call-start = ((), (), s32[]{:S(2)}) async-start(), calls=%async_computation.13 | async-start | bytes 2654208 | tf_op jit(solution)/shard_map/reduce_scatter | solution.py:266
  481.6 28.0 %copy-start.4 = (bf16[4,400,10,64]{1,0,3,2:T(4,128)(2,1)S(1)}, bf16[4,400,10,64]{1,0,3,2:T(4,128)(2,1)}, u32[]{:S(2)}) copy-start(bf16[4,400,10,64]{1,0,3,2:T(4,128)(2,1)} %reshape.145) | copy-start | bytes 6144004
  528.5 2.6 copy-start.3
  530.1 160.1 %reduce-scatter.7.cloned.1.call-start = ((), (), s32[]{:S(2)}) async-start(), calls=%async_computation.12 | async-start | bytes 2654208 | tf_op jit(solution)/shard_map/reduce_scatter | solution.py:265
  550.2 1.7 copy-start.33
  551.8 304.5 %reduce-scatter.15.cloned.1.call-start = ((), (), s32[]{:S(2)}) async-start(), calls=%async_computation.16 | async-start | bytes 10616832 | tf_op jit(solution)/shard_map/reduce_scatter | solution.py:275
  567.3 1.6 copy-start.14
  567.3 455.1 %reduce-scatter.17.cloned.1.call-start = ((), (), s32[]{:S(2)}) async-start(), calls=%async_computation.17 | async-start | bytes 10616832 | tf_op jit(solution)/shard_map/reduce_scatter | solution.py:277
  583.1 517.3 %all-reduce.41.cloned.1.call-start = ((), (), s32[]{:S(2)}) async-start(), calls=%async_computation.18 | async-start | bytes 7077888 | tf_op jit(solution)/shard_map/psum | solution.py:263
  1022.4 6.0 copy-start.29
  1022.5 5.9 copy-start.28
  1022.5 6.0 copy-start.31
  1022.5 6.0 copy-start.30
  1022.5 6.2 copy-start.11
  1028.7 3.6 copy-start.1
  1028.7 3.7 copy-start.9
  1028.7 4.0 copy-start.19
  1100.4 9.2 copy-start.18
Sparse Core Ops, SparseCore 0:
  10.2 43.8 all-gather.7
  56.3 39.6 all-gather.9
  98.2 39.8 all-gather.11
  140.1 39.8 all-gather.13
  182.0 78.6 all-gather.15
  262.7 78.0 all-gather.17
  408.5 67.1 reduce-scatter.12
  479.1 68.0 reduce-scatter.10
  550.7 68.0 reduce-scatter.8
  622.2 67.9 reduce-scatter.6
  693.8 162.5 reduce-scatter.14
  859.8 162.5 reduce-scatter.16
  1025.2 75.1 all-reduce.40
where the time goes:
time: 1120 us
  waiting for transfers between devices  562 us (50%)
  matrix products  261 us (23%)
  local copies, waits for them, and re-layouts  113 us (10%)
  blocking collectives  107 us (10%)
  other arithmetic  55 us (5%)
  between operations  16.7 us (1%)
    reduce_scatter x1, waiting for transfers between devices, on_device(): lax.psum_scatter(ffn_grads[0], 'fsdp', scatter_dimension=0, tiled=True)  166 us
    reduce_scatter x1, waiting for transfers between devices, on_device(): lax.psum_scatter(ffn_grads[2], 'fsdp', scatter_dimension=0, tiled=True)  166 us
    dot_general x6, matrix products, matmul(): return jnp.dot(left, right, preferred_element_type=jnp.float32)  78.6 us
    unnamed x2, blocking collectives  74.4 us
    reduce_scatter x1, waiting for transfers between devices, on_device(): lax.psum_scatter(attn_grads[0], 'fsdp', scatter_dimension=0, tiled=True)  71.3 us
    dot_general x6, matrix products, matmul_nt(): lax.dot_general(left, right, (((1,), (1,)), ((), ())), preferred_element_...  56.4 us
    all_gather x1, waiting for transfers between devices, on_device(): lax.all_gather(up_weight, 'fsdp', axis=0, tiled=True)  47.1 us
    dot_general x6, matrix products, matmul_tn(): lax.dot_general(left, right, (((0,), (0,)), ((), ())), preferred_element_...  36.2 us
  transfers between devices with their start and end apart: 13, of which 8 were waited for; matrix products, arithmetic and copies ran while one was open for 31% of the time, Pallas kernels for 0%

commit v1 on v0

v1 whole, which is shorter than its diff:
```python
import functools
import jax
import jax.numpy as jnp
from jax import lax
from jax.experimental import pallas as pl
from jax.experimental.pallas import tpu as pltpu
from jax.sharding import PartitionSpec as P

HEADS = 10
HEAD_DIM = 64
FF = 2560
D = 640
FRAMES = 400
SPAN = 10
PAIR = 2 * HEAD_DIM
EPS = 1e-05
F32 = jnp.float32
BF16 = jnp.bfloat16
VMEM_LIMIT = 60 * 1024 * 1024
HID = 512


def dot_nn(a, b):
    return lax.dot_general(a, b, (((1,), (0,)), ((), ())), preferred_element_type=F32)


def dot_nt(a, b):
    return lax.dot_general(a, b, (((1,), (1,)), ((), ())), preferred_element_type=F32)


def dot_tn(a, b):
    return lax.dot_general(a, b, (((0,), (0,)), ((), ())), preferred_element_type=F32)


def mean_last(a):
    return jnp.mean(a, axis=-1, keepdims=True)


def rows_sum(a):
    return jnp.sum(a, axis=0, keepdims=True)


def masked_rows(frames_ref, starts_ref, mask_row):
    places = lax.broadcasted_iota(jnp.int32, (FRAMES, starts_ref.shape[-1]), 0)
    ahead = places - starts_ref[0]
    inside = jnp.where((ahead >= 0) & (ahead < SPAN), 1.0, 0.0)
    masked = jnp.max(inside, axis=1, keepdims=True) > 0.5
    return masked, jnp.where(masked, mask_row, frames_ref[...].astype(F32))


def fetch(place_ref, mine, other, sem, parts):
    pieces = mine.shape[0]

    def copies(source, half):
        for core, first, count, column, target in parts:
            if core != half:
                continue
            for piece in range(pieces):
                rows = min(count, target.shape[0] - piece * count)
                if rows > 0:
                    yield pltpu.make_async_copy(
                        source.at[place_ref[1 + piece], pl.ds(first, rows), :],
                        target.at[pl.ds(piece * count, rows), pl.ds(column, D)],
                        sem,
                    )

    for core in (0, 1):

        @pl.when(place_ref[0] == core)
        def _(core=core):
            started = list(copies(mine, core)) + list(copies(other, 1 - core))
            for copy in started:
                copy.start()
            for copy in started:
                copy.wait()


def fetch_attn(place_ref, mine, other, sem, wq, wk, wv, wo):
    count = mine.shape[1] // 2
    parts = []
    for target, core, first in ((wq, 0, 0), (wk, 0, count), (wv, 1, 0), (wo, 1, count)):
        if target is not None:
            parts.append((core, first, count, 0, target))
    fetch(place_ref, mine, other, sem, parts)


def fetch_ffn(place_ref, mine, other, sem, w1, w2):
    count = mine.shape[1]
    part = count // (FF // D)
    parts = [(0, j * part, part, j * D, w1) for j in range(FF // D)]
    fetch(place_ref, mine, other, sem, parts + [(1, 0, count, 0, w2)])


def attn_forward(
    place_ref, mine_ref, other_ref, starts_ref, frames_ref, vec_ref,
    q_ref, k_ref, v_ref, o_ref, lse_ref, n1_ref, rstd_ref,
    wq_ref, wk_ref, wv_ref, wo_ref, sem,
):
    @pl.when(pl.program_id(0) == 0)
    def _():
        fetch_attn(place_ref, mine_ref, other_ref, sem, wq_ref, wk_ref, wv_ref, wo_ref)

    bq, bv, bo = vec_ref[0:1, :], vec_ref[1:2, :], vec_ref[2:3, :]
    masked, x0 = masked_rows(frames_ref, starts_ref, vec_ref[5:6, :])
    h = x0.astype(BF16)
    scale = HEAD_DIM ** (-0.5)
    q_ref[...] = ((dot_nn(h, wq_ref[...]) + bq).astype(BF16).astype(F32) * scale).astype(BF16)
    k_ref[...] = dot_nn(h, wk_ref[...]).astype(BF16)
    v_ref[...] = (dot_nn(h, wv_ref[...]) + bv).astype(BF16)
    low_lanes = lax.broadcasted_iota(jnp.int32, (FRAMES, PAIR), 1) < HEAD_DIM
    lanes = lax.broadcasted_iota(jnp.int32, (FRAMES, 128), 1)
    lse = jnp.zeros((FRAMES, 128), F32)
    for pair in range(HEADS // 2):
        cols = slice(pair * PAIR, (pair + 1) * PAIR)
        qp, kp, vp = q_ref[:, cols], k_ref[:, cols], v_ref[:, cols]
        parts = []
        for half in range(2):
            keep = low_lanes if half == 0 else jnp.logical_not(low_lanes)
            qh = jnp.where(keep, qp.astype(F32), 0.0).astype(BF16)
            scores = dot_nt(qh, kp)
            top = jnp.max(scores, axis=-1, keepdims=True)
            expo = jnp.exp(scores - top)
            total = jnp.sum(expo, axis=-1, keepdims=True)
            parts.append(dot_nn(expo.astype(BF16), vp) * (1.0 / total))
            lse = jnp.where(lanes == 2 * pair + half, top + jnp.log(total), lse)
        o_ref[:, cols] = jnp.where(low_lanes, parts[0], parts[1]).astype(BF16)
    lse_ref[0] = jnp.transpose(lse)[0:16, :]
    r1 = x0 + (dot_nn(o_ref[...], wo_ref[...]) + bo)
    center = r1 - mean_last(r1)
    rstd = lax.rsqrt(mean_last(center * center) + EPS)
    n1_ref[...] = center * rstd
    rstd_ref[...] = rstd


def gelu_parts(u):
    bell = jnp.exp(u * u * -0.5)
    t = 1.0 / (1.0 + (0.3275911 * 0.7071067811865476) * jnp.abs(u))
    poly = t * (
        0.5 * 0.254829592
        + t * (0.5 * -0.284496736 + t * (0.5 * 1.421413741 + t * (0.5 * -1.453152027 + t * (0.5 * 1.061405429))))
    )
    tail = poly * bell
    phi = jnp.where(u >= 0, 1.0 - tail, tail)
    return u * phi, phi + u * bell * 0.3989422804014327


def ffn_forward(
    place_ref, mine_ref, other_ref, n1_ref, cot_ref, vec_ref, b1_ref,
    out_ref, slope_ref, dz_ref, dr2_ref, dw2_ref, small_ref,
    hidden, acc, w1_ref, w2_ref, sem,
):
    step = pl.program_id(0)

    @pl.when(step == 0)
    def _():
        fetch_ffn(place_ref, mine_ref, other_ref, sem, w1_ref, w2_ref)

    g1, s1, g2, s2, b2 = (vec_ref[i : i + 1, :] for i in (3, 4, 6, 7, 8))
    y1 = g1 * n1_ref[...] + s1
    y1b = y1.astype(BF16)
    for c in range(FF // HID):
        cols = slice(c * HID, (c + 1) * HID)
        u = dot_nn(y1b, w1_ref[:, cols]) + b1_ref[0:1, cols]
        act, slope = gelu_parts(u)
        hidden[:, cols] = act.astype(BF16)
        slope_ref[:, cols] = slope.astype(BF16)
    r2 = y1 + (dot_nn(hidden[...], w2_ref[...]) + b2)
    center = r2 - mean_last(r2)
    rstd = lax.rsqrt(mean_last(center * center) + EPS)
    n2 = center * rstd
    out_ref[...] = (n2 * g2 + s2).astype(BF16)
    dy = cot_ref[...].astype(F32)
    e = dy * g2
    dr2 = (e - mean_last(e) - n2 * mean_last(e * n2)) * rstd
    dz = dr2.astype(BF16)
    dr2_ref[...] = dr2
    dz_ref[...] = dz

    @pl.when(step == 0)
    def _():
        small_ref[...] = jnp.zeros_like(small_ref)
        acc[...] = jnp.zeros_like(acc)

    small_ref[0:1, :] += rows_sum(dz.astype(F32))
    small_ref[1:2, :] += rows_sum(dy * n2)
    small_ref[2:3, :] += rows_sum(dy)
    acc[...] += dot_tn(hidden[...], dz)

    @pl.when(step == pl.num_programs(0) - 1)
    def _():
        dw2_ref[0:FF, :] = acc[...].astype(BF16)
        dw2_ref[FF:, :] = jnp.zeros((dw2_ref.shape[0] - FF, D), BF16)


def spread(target, first, count, grad):
    for block in range(target.shape[0]):
        low = block * count
        rows = max(0, min(count, D - low))
        if rows:
            target[block, first : first + rows, :] = grad(low, low + rows).astype(BF16)
        if rows < count:
            target[block, first + rows : first + count, :] = jnp.zeros((count - rows, D), BF16)


def ffn_backward(
    aplace_ref, fplace_ref, amine_ref, aother_ref, fmine_ref, fother_ref,
    n1_ref, rstd_ref, dz_ref, dr2_ref, slope_ref, o_ref, vec_ref,
    dr1_ref, do_ref, grads_ref, small_ref, db1_ref,
    grad_pre, acc1, acco, w1_ref, w2_ref, wo_ref, sem,
):
    step = pl.program_id(0)

    @pl.when(step == 0)
    def _():
        fetch_ffn(fplace_ref, fmine_ref, fother_ref, sem, w1_ref, w2_ref)
        fetch_attn(aplace_ref, amine_ref, aother_ref, sem, None, None, None, wo_ref)
        small_ref[...] = jnp.zeros_like(small_ref)
        db1_ref[...] = jnp.zeros_like(db1_ref)
        acc1[...] = jnp.zeros_like(acc1)
        acco[...] = jnp.zeros_like(acco)

    g1, s1 = vec_ref[3:4, :], vec_ref[4:5, :]
    n1 = n1_ref[...]
    y1b = (g1 * n1 + s1).astype(BF16)
    dz = dz_ref[...]
    for c in range(FF // HID):
        cols = slice(c * HID, (c + 1) * HID)
        du = (dot_nt(dz, w2_ref[cols, :]) * slope_ref[:, cols].astype(F32)).astype(BF16)
        grad_pre[:, cols] = du
        db1_ref[0:1, cols] += rows_sum(du.astype(F32))
    acc1[...] += dot_tn(y1b, grad_pre[...])
    dy1 = dot_nt(grad_pre[...], w1_ref[...]) + dr2_ref[...]
    e = dy1 * g1
    dr1 = (e - mean_last(e) - n1 * mean_last(e * n1)) * rstd_ref[...]
    dr1_ref[...] = dr1
    da = dr1.astype(BF16)
    small_ref[0:1, :] += rows_sum(da.astype(F32))
    small_ref[1:2, :] += rows_sum(dy1 * n1)
    small_ref[2:3, :] += rows_sum(dy1)
    acco[...] += dot_tn(o_ref[...], da)
    do_ref[...] = dot_nt(da, wo_ref[...]).astype(BF16)

    @pl.when(step == pl.num_programs(0) - 1)
    def _():
        count = grads_ref.shape[1] // 5
        for j in range(FF // D):
            spread(grads_ref, j * count, count, lambda low, high: acc1[low:high, j * D : (j + 1) * D])
        spread(grads_ref, 4 * count, count, lambda low, high: acco[low:high, :])


def attn_backward(
    first, starts_ref, frames_ref, vec_ref, q_ref, k_ref, v_ref, do_ref, lse_ref,
    dq_ref, dk_ref, dv_ref, grads_ref, small_ref,
    accq, acck, accv,
):
    step = pl.program_id(0)

    @pl.when(step == 0)
    def _():
        small_ref[...] = jnp.zeros_like(small_ref)
        accq[...] = jnp.zeros_like(accq)
        acck[...] = jnp.zeros_like(acck)
        accv[...] = jnp.zeros_like(accv)

    scale = HEAD_DIM ** (-0.5)
    low_lanes = lax.broadcasted_iota(jnp.int32, (FRAMES, PAIR), 1) < HEAD_DIM
    for pair in range(q_ref.shape[1] // PAIR):
        cols = slice(pair * PAIR, (pair + 1) * PAIR)
        qp, kp, vp, dop = q_ref[:, cols], k_ref[:, cols], v_ref[:, cols], do_ref[:, cols]
        parts = []
        for half in range(2):
            keep = low_lanes if half == 0 else jnp.logical_not(low_lanes)
            kh = jnp.where(keep, kp.astype(F32), 0.0).astype(BF16)
            vh = jnp.where(keep, vp.astype(F32), 0.0).astype(BF16)
            head = first + 2 * pair + half
            prob = jnp.exp(dot_nt(kh, qp) - lse_ref[0, head : head + 1, :])
            dprob = dot_nt(vh, dop)
            inner = jnp.sum(prob * dprob, axis=0, keepdims=True)
            dscore = (prob * (dprob - inner)).astype(BF16)
            parts.append((dot_nn(prob.astype(BF16), dop), dot_nn(dscore, qp), dot_tn(dscore, kp) * scale))
        for ref, one, two in zip((dv_ref, dk_ref, dq_ref), *parts):
            ref[:, cols] = jnp.where(low_lanes, one, two).astype(BF16)
    masked, x0 = masked_rows(frames_ref, starts_ref, vec_ref[5:6, :])
    h = x0.astype(BF16)
    accq[...] += dot_tn(h, dq_ref[...])
    acck[...] += dot_tn(h, dk_ref[...])
    accv[...] += dot_tn(h, dv_ref[...])
    small_ref[0:1, :] += rows_sum(dq_ref[...].astype(F32))
    small_ref[1:2, :] += rows_sum(dv_ref[...].astype(F32))

    @pl.when(step == pl.num_programs(0) - 1)
    def _():
        count = grads_ref.shape[1] // 3
        for j, acc in enumerate((accq, acck, accv)):
            spread(grads_ref, j * count, count, lambda low, high: acc[low:high, :])


def input_backward(
    place_ref, mine_ref, other_ref, starts_ref, dr1_ref, dq_ref, dk_ref, dv_ref,
    grad_ref, small_ref,
    wq_ref, wk_ref, wv_ref, sem,
):
    step = pl.program_id(0)

    @pl.when(step == 0)
    def _():
        fetch_attn(place_ref, mine_ref, other_ref, sem, wq_ref, wk_ref, wv_ref, None)
        small_ref[...] = jnp.zeros_like(small_ref)

    places = lax.broadcasted_iota(jnp.int32, (FRAMES, starts_ref.shape[-1]), 0)
    ahead = places - starts_ref[0]
    inside = jnp.where((ahead >= 0) & (ahead < SPAN), 1.0, 0.0)
    masked = jnp.max(inside, axis=1, keepdims=True) > 0.5
    dx0 = (
        dot_nt(dq_ref[...], wq_ref[...])
        + dot_nt(dk_ref[...], wk_ref[...])
        + dot_nt(dv_ref[...], wv_ref[...])
        + dr1_ref[...]
    )
    grad_ref[...] = jnp.where(masked, 0.0, dx0).astype(BF16)
    small_ref[0:1, :] += rows_sum(jnp.where(masked, dx0, 0.0))


def row_blocks(width):
    return pl.BlockSpec((FRAMES, width), lambda i: (i, 0))


def kept(rows, cols):
    return pl.BlockSpec((rows, cols), lambda i: (0, 0), pipeline_mode=pl.Buffered(1))


def held(rows, cols):
    return pl.BlockSpec((rows, cols), lambda i: (0, 0))


def held3(first, rows, cols):
    return pl.BlockSpec((first, rows, cols), lambda i: (0, 0, 0))


def shape(*sizes, dtype=BF16):
    return jax.ShapeDtypeStruct(sizes, dtype)


SCALARS = pl.BlockSpec(memory_space=pltpu.SMEM)
WHOLE = pl.BlockSpec(memory_space=pl.ANY)
COPIES = pltpu.SemaphoreType.DMA(())


def call(body, utters, in_specs, out_specs, out_shape, scratch=(), flops=0, moved=0, exps=0):
    return pl.pallas_call(
        body,
        grid=(utters,),
        in_specs=in_specs,
        out_specs=out_specs,
        out_shape=out_shape,
        scratch_shapes=list(scratch),
        compiler_params=pltpu.CompilerParams(
            dimension_semantics=("arbitrary",), vmem_limit_bytes=VMEM_LIMIT
        ),
        cost_estimate=pl.CostEstimate(
            flops=int(flops), bytes_accessed=int(moved), transcendentals=int(exps)
        ),
    )


def starts_spec(starts):
    return pl.BlockSpec((1, 1, starts.shape[-1]), lambda i: (i, 0, 0))


def lse_spec():
    return pl.BlockSpec((1, 16, FRAMES), lambda i: (i, 0, 0))


def weights(*sizes):
    return [pltpu.VMEM(size, BF16) for size in sizes] + [COPIES]


def run_attn_forward(place, attn, starts, frames, vec):
    rows = frames.shape[0]
    utters = rows // FRAMES
    return call(
        attn_forward, utters,
        [SCALARS, WHOLE, WHOLE, starts_spec(starts), row_blocks(D), kept(16, D)],
        [row_blocks(D)] * 4 + [lse_spec(), row_blocks(D), row_blocks(1)],
        [shape(rows, D)] * 4
        + [shape(utters, 16, FRAMES, dtype=F32), shape(rows, D, dtype=F32), shape(rows, 1, dtype=F32)],
        weights(*[(D, D)] * 4),
        flops=rows * D * D * 8 + rows * FRAMES * D * 16, moved=rows * D * 14,
    )(place, *attn, starts, frames, vec)


def run_ffn_forward(place, ffn, n1, cot, vec, b1, ff_rows):
    rows = n1.shape[0]
    return call(
        ffn_forward, rows // FRAMES,
        [SCALARS, WHOLE, WHOLE, row_blocks(D), row_blocks(D), kept(16, D), kept(8, FF)],
        [row_blocks(D), row_blocks(FF), row_blocks(D), row_blocks(D), held(ff_rows, D), held(8, D)],
        [shape(rows, D), shape(rows, FF), shape(rows, D), shape(rows, D, dtype=F32),
         shape(ff_rows, D), shape(8, D, dtype=F32)],
        [pltpu.VMEM((FRAMES, FF), BF16), pltpu.VMEM((FF, D), F32)] + weights((D, FF), (FF, D)),
        flops=rows * D * FF * 6, moved=rows * D * 40,
    )(place, *ffn, n1, cot, vec, b1)


def run_ffn_backward(attn_place, ffn_place, attn, ffn, n1, rstd, dz, dr2, slope, o, vec, blocks, count):
    rows = n1.shape[0]
    return call(
        ffn_backward, rows // FRAMES,
        [SCALARS] * 2 + [WHOLE] * 4
        + [row_blocks(D), row_blocks(1), row_blocks(D), row_blocks(D), row_blocks(FF), row_blocks(D), kept(16, D)],
        [row_blocks(D), row_blocks(D), held3(blocks, 5 * count, D), held(8, D), held(8, FF)],
        [shape(rows, D, dtype=F32), shape(rows, D), shape(blocks, 5 * count, D),
         shape(8, D, dtype=F32), shape(8, FF, dtype=F32)],
        [pltpu.VMEM((FRAMES, FF), BF16), pltpu.VMEM((D, FF), F32), pltpu.VMEM((D, D), F32)]
        + weights((D, FF), (FF, D), (D, D)),
        flops=rows * D * FF * 6 + rows * D * D * 4, moved=rows * D * 40,
    )(attn_place, ffn_place, *attn, *ffn, n1, rstd, dz, dr2, slope, o, vec)


def run_attn_backward(starts, frames, vec, q, k, v, do, lse, blocks, count):
    rows = frames.shape[0]
    utters = rows // FRAMES
    return call(
        functools.partial(attn_backward, 0), utters,
        [starts_spec(starts), row_blocks(D), kept(16, D)] + [row_blocks(D)] * 4 + [lse_spec()],
        [row_blocks(D)] * 3 + [held3(blocks, 3 * count, D), held(8, D)],
        [shape(rows, D)] * 3 + [shape(blocks, 3 * count, D), shape(8, D, dtype=F32)],
        [pltpu.VMEM((D, D), F32)] * 3,
        flops=rows * D * D * 6 + rows * FRAMES * D * 10, moved=rows * D * 10,
    )(starts, frames, vec, q, k, v, do, lse)


def run_input_backward(place, attn, starts, dr1, dq, dk, dv):
    rows = dr1.shape[0]
    return call(
        input_backward, rows // FRAMES,
        [SCALARS, WHOLE, WHOLE, starts_spec(starts)] + [row_blocks(D)] * 4,
        [row_blocks(D), held(8, D)],
        [shape(rows, D), shape(8, D, dtype=F32)],
        weights(*[(D, D)] * 3),
        flops=rows * D * D * 6, moved=rows * D * 12,
    )(place, *attn, starts, dr1, dq, dk, dv)


def in_order(value, order):
    return jnp.concatenate([lax.dynamic_slice_in_dim(value, order[i], 1) for i in range(value.shape[0])])


class Grid:
    def __init__(self, dp, fsdp):
        self.dp, self.fsdp = dp, fsdp
        self.dp_bits = [1 << i for i in range(dp.bit_length() - 1)]
        self.fsdp_bits = [1 << i for i in range(fsdp.bit_length() - 1)]

    def bit(self, axis, bit):
        return (lax.axis_index(axis) // bit) % 2

    def swap(self, value, dp_mask, fsdp_mask):
        if not dp_mask:
            return lax.ppermute(value, "fsdp", [(i, i ^ fsdp_mask) for i in range(self.fsdp)])
        if not fsdp_mask:
            return lax.ppermute(value, "dp", [(i, i ^ dp_mask) for i in range(self.dp)])
        pairs = [
            (i * self.fsdp + j, (i ^ dp_mask) * self.fsdp + (j ^ fsdp_mask))
            for i in range(self.dp)
            for j in range(self.fsdp)
        ]
        return lax.ppermute(value, ("dp", "fsdp"), pairs)

    def gather(self, piece):
        gathered = piece[None]
        for bit in reversed(self.fsdp_bits):
            gathered = jnp.concatenate([gathered, self.swap(gathered, 0, bit)])
        return gathered

    def places(self):
        me = lax.axis_index("fsdp")
        code = me ^ jnp.arange(self.fsdp, dtype=jnp.int32)
        place = jnp.zeros_like(code)
        for step, bit in enumerate(reversed(self.fsdp_bits)):
            place = place + ((code // bit) % 2) * (1 << step)
        return place

    def stages(self):
        dp_left, fsdp_left = self.dp_bits[1:], list(self.fsdp_bits)
        order = [[("dp", 1)]]
        while dp_left and fsdp_left:
            order.append([("dp", dp_left.pop(0)), ("fsdp", fsdp_left.pop(0))])
        order += [[("dp", bit)] for bit in dp_left]
        while fsdp_left:
            order.append([("fsdp", bit) for bit in fsdp_left[:2]])
            fsdp_left = fsdp_left[2:]
        return order

    def reduce(self, grads):
        rows, width = grads.shape[1:]
        left = list(reversed(self.fsdp_bits))
        value = grads.reshape((2,) * len(left) + (rows, width))
        halved = []
        for stage in self.stages():
            for axis, bit in stage:
                if axis == "dp":
                    value = value.reshape(value.shape[:-2] + (2, value.shape[-2] // 2, width))
                    halved.append(bit)
            spots = {}
            extra = len(left)
            for axis, bit in stage:
                if axis == "dp":
                    spots[(axis, bit)] = extra
                    extra += 1
                else:
                    spots[(axis, bit)] = left.index(bit)
            total = None
            for code in range(1 << len(stage)):
                starts = [0] * value.ndim
                sizes = list(value.shape)
                masks = {"dp": 0, "fsdp": 0}
                for place, (axis, bit) in enumerate(stage):
                    other = (code >> place) & 1
                    starts[spots[(axis, bit)]] = self.bit(axis, bit) ^ other
                    sizes[spots[(axis, bit)]] = 1
                    masks[axis] += bit * other
                part = lax.dynamic_slice(value, starts, sizes)
                if code:
                    part = self.swap(part, masks["dp"], masks["fsdp"])
                part = part.astype(F32)
                total = part if total is None else total + part
            total = jnp.squeeze(total, tuple(spots.values()))
            left = [bit for bit in left if ("fsdp", bit) not in spots]
            value = total.astype(BF16)
        for bit in reversed(halved):
            other = self.swap(value, bit, 0)
            first = self.bit("dp", bit) == 0
            value = jnp.concatenate([jnp.where(first, value, other), jnp.where(first, other, value)])
        return value.astype(F32)

    def total(self, value):
        for bit in self.dp_bits:
            value = value + self.swap(value, bit, 0)
        for bit in self.fsdp_bits:
            value = value + self.swap(value, 0, bit)
        return value


def on_device(
    sizes, frames, cotangent, span_starts, query_weight, key_weight, value_weight, out_weight,
    query_bias, value_bias, out_bias, first_gain, first_shift, up_weight, up_bias, down_weight,
    down_bias, second_gain, second_shift, mask_vector,
):
    grid = Grid(*sizes)
    owners = grid.fsdp
    count = query_weight.shape[0]
    wide = down_weight.shape[0]
    d_max = count * owners
    core = lax.axis_index("dp") % 2
    direct = count % 16 == 0

    vectors = [query_bias, value_bias, out_bias, first_gain, first_shift, mask_vector,
               second_gain, second_shift, down_bias]
    packed = jnp.concatenate(vectors + [up_bias]).reshape(1, -1)
    attn_half = jnp.where(
        core == 0,
        jnp.concatenate([query_weight[:, :D], key_weight[:, :D]]),
        jnp.concatenate([value_weight[:, :D], out_weight[:, :D]]),
    )
    ffn_half = jnp.where(
        core == 0,
        jnp.concatenate([up_weight[:, j * D : (j + 1) * D] for j in range(FF // D)]),
        down_weight[:, :D],
    )
    packed_all = grid.gather(packed)
    attn_mine = grid.gather(attn_half)
    attn_other = grid.swap(attn_mine, 1, 0)
    ffn_mine = lax.all_gather(ffn_half, "fsdp", axis=0, tiled=False)
    ffn_other = grid.swap(ffn_mine, 1, 0)

    places = grid.places()
    packed_all = in_order(packed_all[:, 0], places)
    vec = packed_all[:, : len(vectors) * count].reshape(owners, len(vectors), count)
    vec = jnp.swapaxes(vec, 0, 1).reshape(len(vectors), d_max)[:, :D].astype(F32)
    vec = jnp.pad(vec, ((0, 16 - len(vectors)), (0, 0)))
    b1 = packed_all[:, len(vectors) * count :].reshape(1, -1)[:, :FF].astype(F32)
    b1 = jnp.broadcast_to(b1, (8, FF))

    if direct:
        attn = (attn_mine, attn_other)
        ffn = (ffn_mine, ffn_other)
        attn_place = jnp.concatenate([core[None], places])
        ffn_place = jnp.concatenate([core[None], jnp.arange(owners, dtype=jnp.int32)])
        blocks, block = owners, count
    else:
        def whole(value, split, order):
            value = (value if order is None else in_order(value, order)).reshape(owners, split, -1, D)
            return jnp.swapaxes(value, 0, 1).reshape(1, -1, D)

        attn = (whole(attn_mine, 2, places), whole(attn_other, 2, places))
        first = core == 0
        up_all = whole(jnp.where(first, ffn_mine, ffn_other), FF // D, None)
        down_all = whole(jnp.where(first, ffn_other, ffn_mine), 1, None)
        ffn = (jnp.where(first, up_all, down_all), jnp.where(first, down_all, up_all))
        attn_place = ffn_place = jnp.stack([core, jnp.zeros_like(core)])
        blocks, block = 1, d_max

    def owner_rows(grads, split):
        if direct:
            return grads
        grads = grads.reshape(split, owners, -1, D)
        return jnp.swapaxes(grads, 0, 1).reshape(owners, -1, D)

    starts = span_starts[:, None, :]
    q, k, v, o, lse, n1, rstd = run_attn_forward(attn_place, attn, starts, frames, vec)
    output, slope, dz, dr2, down_grad, small2 = run_ffn_forward(
        ffn_place, ffn, n1, cotangent, vec, b1, wide * owners
    )
    dr1, do, up_out_grads, small1, up_bias_grad = run_ffn_backward(
        attn_place, ffn_place, attn, ffn, n1, rstd, dz, dr2, slope, o, vec, blocks, block
    )
    dq, dk, dv, qkv_grads, small_a = run_attn_backward(
        starts, frames, vec, q, k, v, do, lse, blocks, block
    )
    frames_grad, small_m = run_input_backward(attn_place, attn, starts, dr1, dq, dk, dv)

    small = jnp.concatenate(
        [small_a[0:2], small1[0:3], small_m[0:1], small2[1:3], small2[0:1],
         up_bias_grad[0].reshape(FF // D, D), jnp.zeros((3, D), F32)]
    )
    down_sum = grid.reduce(down_grad.reshape(owners, wide, D))
    up_out_sum = grid.reduce(owner_rows(up_out_grads, 5))
    qkv_sum = grid.reduce(owner_rows(qkv_grads, 3))
    small = grid.total(small)

    def wide_rows(value):
        return jnp.pad(value, ((0, 0), (0, d_max - D)))

    me = lax.axis_index("fsdp")
    rows = jnp.pad(small[: len(vectors)], ((0, 0), (0, d_max - D)))
    rows = lax.dynamic_slice(rows, (0, me * count), (len(vectors), count))
    names = ("qb", "vb", "ob", "g1", "s1", "m", "g2", "s2", "b2")
    vec_grads = {name: rows[i] for i, name in enumerate(names)}
    b1_grad = jnp.pad(small[len(vectors) : len(vectors) + FF // D].reshape(-1), (0, wide * owners - FF))
    b1_grad = lax.dynamic_slice(b1_grad, (me * wide,), (wide,))
    up_grad = jnp.concatenate(
        [up_out_sum[j * count : (j + 1) * count] for j in range(FF // D)]
        + [jnp.zeros((count, up_weight.shape[1] - FF), F32)],
        axis=1,
    )
    return (
        output,
        frames_grad,
        wide_rows(qkv_sum[:count]),
        wide_rows(qkv_sum[count : 2 * count]),
        wide_rows(qkv_sum[2 * count :]),
        wide_rows(up_out_sum[4 * count :]),
        vec_grads["qb"],
        vec_grads["vb"],
        vec_grads["ob"],
        vec_grads["g1"],
        vec_grads["s1"],
        up_grad,
        b1_grad,
        wide_rows(down_sum),
        vec_grads["b2"],
        vec_grads["g2"],
        vec_grads["s2"],
        vec_grads["m"],
    )


def solution(mesh):
    sizes = (mesh.shape["dp"], mesh.shape["fsdp"])
    tokens = P(("dp", "fsdp"), None)
    matrix, vector = P("fsdp", None), P("fsdp")
    return jax.shard_map(
        functools.partial(on_device, sizes),
        mesh=mesh,
        in_specs=(tokens,) * 3 + (matrix,) * 4 + (vector,) * 5 + (matrix, vector, matrix) + (vector,) * 4,
        out_specs=(tokens,) * 2 + (matrix,) * 4 + (vector,) * 5 + (matrix, vector, matrix) + (vector,) * 4,
        check_vma=False,
    )
```

time: 1120 us -> 455 us (0.41)
  waiting for transfers between devices: 562 us -> 170 us
  matrix products: 261 us -> 0 us
  Pallas kernels: 0 us -> 160 us
  blocking collectives: 107 us -> 0 us
  local copies, waits for them, and re-layouts: 113 us -> 22.5 us
  starting transfers between devices: 1.09 us -> 49.4 us
  other arithmetic: 55 us -> 16 us
  between operations: 16.7 us -> 30.6 us
    reduce_scatter x6 -> x0, waiting for transfers between devices: 438 us -> none  [the longest x1 166 us: on_device(): lax.psum_scatter(ffn_grads[0], 'fsdp', scatter_dimension=0, tiled=True)]
    dot_general x24 -> x0, matrix products: 261 us -> none  [the longest x6 78.6 us: matmul(): return jnp.dot(left, right, preferred_element_type=jnp.float32)]
    pallas_call x0 -> x5, Pallas kernels: none -> 160 us  [the longest x1 43.2 us: run_ffn_forward(): call(ffn_forward, rows // FRAMES, [SCALARS, WHOLE, WHOLE, row_blocks(D),...]
    ppermute x0 -> x40, waiting for transfers between devices: none -> 111 us  [the longest x21 85.1 us: swap(): lax.ppermute(value, 'fsdp', [(i, i ^ fsdp_mask) for i in range(self.fsdp)])]
    unnamed x2 -> x0, blocking collectives: 74.4 us -> none
    ppermute x0 -> x40, starting transfers between devices: none -> 49.3 us  [the longest x21 33.8 us: swap(): lax.ppermute(value, 'fsdp', [(i, i ^ fsdp_mask) for i in range(self.fsdp)])]
    all_gather x6 -> x1, waiting for transfers between devices: 103 us -> 58.6 us  [on_device(): ffn_mine = lax.all_gather(ffn_half, 'fsdp', axis=0, tiled=False)]
    convert_element_type x12 -> x0, local copies, waits for them, and re-layouts: 41.3 us -> none  [the longest x2 11.3 us: on_device(): grad_value = grad_value.reshape(total_rows, D).astype(jnp.bfloat16)]
  transfers between devices with their start and end apart: 13 -> 41, of which waited for: 8 -> 20; matrix products, arithmetic and copies ran while one was open for 31% -> 7% of each run, Pallas kernels for 0% -> 8%
where the time goes in v1:
time: 455 us; the launch traced here: 448 us
  waiting for transfers between devices  170 us (37%)
  Pallas kernels  160 us (35%)
  starting transfers between devices  49.4 us (11%)
  between operations  30.6 us (7%)
  local copies, waits for them, and re-layouts  22.5 us (5%)
  other arithmetic  16 us (4%)
    ppermute x21, waiting for transfers between devices, swap(): lax.ppermute(value, 'fsdp', [(i, i ^ fsdp_mask) for i in range(self.fsdp)])  85.1 us
    all_gather x1, waiting for transfers between devices, on_device(): ffn_mine = lax.all_gather(ffn_half, 'fsdp', axis=0, tiled=False)  58.6 us
    pallas_call x1, Pallas kernels, run_ffn_forward(): call(ffn_forward, rows // FRAMES, [SCALARS, WHOLE, WHOLE, row_blocks(D),...  43.2 us
    pallas_call x1, Pallas kernels, run_ffn_backward(): call(ffn_backward, rows // FRAMES, [SCALARS] * 2 + [WHOLE] * 4 + [row_blo...  43 us
    pallas_call x1, Pallas kernels, run_attn_backward(): call(functools.partial(attn_backward, 0), utters, [starts_spec(starts), r...  36.7 us
    ppermute x21, starting transfers between devices, swap(): lax.ppermute(value, 'fsdp', [(i, i ^ fsdp_mask) for i in range(self.fsdp)])  33.8 us
    ppermute x16, waiting for transfers between devices, swap(): return lax.ppermute(value, 'dp', [(i, i ^ dp_mask) for i in range(self.dp)])  25.8 us
    pallas_call x1, Pallas kernels, run_attn_forward(): call(attn_forward, utters, [SCALARS, WHOLE, WHOLE, starts_spec(starts), r...  25.6 us
  transfers between devices with their start and end apart: 41, of which 20 were waited for; matrix products, arithmetic and copies ran while one was open for 7% of the time, Pallas kernels for 8%

profile of v1, /device:TPU:0, one launch (start us, length us, event | category | flops | bytes accessed | tf_op | source)
XLA Modules:
  0.0 448.1 jit_solution(11324317259498478458)
XLA Ops:
  7.3 1.3 fusion.41
  8.6 1.9 maximum_select_fusion
  10.8 4.1 collective-permute-start.1
  14.9 12.9 %collective-permute-done.1 = bf16[1,192,640]{2,1,0:T(8,128)(2,1)S(1)} collective-permute-done((bf16[1,192,640]{2,1,0:T(8,128)(2,1)S(1)}, bf16[1,192,640]{2,1,0:T(8,128)(2,1)S(1)}, u32[]{:S(2)}, u32[]{:S(2)}) %collective-permute-start.1) | collective-permute-done | bytes 245792 | tf_op jit(solution)/shard_map/ppermute | solution.py:460
  27.9 7.0 %collective-permute-start.2 = (bf16[2,192,640]{2,1,0:T(8,128)(2,1)S(1)}, bf16[2,192,640]{2,1,0:T(8,128)(2,1)S(1)}, u32[]{:S(2)}, u32[]{:S(2)}) collective-permute-start(bf16[2,192,640]{2,1,0:T(8,128)(2,1)S(1)} %pad_maximum_fusion.2), channel_id=1, source_target_pairs={{0,2},{1,3},{2,0},{3,1},{4,6},{5,7},{6,4},{7,5},{8,10},{9,11},{10,... | collective-permute-start | bytes 1474568 | tf_op jit(solution)/shard_map/ppermute | solution.py:460
  34.9 17.6 %collective-permute-done.2 = bf16[2,192,640]{2,1,0:T(8,128)(2,1)S(1)} collective-permute-done((bf16[2,192,640]{2,1,0:T(8,128)(2,1)S(1)}, bf16[2,192,640]{2,1,0:T(8,128)(2,1)S(1)}, u32[]{:S(2)}, u32[]{:S(2)}) %collective-permute-start.2) | collective-permute-done | bytes 491552 | tf_op jit(solution)/shard_map/ppermute | solution.py:460
  52.6 1.6 collective-permute-start.3
  54.2 58.6 %all-gather.3.cloned.1.call-done = bf16[3072,640]{1,0:T(8,128)(2,1)} async-done(((bf16[384,640]{1,0:T(8,128)(2,1)}), bf16[3072,640]{1,0:T(8,128)(2,1)}) %all-gather.3.cloned.1.call-update) | async-done | bytes 3932176 | tf_op jit(solution)/shard_map/all_gather | solution.py:574
  113.1 1.3 collective-permute-start.5
  114.4 1.4 pad_maximum_fusion.mine_ref.amine_ref
  116.2 0.9 fusion.42
  133.3 3.6 collective-permute-done.6
  137.0 1.2 collective-permute-start.7
  138.3 2.6 collective-permute-done.7
  142.0 25.6 %shard_map.322 = (bf16[1600,640]{1,0:T(8,128)(2,1)}, bf16[1600,640]{1,0:T(8,128)(2,1)}, bf16[1600,640]{1,0:T(8,128)(2,1)}, bf16[1600,640]{1,0:T(8,128)(2,1)}, f3...) custom-call(s32[9]{0:T(128)} %get-tuple-element.133.place_ref.aplace_ref, ...), custom_call_target="tpu_custom_call" | custom-call | flops 11796480000 | bytes 14336000 | tf_op jit(solution)/shard_map/pallas_call | solution.py:381
  168.3 43.2 %shard_map.323 = (bf16[1600,640]{1,0:T(8,128)(2,1)}, bf16[1600,2560]{1,0:T(8,128)(2,1)}, bf16[1600,640]{1,0:T(8,128)(2,1)}, f32[1600,640]{1,0:T(8,128)}, bf16[3072,640]{1,0:T(8,128)(2,1)}, /*index=5*/f32[8,640]{1,0:T(8,128)}) custom-call(s32[9]{0:T(128)} %get-tuple-element.132.place_ref.fplace_ref, bf16[8,384,640]{2,1,0:T(8,128)(2,1)} %bitcast.118, ...), custom_call_target="tpu_custom_call" | custom-call | flops 15728640000 | bytes 40960000 | tf_op jit(solution)/shard_map/pallas_call | solution.py:394
  211.5 43.0 %shard_map.324 = (f32[1600,640]{1,0:T(8,128)}, bf16[1600,640]{1,0:T(8,128)(2,1)}, bf16[8,480,640]{2,1,0:T(8,128)(2,1)}, f32[8,640]{1,0:T(8,128)}, f32[8,2560]{1,0:T(8,128)}) custom-call(s32[9]{0:T(128)} %get-tuple-element.133.place_ref.aplace_ref, s32[9]{0:T(128)} %get-tuple-element.132.place_ref.fplace_ref, bf16[8,192,640]{2,1,0:T(8,128)(2,1)} %copy-done.1, ...), custom_call_target="tpu_custom_call" | custom-call | flops 18350080000 | bytes 40960000 | tf_op jit(solution)/shard_map/pallas_call | solution.py:407
  254.5 36.7 %shard_map.325 = (bf16[1600,640]{1,0:T(8,128)(2,1)}, bf16[1600,640]{1,0:T(8,128)(2,1)}, bf16[1600,640]{1,0:T(8,128)(2,1)}, bf16[8,288,640]{2,1,0:T(8,128)(2,1)}, f32[8,640]{1,0:T(8,128)}) custom-call(s32[4,1,32]{2,1,0:T(1,128)} %bitcast.121, bf16[1600,640]{1,0:T(8,128)(2,1)} %frames_ref.3, f32[16,640]{1,0:T(8,128)} %pad_convert_fusion.vec_ref, ...), custom_call_target="tpu_custom_call" | custom-call | flops 8028160000 | bytes 10240000 | tf_op jit(solution)/shard_map/pallas_call | solution.py:423
  291.3 1.5 constant_dynamic-slice_fusion.11
  294.3 11.4 %shard_map.326 = (bf16[1600,640]{1,0:T(8,128)(2,1)}, f32[8,640]{1,0:T(8,128)}) custom-call(s32[9]{0:T(128)} %get-tuple-element.133.place_ref.aplace_ref, bf16[8,192,640]{2,1,0:T(8,128)(2,1)} %copy-done.1, bf16[8,192,640]{2,1,0:T(8,128)(2,1)} %collective-permute-done.4.other_ref.aother_ref, s32[4,1,32]{2,1,0:T(1,128)} %bitcast.122, ...), custom_call_target="tpu_custom_call" | custom-call | flops 3932160000 | bytes 12288000 | tf_op jit(solution)/shard_map/pallas_call | solution.py:435
  307.2 0.9 slice_reduce_fusion
  308.8 0.9 collective-permute-done.26
  309.7 1.3 collective-permute-start.27
  310.9 2.7 collective-permute-done.27
  313.7 1.2 collective-permute-start.28
  314.8 3.0 constant_dynamic-slice_fusion.3
  318.0 3.6 constant_dynamic-slice_fusion.7
  322.0 1.9 collective-permute-start.30
  323.9 1.8 add_convert_fusion.2
  325.7 1.0 constant_dynamic-slice_fusion.10
  327.5 2.2 collective-permute-start.11
  330.9 0.8 add.344
  331.7 13.7 %collective-permute-done.10 = bf16[2,2,1,1,72,640]{5,4,3,2,1,0:T(8,128)(2,1)} collective-permute-done((bf16[2,2,1,1,72,640]{5,4,3,2,1,0:T(8,128)(2,1)}, bf16[2,2,1,1,72,640]{5,4,3,2,1,0:T(8,128)(2,1)}, u32[]{:S(2)}, u32[]{:S(2)}) %collective-permute-start.10) | collective-permute-done | bytes 368672 | tf_op jit(solution)/shard_map/ppermute | solution.py:460
  345.4 1.2 collective-permute-done.9
  346.7 1.4 add_convert_fusion.5
  348.1 1.4 collective-permute-start.12
  349.5 1.5 collective-permute-start.13
  351.0 1.6 collective-permute-start.14
  353.4 5.2 %collective-permute-done.13 = bf16[1,1,72,640]{3,2,1,0:T(8,128)(2,1)S(1)} collective-permute-done((bf16[1,1,72,640]{3,2,1,0:T(8,128)(2,1)S(1)}, bf16[1,1,72,640]{3,2,1,0:T(8,128)(2,1)S(1)}, u32[]{:S(2)}, u32[]{:S(2)}) %collective-permute-start.13) | collective-permute-done | bytes 92192 | tf_op jit(solution)/shard_map/ppermute | solution.py:460
  358.6 1.4 collective-permute-start.15
  360.7 2.6 collective-permute-done.15
  363.4 2.2 add_convert_fusion.1
  365.8 1.4 collective-permute-start.32
  367.2 1.2 collective-permute-start.33
  368.3 1.0 collective-permute-start.34
  369.5 2.4 add_convert_fusion
  372.1 1.4 collective-permute-start.18
  373.5 1.2 collective-permute-start.19
  374.7 5.1 %collective-permute-done.32 = bf16[2,2,1,1,96,640]{5,4,3,2,1,0:T(8,128)(2,1)S(1)} collective-permute-done((bf16[2,2,1,1,96,640]{5,4,3,2,1,0:T(8,128)(2,1)S(1)}, bf16[2,2,1,1,96,640]{5,4,3,2,1,0:T(8,128)(2,1)S(1)}, u32[]{:S(2)}, u32[]{:S(2)}) %collective-permute-start.32) | collective-permute-done | bytes 491552 | tf_op jit(solution)/shard_map/ppermute | solution.py:462
  379.9 1.9 collective-permute-start.20
  384.1 7.7 %collective-permute-done.33 = bf16[2,2,1,1,96,640]{5,4,3,2,1,0:T(8,128)(2,1)S(1)} collective-permute-done((bf16[2,2,1,1,96,640]{5,4,3,2,1,0:T(8,128)(2,1)S(1)}, bf16[2,2,1,1,96,640]{5,4,3,2,1,0:T(8,128)(2,1)S(1)}, u32[]{:S(2)}, u32[]{:S(2)}) %collective-permute-start.33) | collective-permute-done | bytes 491552 | tf_op jit(solution)/shard_map/ppermute | solution.py:460
  392.1 1.6 collective-permute-start.35
  394.2 9.4 %collective-permute-done.18 = bf16[2,2,1,1,120,640]{5,4,3,2,1,0:T(8,128)(2,1)S(1)} collective-permute-done((bf16[2,2,1,1,120,640]{5,4,3,2,1,0:T(8,128)(2,1)S(1)}, bf16[2,2,1,1,120,640]{5,4,3,2,1,0:T(8,128)(2,1)S(1)}, u32[]{:S(2)}, u32[]{:S(2)}) %collective-permute-start.18) | collective-permute-done | bytes 614432 | tf_op jit(solution)/shard_map/ppermute | solution.py:462
  403.6 1.3 collective-permute-start.37
  404.9 12.3 %collective-permute-done.19 = bf16[2,2,1,1,120,640]{5,4,3,2,1,0:T(8,128)(2,1)S(1)} collective-permute-done((bf16[2,2,1,1,120,640]{5,4,3,2,1,0:T(8,128)(2,1)S(1)}, bf16[2,2,1,1,120,640]{5,4,3,2,1,0:T(8,128)(2,1)S(1)}, u32[]{:S(2)}, u32[]{:S(2)}) %collective-permute-start.19) | collective-permute-done | bytes 614432 | tf_op jit(solution)/shard_map/ppermute | solution.py:460
  417.6 1.6 collective-permute-start.21
  419.7 2.4 collective-permute-start.23
  422.1 1.0 collective-permute-start.38
  423.2 1.0 collective-permute-done.21
  424.2 8.2 %collective-permute-done.22 = bf16[1,1,120,640]{3,2,1,0:T(8,128)(2,1)S(1)} collective-permute-done((bf16[1,1,120,640]{3,2,1,0:T(8,128)(2,1)S(1)}, bf16[1,1,120,640]{3,2,1,0:T(8,128)(2,1)S(1)}, u32[]{:S(2)}, u32[]{:S(2)}) %collective-permute-start.22) | collective-permute-done | bytes 153632 | tf_op jit(solution)/shard_map/ppermute | solution.py:460
  432.5 1.7 collective-permute-start.24
  434.3 3.4 collective-permute-done.24
  438.0 1.1 fusion.3
  439.8 0.8 pad.39
  (157 shorter events, 17.2 us)
Async XLA Ops:
  7.2 3.3 copy-start.3
  7.2 3.3 copy-start.2
  7.2 3.4 copy-start.5
  7.2 3.4 copy-start.4
  7.2 105.7 %all-gather.3.cloned.1.call-start = ((), (), s32[]{:S(2)}) async-start(), calls=%async_computation | async-start | bytes 4423680 | tf_op jit(solution)/shard_map/all_gather | solution.py:574
  10.6 102.3 %copy-start.9 = (bf16[384]{0:T(512)(128)(2,1)S(1)}, bf16[384]{0:T(512)(128)(2,1)}, u32[]{:S(2)}) copy-start(bf16[384]{0:T(512)(128)(2,1)} %param.32) | copy-start | bytes 2308
  10.7 102.3 %copy-start.10 = (bf16[96]{0:T(256)(128)(2,1)S(1)}, bf16[96]{0:T(256)(128)(2,1)}, u32[]{:S(2)}) copy-start(bf16[96]{0:T(256)(128)(2,1)} %param.26) | copy-start | bytes 580
  10.7 102.2 %copy-start.11 = (bf16[96]{0:T(256)(128)(2,1)S(1)}, bf16[96]{0:T(256)(128)(2,1)}, u32[]{:S(2)}) copy-start(bf16[96]{0:T(256)(128)(2,1)} %param.27) | copy-start | bytes 580
  10.7 102.2 %copy-start.12 = (bf16[96]{0:T(256)(128)(2,1)S(1)}, bf16[96]{0:T(256)(128)(2,1)}, u32[]{:S(2)}) copy-start(bf16[96]{0:T(256)(128)(2,1)} %param.28) | copy-start | bytes 580
  10.7 102.2 %copy-start.13 = (bf16[96]{0:T(256)(128)(2,1)S(1)}, bf16[96]{0:T(256)(128)(2,1)}, u32[]{:S(2)}) copy-start(bf16[96]{0:T(256)(128)(2,1)} %param.29) | copy-start | bytes 580
  10.7 102.2 %copy-start.14 = (bf16[96]{0:T(256)(128)(2,1)S(1)}, bf16[96]{0:T(256)(128)(2,1)}, u32[]{:S(2)}) copy-start(bf16[96]{0:T(256)(128)(2,1)} %param.30) | copy-start | bytes 580
  10.7 102.2 %copy-start.15 = (bf16[96]{0:T(256)(128)(2,1)S(1)}, bf16[96]{0:T(256)(128)(2,1)}, u32[]{:S(2)}) copy-start(bf16[96]{0:T(256)(128)(2,1)} %param.37) | copy-start | bytes 580
  10.7 102.2 %copy-start.16 = (bf16[96]{0:T(256)(128)(2,1)S(1)}, bf16[96]{0:T(256)(128)(2,1)}, u32[]{:S(2)}) copy-start(bf16[96]{0:T(256)(128)(2,1)} %param.35) | copy-start | bytes 580
  10.7 102.2 %copy-start.17 = (bf16[96]{0:T(256)(128)(2,1)S(1)}, bf16[96]{0:T(256)(128)(2,1)}, u32[]{:S(2)}) copy-start(bf16[96]{0:T(256)(128)(2,1)} %param.36) | copy-start | bytes 580
  10.7 102.2 %copy-start.18 = (bf16[96]{0:T(256)(128)(2,1)S(1)}, bf16[96]{0:T(256)(128)(2,1)}, u32[]{:S(2)}) copy-start(bf16[96]{0:T(256)(128)(2,1)} %param.34) | copy-start | bytes 580
  10.8 17.0 %collective-permute-start.1 = (bf16[1,192,640]{2,1,0:T(8,128)(2,1)S(1)}, bf16[1,192,640]{2,1,0:T(8,128)(2,1)S(1)}, u32[]{:S(2)}, u32[]{:S(2)}) collective-permute-start(bf16[1,192,640]{2,1,0:T(8,128)(2,1)S(1)} %maximum_select_fusion.1), channel_id=1, source_target_pairs={{0,4},{1,5},{2,6},{3,7},{4,0},{5,1},{6,2},{7,3},{8,12},{9,13},{10,... | collective-permute-start | bytes 737288 | tf_op jit(solution)/shard_map/ppermute | solution.py:460
  27.9 24.6 %collective-permute-start.2 = (bf16[2,192,640]{2,1,0:T(8,128)(2,1)S(1)}, bf16[2,192,640]{2,1,0:T(8,128)(2,1)S(1)}, u32[]{:S(2)}, u32[]{:S(2)}) collective-permute-start(bf16[2,192,640]{2,1,0:T(8,128)(2,1)S(1)} %pad_maximum_fusion.2), channel_id=1, source_target_pairs={{0,2},{1,3},{2,0},{3,1},{4,6},{5,7},{6,4},{7,5},{8,10},{9,11},{10,... | collective-permute-start | bytes 1474568 | tf_op jit(solution)/shard_map/ppermute | solution.py:460
  52.6 61.8 %collective-permute-start.3 = (bf16[4,192,640]{2,1,0:T(8,128)(2,1)S(1)}, bf16[4,192,640]{2,1,0:T(8,128)(2,1)}, u32[]{:S(2)}, u32[]{:S(2)}) collective-permute-start(bf16[4,192,640]{2,1,0:T(8,128)(2,1)S(1)} %pad_maximum_fusion.1), channel_id=1, source_target_pairs={{0,1},{1,0},{2,3},{3,2},{4,5},{5,4},{6,7},{7,6},{8,9},{9,8},{10,11... | collective-permute-start | bytes 2949128 | tf_op jit(solution)/shard_map/ppermute | solution.py:460
  112.9 54.8 %collective-permute-start = (bf16[8,384,640]{2,1,0:T(8,128)(2,1)}, bf16[8,384,640]{2,1,0:T(8,128)(2,1)}, u32[]{:S(2)}, u32[]{:S(2)}) collective-permute-start(bf16[8,384,640]{2,1,0:T(8,128)(2,1)} %bitcast.117), channel_id=1, source_target_pairs={{0,8},{8,0},{16,24},{24,16},{1,9},{9,1},{17,25},{25,17},{2,10},{10... | collective-permute-start | bytes 11796488 | tf_op jit(solution)/shard_map/ppermute | solution.py:462
  113.1 20.1 %collective-permute-start.5 = (bf16[1,1,1248]{2,1,0:T(2,128)(2,1)S(1)}, bf16[1,1,1248]{2,1,0:T(2,128)(2,1)S(1)}, u32[]{:S(2)}, u32[]{:S(2)}) collective-permute-start(bf16[1,1,1248]{2,1,0:T(2,128)(2,1)S(1)} %broadcast_in_dim_reshape.3), channel_id=1, source_target_pairs={{0,4},{1,5},{2,6},{3,7},{4,0},{5,1},{6,2},{7,3},{8,12},{9,13},{10,... | collective-permute-start | bytes 7496 | tf_op jit(solution)/shard_map/ppermute | solution.py:460
  115.9 26.2 %copy-start.1 = (bf16[8,192,640]{2,1,0:T(8,128)(2,1)}, bf16[8,192,640]{2,1,0:T(8,128)(2,1)S(1)}, u32[]{:S(2)}) copy-start(bf16[8,192,640]{2,1,0:T(8,128)(2,1)S(1)} %pad_maximum_fusion.mine_ref.amine_ref) | copy-start | bytes 5898244
  115.9 26.1 %collective-permute-start.4 = (bf16[8,192,640]{2,1,0:T(8,128)(2,1)S(1)}, bf16[8,192,640]{2,1,0:T(8,128)(2,1)}, u32[]{:S(2)}, u32[]{:S(2)}) collective-permute-start(bf16[8,192,640]{2,1,0:T(8,128)(2,1)S(1)} %pad_maximum_fusion.mine_ref.amine_ref), channel_id=1, source_target_pairs={{0,8},{8,0},{16,24},{24,16},{1,9},{9,1},{17,25},{25,17},{2,10},{10... | collective-permute-start | bytes 5898248 | tf_op jit(solution)/shard_map/ppermute | solution.py:462
  133.2 3.7 collective-permute-start.6
  137.0 3.8 collective-permute-start.7
  292.8 31.2 %collective-permute-start.8 = (bf16[2,2,2,1,144,640]{5,4,3,2,1,0:T(8,128)(2,1)S(1)}, bf16[2,2,2,1,144,640]{5,4,3,2,1,0:T(8,128)(2,1)}, u32[]{:S(2)}, u32[]{:S(2)}) collective-permute-start(bf16[2,2,2,1,144,640]{5,4,3,2,1,0:T(8,128)(2,1)S(1)} %constant_dynamic-slice_fusion.11), channel_id=1, source_target_pairs={{0,8},{8,0},{16,24},{24,16},{1,9},{9,1},{17,25},{25,17},{2,10},{10... | collective-permute-start | bytes 4423688 | tf_op jit(solution)/shard_map/ppermute | solution.py:462
  294.3 13.8 %copy-start.8 = (f32[8,640]{1,0:T(8,128)S(1)}, f32[8,640]{1,0:T(8,128)}, u32[]{:S(2)}) copy-start(f32[8,640]{1,0:T(8,128)} %get-tuple-element.63) | copy-start | bytes 61444
  308.2 1.5 collective-permute-start.26
  309.7 4.0 collective-permute-start.27
  313.7 4.2 collective-permute-start.28
  317.8 45.5 %collective-permute-start.31 = (bf16[2,2,2,1,192,640]{5,4,3,2,1,0:T(8,128)(2,1)}, bf16[2,2,2,1,192,640]{5,4,3,2,1,0:T(8,128)(2,1)S(1)}, u32[]{:S(2)}, u32[]{:S(2)}) collective-permute-start(bf16[2,2,2,1,192,640]{5,4,3,2,1,0:T(8,128)(2,1)} %constant_dynamic-slice_fusion.3), channel_id=1, source_target_pairs={{0,8},{8,0},{16,24},{24,16},{1,9},{9,1},{17,25},{25,17},{2,10},{10... | collective-permute-start | bytes 5898248 | tf_op jit(solution)/shard_map/ppermute | solution.py:462
  317.9 4.2 collective-permute-start.29
  317.9 6.0 %copy-start = (bf16[8,288,640]{2,1,0:T(8,128)(2,1)S(1)}, bf16[8,288,640]{2,1,0:T(8,128)(2,1)}, u32[]{:S(2)}) copy-start(bf16[8,288,640]{2,1,0:T(8,128)(2,1)} %get-tuple-element.60) | copy-start | bytes 8847364
  321.5 47.9 %collective-permute-start.17 = (bf16[2,2,2,1,240,640]{5,4,3,2,1,0:T(8,128)(2,1)}, bf16[2,2,2,1,240,640]{5,4,3,2,1,0:T(8,128)(2,1)}, u32[]{:S(2)}, u32[]{:S(2)}) collective-permute-start(bf16[2,2,2,1,240,640]{5,4,3,2,1,0:T(8,128)(2,1)} %constant_dynamic-slice_fusion.7), channel_id=1, source_target_pairs={{0,8},{8,0},{16,24},{24,16},{1,9},{9,1},{17,25},{25,17},{2,10},{10... | collective-permute-start | bytes 7372808 | tf_op jit(solution)/shard_map/ppermute | solution.py:462
  322.0 7.7 %collective-permute-start.30 = (f32[16,640]{1,0:T(8,128)S(1)}, f32[16,640]{1,0:T(8,128)S(1)}, u32[]{:S(2)}, u32[]{:S(2)}) collective-permute-start(f32[16,640]{1,0:T(8,128)S(1)} %add.343), channel_id=1, source_target_pairs={{0,4},{1,5},{2,6},{3,7},{4,0},{5,1},{6,2},{7,3},{8,12},{9,13},{10,... | collective-permute-start | bytes 122888 | tf_op jit(solution)/shard_map/ppermute | solution.py:460
  326.8 18.6 %collective-permute-start.10 = (bf16[2,2,1,1,72,640]{5,4,3,2,1,0:T(8,128)(2,1)}, bf16[2,2,1,1,72,640]{5,4,3,2,1,0:T(8,128)(2,1)}, u32[]{:S(2)}, u32[]{:S(2)}) collective-permute-start(bf16[2,2,1,1,72,640]{5,4,3,2,1,0:T(8,128)(2,1)} %get-tuple-element.76), channel_id=1, source_target_pairs={{0,1},{1,0},{2,3},{3,2},{4,5},{5,4},{6,7},{7,6},{8,9},{9,8},{10,11... | collective-permute-start | bytes 1105928 | tf_op jit(solution)/shard_map/ppermute | solution.py:460
  327.5 17.9 %collective-permute-start.11 = (bf16[2,2,1,1,72,640]{5,4,3,2,1,0:T(8,128)(2,1)}, bf16[2,2,1,1,72,640]{5,4,3,2,1,0:T(8,128)(2,1)}, u32[]{:S(2)}, u32[]{:S(2)}) collective-permute-start(bf16[2,2,1,1,72,640]{5,4,3,2,1,0:T(8,128)(2,1)} %get-tuple-element.75), channel_id=1, source_target_pairs={{0,17},{1,16},{2,19},{3,18},{4,21},{5,20},{6,23},{7,22},{8,25},{9,... | collective-permute-start | bytes 1105928 | tf_op jit(solution)/shard_map/ppermute | solution.py:468
  329.7 0.6 copy-start.7
  330.4 16.3 %collective-permute-start.9 = (bf16[2,2,1,1,72,640]{5,4,3,2,1,0:T(8,128)(2,1)}, bf16[2,2,1,1,72,640]{5,4,3,2,1,0:T(8,128)(2,1)}, u32[]{:S(2)}, u32[]{:S(2)}) collective-permute-start(bf16[2,2,1,1,72,640]{5,4,3,2,1,0:T(8,128)(2,1)} %get-tuple-element.74), channel_id=1, source_target_pairs={{0,16},{8,24},{16,0},{24,8},{1,17},{9,25},{17,1},{25,9},{2,18},{10... | collective-permute-start | bytes 1105928 | tf_op jit(solution)/shard_map/ppermute | solution.py:462
  348.1 5.3 %collective-permute-start.12 = (bf16[1,1,72,640]{3,2,1,0:T(8,128)(2,1)S(1)}, bf16[1,1,72,640]{3,2,1,0:T(8,128)(2,1)S(1)}, u32[]{:S(2)}, u32[]{:S(2)}) collective-permute-start(bf16[1,1,72,640]{3,2,1,0:T(8,128)(2,1)S(1)} %get-tuple-element.98), channel_id=1, source_target_pairs={{0,2},{1,3},{2,0},{3,1},{4,6},{5,7},{6,4},{7,5},{8,10},{9,11},{10,... | collective-permute-start | bytes 276488 | tf_op jit(solution)/shard_map/ppermute | solution.py:460
  349.5 9.0 %collective-permute-start.13 = (bf16[1,1,72,640]{3,2,1,0:T(8,128)(2,1)S(1)}, bf16[1,1,72,640]{3,2,1,0:T(8,128)(2,1)S(1)}, u32[]{:S(2)}, u32[]{:S(2)}) collective-permute-start(bf16[1,1,72,640]{3,2,1,0:T(8,128)(2,1)S(1)} %get-tuple-element.100), channel_id=1, source_target_pairs={{0,4},{1,5},{2,6},{3,7},{4,0},{5,1},{6,2},{7,3},{8,12},{9,13},{10,... | collective-permute-start | bytes 276488 | tf_op jit(solution)/shard_map/ppermute | solution.py:460
  351.0 7.6 %collective-permute-start.14 = (bf16[1,1,72,640]{3,2,1,0:T(8,128)(2,1)S(1)}, bf16[1,1,72,640]{3,2,1,0:T(8,128)(2,1)S(1)}, u32[]{:S(2)}, u32[]{:S(2)}) collective-permute-start(bf16[1,1,72,640]{3,2,1,0:T(8,128)(2,1)S(1)} %get-tuple-element.99), channel_id=1, source_target_pairs={{0,6},{1,7},{2,4},{3,5},{4,2},{5,3},{6,0},{7,1},{8,14},{9,15},{10,... | collective-permute-start | bytes 276488 | tf_op jit(solution)/shard_map/ppermute | solution.py:460
  358.6 4.6 %collective-permute-start.15 = (bf16[72,640]{1,0:T(8,128)(2,1)S(1)}, bf16[72,640]{1,0:T(8,128)(2,1)S(1)}, u32[]{:S(2)}, u32[]{:S(2)}) collective-permute-start(bf16[72,640]{1,0:T(8,128)(2,1)S(1)} %fusion.15), channel_id=1, source_target_pairs={{0,16},{8,24},{16,0},{24,8},{1,17},{9,25},{17,1},{25,9},{2,18},{10... | collective-permute-start | bytes 276488 | tf_op jit(solution)/shard_map/ppermute | solution.py:462
  363.2 6.2 %slice-start = ((s8[4915200]{0:T(1024)(128)(4,1)}), s8[4194304]{0:T(1024)(128)(4,1)S(1)}, s32[]{:S(2)}) async-start(s8[4915200]{0:T(1024)(128)(4,1)} %bitcast.107), calls=%async_computation.1 | async-start | bytes 8388608
  363.3 6.2 %slice-start.1 = ((s8[4915200]{0:T(1024)(128)(4,1)}), s8[720896]{0:T(1024)(128)(4,1)S(1)}, s32[]{:S(2)}) async-start(s8[4915200]{0:T(1024)(128)(4,1)} %bitcast.107), calls=%async_computation.2 | async-start | bytes 1441792
  363.3 6.0 %collective-permute-start.16 = (bf16[144,640]{1,0:T(8,128)(2,1)S(1)}, bf16[144,640]{1,0:T(8,128)(2,1)S(1)}, u32[]{:S(2)}, u32[]{:S(2)}) collective-permute-start(bf16[144,640]{1,0:T(8,128)(2,1)S(1)} %pad_maximum_fusion.5), channel_id=1, source_target_pairs={{0,8},{8,0},{16,24},{24,16},{1,9},{9,1},{17,25},{25,17},{2,10},{10... | collective-permute-start | bytes 552968 | tf_op jit(solution)/shard_map/ppermute | solution.py:462
  365.8 14.1 %collective-permute-start.32 = (bf16[2,2,1,1,96,640]{5,4,3,2,1,0:T(8,128)(2,1)S(1)}, bf16[2,2,1,1,96,640]{5,4,3,2,1,0:T(8,128)(2,1)S(1)}, u32[]{:S(2)}, u32[]{:S(2)}) collective-permute-start(bf16[2,2,1,1,96,640]{5,4,3,2,1,0:T(8,128)(2,1)S(1)} %get-tuple-element.71), channel_id=1, source_target_pairs={{0,16},{8,24},{16,0},{24,8},{1,17},{9,25},{17,1},{25,9},{2,18},{10... | collective-permute-start | bytes 1474568 | tf_op jit(solution)/shard_map/ppermute | solution.py:462
  367.2 24.6 %collective-permute-start.33 = (bf16[2,2,1,1,96,640]{5,4,3,2,1,0:T(8,128)(2,1)S(1)}, bf16[2,2,1,1,96,640]{5,4,3,2,1,0:T(8,128)(2,1)S(1)}, u32[]{:S(2)}, u32[]{:S(2)}) collective-permute-start(bf16[2,2,1,1,96,640]{5,4,3,2,1,0:T(8,128)(2,1)S(1)} %get-tuple-element.73), channel_id=1, source_target_pairs={{0,1},{1,0},{2,3},{3,2},{4,5},{5,4},{6,7},{7,6},{8,9},{9,8},{10,11... | collective-permute-start | bytes 1474568 | tf_op jit(solution)/shard_map/ppermute | solution.py:460
  368.3 23.4 %collective-permute-start.34 = (bf16[2,2,1,1,96,640]{5,4,3,2,1,0:T(8,128)(2,1)S(1)}, bf16[2,2,1,1,96,640]{5,4,3,2,1,0:T(8,128)(2,1)S(1)}, u32[]{:S(2)}, u32[]{:S(2)}) collective-permute-start(bf16[2,2,1,1,96,640]{5,4,3,2,1,0:T(8,128)(2,1)S(1)} %get-tuple-element.72), channel_id=1, source_target_pairs={{0,17},{1,16},{2,19},{3,18},{4,21},{5,20},{6,23},{7,22},{8,25},{9,... | collective-permute-start | bytes 1474568 | tf_op jit(solution)/shard_map/ppermute | solution.py:468
  372.1 31.5 %collective-permute-start.18 = (bf16[2,2,1,1,120,640]{5,4,3,2,1,0:T(8,128)(2,1)S(1)}, bf16[2,2,1,1,120,640]{5,4,3,2,1,0:T(8,128)(2,1)S(1)}, u32[]{:S(2)}, u32[]{:S(2)}) collective-permute-start(bf16[2,2,1,1,120,640]{5,4,3,2,1,0:T(8,128)(2,1)S(1)} %get-tuple-element.68), channel_id=1, source_target_pairs={{0,16},{8,24},{16,0},{24,8},{1,17},{9,25},{17,1},{25,9},{2,18},{10... | collective-permute-start | bytes 1843208 | tf_op jit(solution)/shard_map/ppermute | solution.py:462
  373.5 43.7 %collective-permute-start.19 = (bf16[2,2,1,1,120,640]{5,4,3,2,1,0:T(8,128)(2,1)S(1)}, bf16[2,2,1,1,120,640]{5,4,3,2,1,0:T(8,128)(2,1)S(1)}, u32[]{:S(2)}, u32[]{:S(2)}) collective-permute-start(bf16[2,2,1,1,120,640]{5,4,3,2,1,0:T(8,128)(2,1)S(1)} %get-tuple-element.70), channel_id=1, source_target_pairs={{0,1},{1,0},{2,3},{3,2},{4,5},{5,4},{6,7},{7,6},{8,9},{9,8},{10,11... | collective-permute-start | bytes 1843208 | tf_op jit(solution)/shard_map/ppermute | solution.py:460
  379.9 37.3 %collective-permute-start.20 = (bf16[2,2,1,1,120,640]{5,4,3,2,1,0:T(8,128)(2,1)S(1)}, bf16[2,2,1,1,120,640]{5,4,3,2,1,0:T(8,128)(2,1)S(1)}, u32[]{:S(2)}, u32[]{:S(2)}) collective-permute-start(bf16[2,2,1,1,120,640]{5,4,3,2,1,0:T(8,128)(2,1)S(1)} %get-tuple-element.69), channel_id=1, source_target_pairs={{0,17},{1,16},{2,19},{3,18},{4,21},{5,20},{6,23},{7,22},{8,25},{9,... | collective-permute-start | bytes 1843208 | tf_op jit(solution)/shard_map/ppermute | solution.py:468
  392.1 27.6 %collective-permute-start.35 = (bf16[1,1,96,640]{3,2,1,0:T(8,128)(2,1)S(1)}, bf16[1,1,96,640]{3,2,1,0:T(8,128)(2,1)S(1)}, u32[]{:S(2)}, u32[]{:S(2)}) collective-permute-start(bf16[1,1,96,640]{3,2,1,0:T(8,128)(2,1)S(1)} %get-tuple-element.93), channel_id=1, source_target_pairs={{0,2},{1,3},{2,0},{3,1},{4,6},{5,7},{6,4},{7,5},{8,10},{9,11},{10,... | collective-permute-start | bytes 368648 | tf_op jit(solution)/shard_map/ppermute | solution.py:460
  393.7 28.4 %collective-permute-start.36 = (bf16[1,1,96,640]{3,2,1,0:T(8,128)(2,1)S(1)}, bf16[1,1,96,640]{3,2,1,0:T(8,128)(2,1)S(1)}, u32[]{:S(2)}, u32[]{:S(2)}) collective-permute-start(bf16[1,1,96,640]{3,2,1,0:T(8,128)(2,1)S(1)} %get-tuple-element.95), channel_id=1, source_target_pairs={{0,4},{1,5},{2,6},{3,7},{4,0},{5,1},{6,2},{7,3},{8,12},{9,13},{10,... | collective-permute-start | bytes 368648 | tf_op jit(solution)/shard_map/ppermute | solution.py:460
  403.6 18.5 %collective-permute-start.37 = (bf16[1,1,96,640]{3,2,1,0:T(8,128)(2,1)S(1)}, bf16[1,1,96,640]{3,2,1,0:T(8,128)(2,1)S(1)}, u32[]{:S(2)}, u32[]{:S(2)}) collective-permute-start(bf16[1,1,96,640]{3,2,1,0:T(8,128)(2,1)S(1)} %get-tuple-element.94), channel_id=1, source_target_pairs={{0,6},{1,7},{2,4},{3,5},{4,2},{5,3},{6,0},{7,1},{8,14},{9,15},{10,... | collective-permute-start | bytes 368648 | tf_op jit(solution)/shard_map/ppermute | solution.py:460
  417.6 6.6 %collective-permute-start.21 = (bf16[1,1,120,640]{3,2,1,0:T(8,128)(2,1)S(1)}, bf16[1,1,120,640]{3,2,1,0:T(8,128)(2,1)S(1)}, u32[]{:S(2)}, u32[]{:S(2)}) collective-permute-start(bf16[1,1,120,640]{3,2,1,0:T(8,128)(2,1)S(1)} %get-tuple-element.84), channel_id=1, source_target_pairs={{0,2},{1,3},{2,0},{3,1},{4,6},{5,7},{6,4},{7,5},{8,10},{9,11},{10,... | collective-permute-start | bytes 460808 | tf_op jit(solution)/shard_map/ppermute | solution.py:460
  419.2 13.1 %collective-permute-start.22 = (bf16[1,1,120,640]{3,2,1,0:T(8,128)(2,1)S(1)}, bf16[1,1,120,640]{3,2,1,0:T(8,128)(2,1)S(1)}, u32[]{:S(2)}, u32[]{:S(2)}) collective-permute-start(bf16[1,1,120,640]{3,2,1,0:T(8,128)(2,1)S(1)} %get-tuple-element.86), channel_id=1, source_target_pairs={{0,4},{1,5},{2,6},{3,7},{4,0},{5,1},{6,2},{7,3},{8,12},{9,13},{10,... | collective-permute-start | bytes 460808 | tf_op jit(solution)/shard_map/ppermute | solution.py:460
  419.7 12.7 %collective-permute-start.23 = (bf16[1,1,120,640]{3,2,1,0:T(8,128)(2,1)S(1)}, bf16[1,1,120,640]{3,2,1,0:T(8,128)(2,1)S(1)}, u32[]{:S(2)}, u32[]{:S(2)}) collective-permute-start(bf16[1,1,120,640]{3,2,1,0:T(8,128)(2,1)S(1)} %get-tuple-element.85), channel_id=1, source_target_pairs={{0,6},{1,7},{2,4},{3,5},{4,2},{5,3},{6,0},{7,1},{8,14},{9,15},{10,... | collective-permute-start | bytes 460808 | tf_op jit(solution)/shard_map/ppermute | solution.py:460
  422.1 12.0 %collective-permute-start.38 = (bf16[96,640]{1,0:T(8,128)(2,1)S(1)}, bf16[96,640]{1,0:T(8,128)(2,1)S(1)}, u32[]{:S(2)}, u32[]{:S(2)}) collective-permute-start(bf16[96,640]{1,0:T(8,128)(2,1)S(1)} %fusion.14), channel_id=1, source_target_pairs={{0,16},{8,24},{16,0},{24,8},{1,17},{9,25},{17,1},{25,9},{2,18},{10... | collective-permute-start | bytes 368648 | tf_op jit(solution)/shard_map/ppermute | solution.py:462
  432.5 5.3 %collective-permute-start.24 = (bf16[120,640]{1,0:T(8,128)(2,1)S(1)}, bf16[120,640]{1,0:T(8,128)(2,1)S(1)}, u32[]{:S(2)}, u32[]{:S(2)}) collective-permute-start(bf16[120,640]{1,0:T(8,128)(2,1)S(1)} %fusion.13), channel_id=1, source_target_pairs={{0,16},{8,24},{16,0},{24,8},{1,17},{9,25},{17,1},{25,9},{2,18},{10... | collective-permute-start | bytes 460808 | tf_op jit(solution)/shard_map/ppermute | solution.py:462
  434.2 3.7 collective-permute-start.39
  437.8 1.7 collective-permute-start.25
  439.8 1.1 copy-start.6
Sparse Core Ops, SparseCore 0:
  10.8 102.0 all-gather.2

commit v2 on v1

v2 whole, which is shorter than its diff:
```python
import functools
import jax
import jax.numpy as jnp
from jax import lax
from jax.experimental import pallas as pl
from jax.experimental.pallas import tpu as pltpu
from jax.sharding import PartitionSpec as P

HEADS = 10
HEAD_DIM = 64
FF = 2560
D = 640
FRAMES = 400
SPAN = 10
PAIR = 2 * HEAD_DIM
FIRST_PAIRS = 3
EPS = 1e-05
F32 = jnp.float32
BF16 = jnp.bfloat16
VMEM_LIMIT = 60 * 1024 * 1024
HID = 512


def dot_nn(a, b):
    return lax.dot_general(a, b, (((1,), (0,)), ((), ())), preferred_element_type=F32)


def dot_nt(a, b):
    return lax.dot_general(a, b, (((1,), (1,)), ((), ())), preferred_element_type=F32)


def dot_tn(a, b):
    return lax.dot_general(a, b, (((0,), (0,)), ((), ())), preferred_element_type=F32)


def mean_last(a):
    return jnp.mean(a, axis=-1, keepdims=True)


def rows_sum(a):
    return jnp.sum(a, axis=0, keepdims=True)


def masked_frames(starts_ref):
    places = lax.broadcasted_iota(jnp.int32, (FRAMES, starts_ref.shape[-1]), 0)
    ahead = places - starts_ref[0]
    inside = jnp.where((ahead >= 0) & (ahead < SPAN), 1.0, 0.0)
    return jnp.max(inside, axis=1, keepdims=True) > 0.5


def fetch(place_ref, sem, *wanted):
    def copies(arrays, role, parts):
        for group, source in enumerate(arrays):
            for piece in range(source.shape[0]):
                owner = place_ref[1] ^ (piece * len(arrays) + group)
                for core, first, rows, stride, row, column, target in parts:
                    if core == role:
                        low = pl.multiple_of(owner * stride + row, 16)
                        yield pltpu.make_async_copy(
                            source.at[piece, pl.ds(first, rows), :],
                            target.at[pl.ds(low, rows), pl.ds(column, D)],
                            sem,
                        )

    for core in (0, 1):

        @pl.when(place_ref[0] == core)
        def _(core=core):
            started = []
            for (mine, other), parts in wanted:
                started += list(copies(mine, core, parts)) + list(copies(other, 1 - core, parts))
            for copy in started:
                copy.start()
            for copy in started:
                copy.wait()


def attn_parts(one, two, rows):
    parts = [(0, 0, rows, rows, 0, 0, one), (1, 0, rows, rows, 0, 0, two)]
    return [part for part in parts if part[-1] is not None]


def up_parts(target, rows):
    return [(j // 2, (j % 2) * rows, rows, rows, 0, j * D, target) for j in range(FF // D)]


def down_parts(target, rows):
    return [(core, 0, rows // 2, rows, core * (rows // 2), 0, target) for core in (0, 1)]


def attn_forward(
    place_ref, one, two, starts_ref, frames_ref, vec_ref,
    q_ref, k_ref, v_ref, o_ref, lse_ref, n1_ref, rstd_ref,
    wq_ref, wk_ref, wv_ref, wo_ref, sem, *, rows,
):
    @pl.when(pl.program_id(0) == 0)
    def _():
        fetch(
            place_ref, sem,
            (one, attn_parts(wq_ref, wk_ref, rows)), (two, attn_parts(wv_ref, wo_ref, rows)),
        )

    bq, bv, bo = vec_ref[0:1, :], vec_ref[1:2, :], vec_ref[2:3, :]
    x0 = jnp.where(masked_frames(starts_ref), vec_ref[5:6, :], frames_ref[...].astype(F32))
    h = x0.astype(BF16)
    scale = HEAD_DIM ** (-0.5)
    q_ref[...] = ((dot_nn(h, wq_ref[0:D, :]) + bq).astype(BF16).astype(F32) * scale).astype(BF16)
    k_ref[...] = dot_nn(h, wk_ref[0:D, :]).astype(BF16)
    v_ref[...] = (dot_nn(h, wv_ref[0:D, :]) + bv).astype(BF16)
    low_lanes = lax.broadcasted_iota(jnp.int32, (FRAMES, PAIR), 1) < HEAD_DIM
    lanes = lax.broadcasted_iota(jnp.int32, (FRAMES, 128), 1)
    lse = jnp.zeros((FRAMES, 128), F32)
    for pair in range(HEADS // 2):
        cols = slice(pair * PAIR, (pair + 1) * PAIR)
        qp, kp, vp = q_ref[:, cols], k_ref[:, cols], v_ref[:, cols]
        parts = []
        for half in range(2):
            keep = low_lanes if half == 0 else jnp.logical_not(low_lanes)
            qh = jnp.where(keep, qp.astype(F32), 0.0).astype(BF16)
            scores = dot_nt(qh, kp)
            top = jnp.max(scores, axis=-1, keepdims=True)
            expo = jnp.exp(scores - top)
            total = jnp.sum(expo, axis=-1, keepdims=True)
            parts.append(dot_nn(expo.astype(BF16), vp) * (1.0 / total))
            lse = jnp.where(lanes == 2 * pair + half, top + jnp.log(total), lse)
        o_ref[:, cols] = jnp.where(low_lanes, parts[0], parts[1]).astype(BF16)
    lse_ref[0] = jnp.transpose(lse)[0:16, :]
    r1 = x0 + (dot_nn(o_ref[...], wo_ref[0:D, :]) + bo)
    center = r1 - mean_last(r1)
    rstd = lax.rsqrt(mean_last(center * center) + EPS)
    n1_ref[...] = center * rstd
    rstd_ref[...] = rstd


def gelu_parts(u):
    bell = jnp.exp(u * u * -0.5)
    t = 1.0 / (1.0 + (0.3275911 * 0.7071067811865476) * jnp.abs(u))
    poly = t * (
        0.5 * 0.254829592
        + t * (0.5 * -0.284496736 + t * (0.5 * 1.421413741 + t * (0.5 * -1.453152027 + t * (0.5 * 1.061405429))))
    )
    tail = poly * bell
    phi = jnp.where(u >= 0, 1.0 - tail, tail)
    return u * phi, phi + u * bell * 0.3989422804014327


def ffn_up(place_ref, up, n1_ref, vec_ref, b1_ref, hidden_ref, slope_ref, w1_ref, sem, *, rows):
    @pl.when(pl.program_id(0) == 0)
    def _():
        fetch(place_ref, sem, (up, up_parts(w1_ref, rows)))

    y1b = (vec_ref[3:4, :] * n1_ref[...] + vec_ref[4:5, :]).astype(BF16)
    for c in range(FF // HID):
        cols = slice(c * HID, (c + 1) * HID)
        u = dot_nn(y1b, w1_ref[0:D, cols]) + b1_ref[0:1, cols]
        act, slope = gelu_parts(u)
        hidden_ref[:, cols] = act.astype(BF16)
        slope_ref[:, cols] = slope.astype(BF16)


def ffn_down(
    place_ref, down, n1_ref, hidden_ref, cot_ref, vec_ref,
    out_ref, dz_ref, dr2_ref, small_ref, *rest, rows, halves,
):
    grads_refs, (acc, w2_ref, sem) = rest[:-3], rest[-3:]
    step = pl.program_id(0)

    @pl.when(step == 0)
    def _():
        small_ref[...] = jnp.zeros_like(small_ref)
        acc[...] = jnp.zeros_like(acc)
        fetch(place_ref, sem, (down, down_parts(w2_ref, rows)))

    g1, s1, g2, s2, b2 = (vec_ref[i : i + 1, :] for i in (3, 4, 6, 7, 8))
    y1 = g1 * n1_ref[...] + s1
    r2 = y1 + (dot_nn(hidden_ref[...], w2_ref[0:FF, :]) + b2)
    center = r2 - mean_last(r2)
    rstd = lax.rsqrt(mean_last(center * center) + EPS)
    n2 = center * rstd
    out_ref[...] = (n2 * g2 + s2).astype(BF16)
    dy = cot_ref[...].astype(F32)
    e = dy * g2
    dr2 = (e - mean_last(e) - n2 * mean_last(e * n2)) * rstd
    dz = dr2.astype(BF16)
    dr2_ref[...] = dr2
    dz_ref[...] = dz
    small_ref[0:1, :] += rows_sum(dz.astype(F32))
    small_ref[1:2, :] += rows_sum(dy * n2)
    small_ref[2:3, :] += rows_sum(dy)
    acc[0:FF, :] += dot_tn(hidden_ref[...], dz)

    @pl.when(step == pl.num_programs(0) - 1)
    def _():
        deliver(place_ref, grads_refs, [(acc, 0, rows)], halves)


def deliver(place_ref, refs, sources, halves):
    if not halves:
        for ref, (acc, column, _) in zip(refs, sources):
            ref[...] = acc[:, column : column + ref.shape[1]].astype(BF16)
        return
    for ref, core in zip(refs, (place_ref[0], 1 - place_ref[0])):
        owners, parts, _, width = ref.shape
        for owner in range(owners):
            for part in range(parts):
                pieces = []
                for acc, column, rows in sources:
                    size = rows // 4
                    low = pl.multiple_of(owner * rows + (2 * core + part) * size, 8)
                    pieces.append(acc[pl.ds(low, size), column : column + width])
                ref[owner, part] = jnp.concatenate(pieces, axis=0).astype(BF16)


def ffn_backward(
    place_ref, two, up, down, n1_ref, rstd_ref, dz_ref, dr2_ref, slope_ref, o_ref, vec_ref,
    dr1_ref, do_ref, small_ref, db1_ref, *rest, rows, halves,
):
    grads_refs = rest[:-7]
    grad_pre, acc1, acco, w1_ref, w2_ref, wo_ref, sem = rest[-7:]
    step = pl.program_id(0)

    @pl.when(step == 0)
    def _():
        small_ref[...] = jnp.zeros_like(small_ref)
        db1_ref[...] = jnp.zeros_like(db1_ref)
        acc1[...] = jnp.zeros_like(acc1)
        acco[...] = jnp.zeros_like(acco)
        fetch(
            place_ref, sem,
            (two, attn_parts(None, wo_ref, rows[0])), (up, up_parts(w1_ref, rows[0])), (down, down_parts(w2_ref, rows[1])),
        )

    g1, s1 = vec_ref[3:4, :], vec_ref[4:5, :]
    n1 = n1_ref[...]
    y1b = (g1 * n1 + s1).astype(BF16)
    dz = dz_ref[...]
    for c in range(FF // HID):
        cols = slice(c * HID, (c + 1) * HID)
        du = (dot_nt(dz, w2_ref[cols, :]) * slope_ref[:, cols].astype(F32)).astype(BF16)
        grad_pre[:, cols] = du
        db1_ref[0:1, cols] += rows_sum(du.astype(F32))
    acc1[0:D, :] += dot_tn(y1b, grad_pre[...])
    dy1 = dot_nt(grad_pre[...], w1_ref[0:D, :]) + dr2_ref[...]
    e = dy1 * g1
    dr1 = (e - mean_last(e) - n1 * mean_last(e * n1)) * rstd_ref[...]
    dr1_ref[...] = dr1
    da = dr1.astype(BF16)
    small_ref[0:1, :] += rows_sum(da.astype(F32))
    small_ref[1:2, :] += rows_sum(dy1 * n1)
    small_ref[2:3, :] += rows_sum(dy1)
    acco[0:D, :] += dot_tn(o_ref[...], da)
    do_ref[...] = dot_nt(da, wo_ref[0:D, :]).astype(BF16)

    @pl.when(step == pl.num_programs(0) - 1)
    def _():
        sources = [(acc1, j * D, rows[0]) for j in range(FF // D)] + [(acco, 0, rows[0])]
        deliver(place_ref, grads_refs, sources, halves)


def attn_backward(
    place_ref, starts_ref, frames_ref, vec_ref, q_ref, k_ref, v_ref, do_ref, lse_ref,
    dq_ref, dk_ref, dv_ref, small_ref, *rest, first, rows, halves,
):
    grads_refs, (accq, acck, accv) = rest[:-3], rest[-3:]
    step = pl.program_id(0)

    @pl.when(step == 0)
    def _():
        small_ref[...] = jnp.zeros_like(small_ref)
        accq[...] = jnp.zeros_like(accq)
        acck[...] = jnp.zeros_like(acck)
        accv[...] = jnp.zeros_like(accv)

    scale = HEAD_DIM ** (-0.5)
    low_lanes = lax.broadcasted_iota(jnp.int32, (FRAMES, PAIR), 1) < HEAD_DIM
    for pair in range(dq_ref.shape[1] // PAIR):
        source = slice((first + pair) * PAIR, (first + pair + 1) * PAIR)
        cols = slice(pair * PAIR, (pair + 1) * PAIR)
        qp, kp, vp, dop = q_ref[:, source], k_ref[:, source], v_ref[:, source], do_ref[:, source]
        parts = []
        for half in range(2):
            keep = low_lanes if half == 0 else jnp.logical_not(low_lanes)
            kh = jnp.where(keep, kp.astype(F32), 0.0).astype(BF16)
            vh = jnp.where(keep, vp.astype(F32), 0.0).astype(BF16)
            head = 2 * (first + pair) + half
            prob = jnp.exp(dot_nt(kh, qp) - lse_ref[0, head : head + 1, :])
            dprob = dot_nt(vh, dop)
            inner = jnp.sum(prob * dprob, axis=0, keepdims=True)
            dscore = (prob * (dprob - inner)).astype(BF16)
            parts.append((dot_nn(prob.astype(BF16), dop), dot_nn(dscore, qp), dot_tn(dscore, kp) * scale))
        for ref, one, two in zip((dv_ref, dk_ref, dq_ref), *parts):
            ref[:, cols] = jnp.where(low_lanes, one, two).astype(BF16)
    x0 = jnp.where(masked_frames(starts_ref), vec_ref[5:6, :], frames_ref[...].astype(F32))
    h = x0.astype(BF16)
    accq[0:D, :] += dot_tn(h, dq_ref[...])
    acck[0:D, :] += dot_tn(h, dk_ref[...])
    accv[0:D, :] += dot_tn(h, dv_ref[...])
    small_ref[0:1, :] += rows_sum(dq_ref[...].astype(F32))
    small_ref[1:2, :] += rows_sum(dv_ref[...].astype(F32))

    @pl.when(step == pl.num_programs(0) - 1)
    def _():
        deliver(place_ref, grads_refs, [(acc, 0, rows) for acc in (accq, acck, accv)], halves)


def input_backward(
    place_ref, one, two, starts_ref, dr1_ref, *rest, rows,
):
    parts, (grad_ref, small_ref, wq_ref, wk_ref, wv_ref, sem) = rest[:-6], rest[-6:]

    @pl.when(pl.program_id(0) == 0)
    def _():
        small_ref[...] = jnp.zeros_like(small_ref)
        fetch(
            place_ref, sem,
            (one, attn_parts(wq_ref, wk_ref, rows)), (two, attn_parts(wv_ref, None, rows)),
        )

    masked = masked_frames(starts_ref)
    dx0 = dr1_ref[...]
    column = 0
    for group in range(0, len(parts), 3):
        width = parts[group].shape[1]
        for grad, weight in zip(parts[group : group + 3], (wq_ref, wk_ref, wv_ref)):
            dx0 += dot_nt(grad[...], weight[0:D, column : column + width])
        column += width
    grad_ref[...] = jnp.where(masked, 0.0, dx0).astype(BF16)
    small_ref[0:1, :] += rows_sum(jnp.where(masked, dx0, 0.0))


def row_blocks(width):
    return pl.BlockSpec((FRAMES, width), lambda i, *_: (i, 0))


def kept(rows, cols):
    return pl.BlockSpec((rows, cols), lambda i, *_: (0, 0), pipeline_mode=pl.Buffered(1))


def held(*sizes):
    return pl.BlockSpec(sizes, lambda i, *_: (0,) * len(sizes))


def shape(*sizes, dtype=BF16):
    return jax.ShapeDtypeStruct(sizes, dtype)


SCALARS = pl.BlockSpec(memory_space=pltpu.SMEM)
WHOLE = pl.BlockSpec(memory_space=pl.ANY)
COPIES = pltpu.SemaphoreType.DMA(())


def call(body, steps, place, units, operands, in_specs, outputs, scratch=(), after=(), flops=0, moved=0):
    flat = [array for unit in units for arrays in unit for array in arrays]

    def kernel(place_ref, *refs):
        refs = refs[len(after) :]
        given = []
        for mine, other in units:
            given.append((refs[: len(mine)], refs[len(mine) : len(mine) + len(other)]))
            refs = refs[len(mine) + len(other) :]
        body(place_ref, *given, *refs)

    return pl.pallas_call(
        kernel,
        grid=(steps,),
        in_specs=[SCALARS] + [WHOLE] * (len(after) + len(flat)) + in_specs,
        out_specs=[spec for spec, _ in outputs],
        out_shape=[out for _, out in outputs],
        scratch_shapes=list(scratch),
        compiler_params=pltpu.CompilerParams(
            dimension_semantics=("arbitrary",), vmem_limit_bytes=VMEM_LIMIT
        ),
        cost_estimate=pl.CostEstimate(flops=int(flops), bytes_accessed=int(moved), transcendentals=0),
    )(place, *after, *flat, *operands)


def starts_spec(starts):
    return pl.BlockSpec((1, 1, starts.shape[-1]), lambda i: (i, 0, 0))


def lse_spec():
    return pl.BlockSpec((1, 16, FRAMES), lambda i: (i, 0, 0))


def weights(*sizes):
    return [pltpu.VMEM(size, BF16) for size in sizes] + [COPIES]


def by_rows(rows, width, dtype=BF16):
    return (row_blocks(width), shape(rows, width, dtype=dtype))


def summed(rows, width):
    return (held(rows, width), shape(rows, width, dtype=F32))


def grads_out(halves, sources):
    if not halves:
        return [(held(rows, width), shape(rows, width)) for rows, width, _ in sources]
    rows, width, count = sources[0]
    sizes = (rows // count, 2, sum(part[2] for part in sources) // 4, width)
    return [(held(*sizes), shape(*sizes))] * 2


class Layer:
    def __init__(self, place, starts, frames, vec, b1, d_rows, ff_rows, d_max, ff_max, halves):
        self.place, self.starts, self.frames, self.vec, self.b1 = place, starts, frames, vec, b1
        self.d_rows, self.ff_rows, self.d_max, self.ff_max, self.halves = d_rows, ff_rows, d_max, ff_max, halves
        self.rows = frames.shape[0]
        self.steps = self.rows // FRAMES

    def attn_forward(self, one, two, after=()):
        rows = self.rows
        return call(
            functools.partial(attn_forward, rows=self.d_rows), self.steps, self.place, (one, two),
            (self.starts, self.frames, self.vec), [starts_spec(self.starts), row_blocks(D), kept(16, D)],
            [by_rows(rows, D)] * 4
            + [(lse_spec(), shape(self.steps, 16, FRAMES, dtype=F32)), by_rows(rows, D, F32), by_rows(rows, 1, F32)],
            weights(*[(self.d_max, D)] * 4), after,
            flops=rows * D * D * 8 + rows * FRAMES * D * 16, moved=rows * D * 14,
        )

    def ffn_up(self, up, n1, after=()):
        rows = self.rows
        return call(
            functools.partial(ffn_up, rows=self.d_rows), self.steps, self.place, (up,),
            (n1, self.vec, self.b1), [row_blocks(D), kept(16, D), kept(8, FF)],
            [by_rows(rows, FF)] * 2, weights((self.d_max, FF)), after,
            flops=rows * D * FF * 4, moved=rows * FF * 6,
        )

    def ffn_down(self, down, n1, hidden, cotangent, halves, after=()):
        rows = self.rows
        return call(
            functools.partial(ffn_down, rows=self.ff_rows, halves=halves), self.steps, self.place, (down,),
            (n1, hidden, cotangent, self.vec), [row_blocks(D), row_blocks(FF), row_blocks(D), kept(16, D)],
            [by_rows(rows, D), by_rows(rows, D), by_rows(rows, D, F32), summed(8, D)]
            + grads_out(halves, [(self.ff_max, D, self.ff_rows)]),
            [pltpu.VMEM((self.ff_max, D), F32)] + weights((self.ff_max, D)), after,
            flops=rows * D * FF * 6, moved=rows * FF * 8,
        )

    def ffn_backward(self, two, up, down, n1, rstd, dz, dr2, slope, o, after=()):
        rows = self.rows
        return call(
            functools.partial(ffn_backward, rows=(self.d_rows, self.ff_rows), halves=self.halves),
            self.steps, self.place, (two, up, down), (n1, rstd, dz, dr2, slope, o, self.vec),
            [row_blocks(w) for w in (D, 1, D, D, FF, D)] + [kept(16, D)],
            [by_rows(rows, D, F32), by_rows(rows, D), summed(8, D), summed(8, FF)]
            + grads_out(
                self.halves,
                [(self.d_max, D, self.d_rows)] * 5,
            ),
            [pltpu.VMEM((FRAMES, FF), BF16), pltpu.VMEM((self.d_max, FF), F32), pltpu.VMEM((self.d_max, D), F32)]
            + weights((self.d_max, FF), (self.ff_max, D), (self.d_max, D)), after,
            flops=rows * D * FF * 8 + rows * D * D * 4, moved=rows * FF * 8,
        )

    def attn_backward(self, first, pairs, q, k, v, do, lse, after=()):
        rows, width = self.rows, pairs * PAIR
        return call(
            functools.partial(attn_backward, first=first, rows=self.d_rows, halves=self.halves),
            self.steps, self.place, (), (self.starts, self.frames, self.vec, q, k, v, do, lse),
            [starts_spec(self.starts), row_blocks(D), kept(16, D)] + [row_blocks(D)] * 4 + [lse_spec()],
            [by_rows(rows, width)] * 3 + [summed(8, width)]
            + grads_out(self.halves, [(self.d_max, width, self.d_rows)] * 3),
            [pltpu.VMEM((self.d_max, width), F32)] * 3, after,
            flops=rows * D * width * 6 + rows * FRAMES * width * 40, moved=rows * D * 10,
        )

    def input_backward(self, one, two, dr1, parts, after=()):
        rows = self.rows
        return call(
            functools.partial(input_backward, rows=self.d_rows), self.steps, self.place, (one, two),
            (self.starts, dr1, *parts),
            [starts_spec(self.starts), row_blocks(D)] + [row_blocks(part.shape[1]) for part in parts],
            [by_rows(rows, D), summed(8, D)], weights(*[(self.d_max, D)] * 3), after,
            flops=rows * D * D * 8, moved=rows * D * 12,
        )


def local(kernel, outputs, place, operands, scratch=(), cost=0):
    count = len(operands)

    def body(place_ref, *refs):
        sources, outs = refs[:count], refs[count : count + len(outputs)]
        held_refs, sems = refs[count + len(outputs) : -1], refs[-1]
        copies = [
            pltpu.make_async_copy(source, target, sems.at[i])
            for i, (source, target) in enumerate(zip(sources, held_refs))
        ]
        for copy in copies:
            copy.start()
        for copy in copies:
            copy.wait()
        kernel(place_ref, held_refs, outs)

    vmem = pl.BlockSpec(memory_space=pltpu.VMEM)
    return pl.pallas_call(
        body,
        in_specs=[SCALARS] + [WHOLE] * count,
        out_specs=[vmem] * len(outputs),
        out_shape=outputs,
        scratch_shapes=[pltpu.VMEM(array.shape, array.dtype) for array in operands]
        + [pltpu.SemaphoreType.DMA((count,))],
        compiler_params=pltpu.CompilerParams(vmem_limit_bytes=VMEM_LIMIT),
        cost_estimate=pl.CostEstimate(flops=1000, bytes_accessed=4 * sum(a.size for a in operands), transcendentals=0),
    )(place, *operands)


def first_sums(place, kept_half, received):
    owners, _, rows, width = kept_half.shape

    def kernel(place_ref, refs, outs):
        for j in range(4):
            for z in range(owners // 2):
                owner, part = 2 * z + ((place_ref[1] % 2) ^ (j // 2)), place_ref[2] ^ (j % 2)
                outs[j][z] = (refs[0][owner, part].astype(F32) + refs[1][owner, part].astype(F32)).astype(BF16)

    return local(kernel, [shape(owners // 2, rows, width)] * 4, place, [kept_half, received])


def next_sums(place, parts, split):
    rows, width = parts[0].shape[-2:]

    def kernel(place_ref, refs, outs):
        for j, out in enumerate(outs):
            pick = (lambda ref, j=j: ref[(place_ref[1] // 2) ^ j]) if split else (lambda ref: ref[...])
            total = pick(refs[0]).astype(F32)
            for ref in refs[1:]:
                total = total + pick(ref).astype(F32)
            out[...] = total.astype(BF16)

    return local(kernel, [shape(rows, width)] * (4 if split else 1), place, parts)


def finish(place, groups, outputs):
    def kernel(place_ref, refs, outs):
        for ref in outs:
            ref[:, D:] = jnp.zeros((ref.shape[0], ref.shape[1] - D), F32)
        for index in range(len(groups)):
            for j in range(4):
                value = refs[4 * index + j][...].astype(F32)
                quarter = 2 * (place_ref[0] ^ (j // 2)) + (place_ref[2] ^ (j % 2))
                for ref, (rows, _, sources) in zip(outs, outputs):
                    size = rows // 4
                    for source, weight, column in sources:
                        if source == index:
                            ref[pl.ds(pl.multiple_of(quarter * size, 8), size), column : column + value.shape[1]] = (
                                value[weight * size : (weight + 1) * size]
                            )

    return local(
        kernel, [shape(rows, cols, dtype=F32) for rows, cols, _ in outputs], place,
        [array for group in groups for array in group],
    )


def unpack(place, stacks, first, count, wide, names):
    owners = 2 * stacks[0].shape[0]

    def kernel(place_ref, refs, outs):
        vec_ref, wide_ref = outs
        lanes = lax.broadcasted_iota(jnp.int32, (16, owners * count), 1)
        total = jnp.zeros((16, owners * count), F32)
        for code in range(owners):
            owner = place_ref[1] ^ code
            rows = refs[code % 2][code // 2, first : first + 16, :].astype(F32)
            row = jnp.pad(rows[:, :count], ((0, 0), (0, (owners - 1) * count)))
            total = total + pltpu.roll(row, owner * count, 1)
            wide_ref[:, pl.ds(pl.multiple_of(owner * wide, 128), wide)] = jnp.broadcast_to(
                rows[names : names + 1, :wide], (8, wide)
            )
        vec_ref[...] = total[:, :D]

    return local(
        kernel, [shape(16, D, dtype=F32), shape(8, owners * wide, dtype=F32)], place, stacks
    )


def small_total(place, attn_a, attn_b, one, mask, two, wide):
    def kernel(place_ref, refs, outs):
        a, b, first, masked, second, broad = (ref[...] for ref in refs)
        rows = [jnp.concatenate([a[0:2], b[0:2]], axis=1), first[0:3], masked[0:1], second[1:3], second[0:1]]
        rows += [broad[0:1, j * D : (j + 1) * D] for j in range(FF // D)]
        rows.append(jnp.zeros((16 - len(VECTORS) - FF // D, D), F32))
        row = 0
        for part in rows:
            outs[0][row : row + part.shape[0], :] = part
            row += part.shape[0]

    return local(kernel, [shape(16, D, dtype=F32)], place, [attn_a, attn_b, one, mask, two, wide])[0]


def tie(value, *before):
    return lax.optimization_barrier((value, *before))[0]


def in_order(value, order):
    return jnp.concatenate([lax.dynamic_slice_in_dim(value, order[i], 1) for i in range(value.shape[0])])


class Grid:
    def __init__(self, dp, fsdp):
        self.dp, self.fsdp = dp, fsdp
        self.dp_bits = [1 << i for i in range(dp.bit_length() - 1)]
        self.fsdp_bits = [1 << i for i in range(fsdp.bit_length() - 1)]

    def bit(self, axis, bit):
        return (lax.axis_index(axis) // bit) % 2

    def swap(self, value, dp_mask, fsdp_mask):
        if not dp_mask:
            return lax.ppermute(value, "fsdp", [(i, i ^ fsdp_mask) for i in range(self.fsdp)])
        if not fsdp_mask:
            return lax.ppermute(value, "dp", [(i, i ^ dp_mask) for i in range(self.dp)])
        pairs = [
            (i * self.fsdp + j, (i ^ dp_mask) * self.fsdp + (j ^ fsdp_mask))
            for i in range(self.dp)
            for j in range(self.fsdp)
        ]
        return lax.ppermute(value, ("dp", "fsdp"), pairs)

    def gather(self, piece):
        gathered = piece[None]
        for bit in self.fsdp_bits:
            gathered = jnp.concatenate([gathered, self.swap(gathered, 0, bit)])
        return gathered

    def from_far(self, piece):
        return [piece] + [self.swap(piece, 0, 2 * code) for code in range(1, self.fsdp // 2)]

    def stages(self):
        dp_left, fsdp_left = self.dp_bits[1:], list(self.fsdp_bits)
        order = [[("dp", 1)]]
        while dp_left and fsdp_left:
            order.append([("dp", dp_left.pop(0)), ("fsdp", fsdp_left.pop(0))])
        order += [[("dp", bit)] for bit in dp_left]
        while fsdp_left:
            order.append([("fsdp", bit) for bit in fsdp_left[:2]])
            fsdp_left = fsdp_left[2:]
        return order

    def reduce(self, grads):
        rows, width = grads.shape[1:]
        left = list(reversed(self.fsdp_bits))
        value = grads.reshape((2,) * len(left) + (rows, width))
        halved = []
        for stage in self.stages():
            for axis, bit in stage:
                if axis == "dp":
                    value = value.reshape(value.shape[:-2] + (2, value.shape[-2] // 2, width))
                    halved.append(bit)
            spots = {}
            extra = len(left)
            for axis, bit in stage:
                if axis == "dp":
                    spots[(axis, bit)] = extra
                    extra += 1
                else:
                    spots[(axis, bit)] = left.index(bit)
            total = None
            for code in range(1 << len(stage)):
                starts = [0] * value.ndim
                sizes = list(value.shape)
                masks = {"dp": 0, "fsdp": 0}
                for place, (axis, bit) in enumerate(stage):
                    other = (code >> place) & 1
                    starts[spots[(axis, bit)]] = self.bit(axis, bit) ^ other
                    sizes[spots[(axis, bit)]] = 1
                    masks[axis] += bit * other
                part = lax.dynamic_slice(value, starts, sizes)
                if code:
                    part = self.swap(part, masks["dp"], masks["fsdp"])
                part = part.astype(F32)
                total = part if total is None else total + part
            total = jnp.squeeze(total, tuple(spots.values()))
            left = [bit for bit in left if ("fsdp", bit) not in spots]
            value = total.astype(BF16)
        for bit in reversed(halved):
            other = self.swap(value, bit, 0)
            first = self.bit("dp", bit) == 0
            value = jnp.concatenate([jnp.where(first, value, other), jnp.where(first, other, value)])
        return value.astype(F32)

    def total(self, value):
        for bit in self.dp_bits:
            value = value + self.swap(value, bit, 0)
        for bit in self.fsdp_bits:
            value = value + self.swap(value, 0, bit)
        return value


def packed_vectors(rows, count, wide, names):
    owners = rows.shape[0]
    vec = rows[:, : names * count].reshape(owners, names, count)
    vec = jnp.swapaxes(vec, 0, 1).reshape(names, owners * count)[:, :D].astype(F32)
    b1 = rows[:, names * count : names * count + wide].reshape(1, -1)[:, :FF].astype(F32)
    return jnp.pad(vec, ((0, 16 - names), (0, 0))), jnp.broadcast_to(b1, (8, FF))


VECTORS = ("qb", "vb", "ob", "g1", "s1", "m", "g2", "s2", "b2")


def vector_grads(small, count, wide, d_max, ff_max):
    me = lax.axis_index("fsdp")
    rows = jnp.pad(small[: len(VECTORS)], ((0, 0), (0, d_max - D)))
    rows = lax.dynamic_slice(rows, (0, me * count), (len(VECTORS), count))
    grads = {name: rows[i] for i, name in enumerate(VECTORS)}
    b1 = jnp.pad(small[len(VECTORS) : len(VECTORS) + FF // D].reshape(-1), (0, ff_max - FF))
    grads["b1"] = lax.dynamic_slice(b1, (me * wide,), (wide,))
    return grads


def small_rows(attn, one, mask, two, wide):
    return jnp.concatenate(
        [attn[0:2], one[0:3], mask[0:1], two[1:3], two[0:1], wide[0].reshape(FF // D, D), jnp.zeros((3, D), F32)]
    )


def in_columns(weight):
    return [weight[:, j * D : (j + 1) * D] for j in range(FF // D)]


def any_grid(grid, frames, cotangent, span_starts, matrices, vectors, up_bias):
    query, key, value, out, up, down = matrices
    count, wide = query.shape[0], down.shape[0]
    owners = grid.fsdp
    d_max, ff_max = count * owners, wide * owners
    me, core = lax.axis_index("fsdp"), lax.axis_index("dp") % 2
    codes = me ^ jnp.arange(owners, dtype=jnp.int32)

    def gathered(pieces):
        stack = in_order(grid.gather(jnp.concatenate(pieces)), codes)
        stack = stack.reshape(owners, len(pieces), -1, D)
        return [stack[:, i].reshape(-1, D) for i in range(len(pieces))]

    packed = jnp.concatenate(vectors + [up_bias]).reshape(1, -1)
    packed = in_order(grid.gather(packed)[:, 0], codes)
    vec, b1 = packed_vectors(packed, count, wide, len(vectors))
    wq, wk, wv, wo = gathered([piece[:, :D] for piece in (query, key, value, out)])
    up_blocks = gathered(in_columns(up))
    (w2,) = gathered([down[:, :D]])

    def unit(role_zero, role_one):
        first = core == 0
        return ([jnp.where(first, role_zero, role_one)[None]], [jnp.where(first, role_one, role_zero)[None]])

    one, two = unit(wq, wk), unit(wv, wo)
    up_unit = unit(jnp.concatenate(up_blocks[:2]), jnp.concatenate(up_blocks[2:]))
    down_unit = unit(w2[: ff_max // 2], w2[ff_max // 2 :])
    place = jnp.stack([core, jnp.zeros_like(core), jnp.zeros_like(core)])
    layer = Layer(place, span_starts[:, None, :], frames, vec, b1, d_max, ff_max, d_max, ff_max, False)
    q, k, v, o, lse, n1, rstd = layer.attn_forward(one, two)
    hidden, slope = layer.ffn_up(up_unit, n1)
    output, dz, dr2, small2, down_grad = layer.ffn_down(down_unit, n1, hidden, cotangent, False)
    dr1, do, small1, wide_small, *up_out = layer.ffn_backward(
        two, up_unit, down_unit, n1, rstd, dz, dr2, slope, o
    )
    dq, dk, dv, small_a, *qkv = layer.attn_backward(0, HEADS // 2, q, k, v, do, lse)
    frames_grad, small_m = layer.input_backward(one, two, dr1, (dq, dk, dv))
    small = grid.total(small_rows(small_a, small1, small_m, small2, wide_small))

    def reduced(grads):
        total = grid.reduce(jnp.concatenate([grad.reshape(owners, -1, D) for grad in grads], axis=1))
        return [part for part in total.reshape(len(grads), -1, D)]

    def wide_rows(grad):
        return jnp.pad(grad, ((0, 0), (0, d_max - D)))

    sums = [wide_rows(grad) for grad in reduced(qkv)]
    up_out = reduced(up_out)
    sums.append(wide_rows(up_out[-1]))
    zeros = jnp.zeros((count, up.shape[1] - FF), F32)
    sums.append(jnp.concatenate(up_out[:-1] + [zeros], axis=1))
    sums.append(wide_rows(reduced([down_grad])[0]))
    return output, frames_grad, sums, vector_grads(small, count, wide, d_max, ff_max)


def four_by_eight(grid, frames, cotangent, span_starts, matrices, vectors, up_bias):
    query, key, value, out, up, down = matrices
    count, wide = query.shape[0], down.shape[0]
    owners = grid.fsdp
    d_max, ff_max = count * owners, wide * owners
    me, dp_at = lax.axis_index("fsdp"), lax.axis_index("dp")
    core = dp_at % 2
    first = core == 0
    place = jnp.stack([core, me, dp_at // 2])

    packed = jnp.pad(jnp.stack(vectors), ((0, 0), (0, D - count)))
    packed = jnp.concatenate([packed, jnp.pad(up_bias, (0, D - wide))[None]])
    packed = jnp.pad(packed, ((0, 16 - packed.shape[0]), (0, 0)))
    half = wide // 2
    blocks = in_columns(up)
    pieces = (
        jnp.where(first, query[:, :D], key[:, :D]),
        jnp.concatenate([jnp.where(first, value[:, :D], out[:, :D]), packed]),
        jnp.where(first, jnp.concatenate(blocks[:2]), jnp.concatenate(blocks[2:])),
        jnp.where(first, down[:half, :D], down[half:, :D]),
    )
    far, near = [], []
    for piece in pieces[:3]:
        far.append(jnp.stack(grid.from_far(tie(piece, far[-1]) if far else piece)))
    for stack in far:
        near.append(grid.swap(tie(stack, near[-1]) if near else stack, 0, 1))
    last = grid.from_far(tie(pieces[3], far[-1]))

    def other_core(stacks, *before):
        return stacks, [grid.swap(tie(stack, *before) if before else stack, 1, 0) for stack in stacks]

    stacks = list(zip(far, near))
    one, two = other_core(stacks[0]), other_core(stacks[1])
    vec, b1 = unpack(place, stacks[1], count, count, wide, len(vectors))

    layer = Layer(place, span_starts[:, None, :], frames, vec, b1, count, wide, d_max, ff_max, True)
    q, k, v, o, lse, n1, rstd = layer.attn_forward(one, two, after=(far[2],))
    last = jnp.stack([last[0]] + [tie(piece, n1) for piece in last[1:]])
    up_unit = other_core(stacks[2], n1, last)
    hidden, slope = layer.ffn_up(up_unit, n1)
    down_unit = other_core((last, grid.swap(tie(last, near[2]), 0, 1)), hidden)
    output, dz, dr2, small2, down_grad = layer.ffn_down(down_unit, n1, hidden, cotangent, False)
    down_sum = lax.psum_scatter(down_grad.reshape(owners, wide, D), "fsdp", scatter_dimension=0)
    dr1, do, small1, wide_small, *up_out = layer.ffn_backward(
        two, up_unit, down_unit, n1, rstd, dz, dr2, slope, o
    )

    def spread(kept_half, sent_half, *before):
        parts = first_sums(place, kept_half, grid.swap(tie(sent_half, *before), 1, 0))
        return parts[0], [grid.swap(parts[j], 2 * (j % 2), j // 2) for j in range(1, 4)]

    def spread_far(own, received):
        parts = next_sums(place, [own] + received, True)
        return parts[0], [grid.swap(parts[j], 0, 2 * j) for j in range(1, 4)]

    def closing(own, received):
        total = next_sums(place, [own] + received, False)[0]
        along = grid.swap(total, 2, 0)
        return total, along, grid.swap(total, 1, 0), grid.swap(along, 1, 0)

    own_u, got_u = spread(*up_out)
    split = FIRST_PAIRS
    dqa, dka, dva, small_a, *qkv_a = layer.attn_backward(0, split, q, k, v, do, lse, after=(own_u,))
    far_u, got_far_u = spread_far(own_u, got_u)
    own_a, got_a = spread(*qkv_a, far_u)
    for bit in grid.dp_bits:
        low = down_sum.astype(BF16)
        down_sum = low.astype(F32) + grid.swap(low, bit, 0).astype(F32)
    dqb, dkb, dvb, small_b, *qkv_b = layer.attn_backward(
        split, HEADS // 2 - split, q, k, v, do, lse, after=(far_u, own_a)
    )
    own_b, got_b = spread(*qkv_b, *got_a, *got_far_u[:2])
    far_a, got_far_a = spread_far(tie(own_a, own_b), got_a)
    frames_grad, small_m = layer.input_backward(
        one, two, dr1, (dqa, dka, dva, dqb, dkb, dvb), after=(far_a,)
    )
    far_b, got_far_b = spread_far(own_b, got_b)
    small = grid.total(tie(small_total(place, small_a, small_b, small1, small_m, small2, wide_small), far_b))
    all_u = closing(tie(far_u, far_b), got_far_u)
    all_a = closing(tie(far_a, far_b), got_far_a)
    all_b = closing(far_b, got_far_b)
    up_sum, out_sum = finish(
        place, [all_u],
        [(count, up.shape[1], [(0, j, j * D) for j in range(FF // D)]), (count, d_max, [(0, FF // D, 0)])],
    )
    qkv_sums = finish(
        place, [all_a, all_b],
        [(count, d_max, [(0, j, 0), (1, j, split * PAIR)]) for j in range(3)],
    )
    sums = list(qkv_sums) + [out_sum, up_sum, jnp.pad(down_sum, ((0, 0), (0, d_max - D)))]
    return output, frames_grad, sums, vector_grads(small, count, wide, d_max, ff_max)


def on_device(
    sizes, frames, cotangent, span_starts, query_weight, key_weight, value_weight, out_weight,
    query_bias, value_bias, out_bias, first_gain, first_shift, up_weight, up_bias, down_weight,
    down_bias, second_gain, second_shift, mask_vector,
):
    grid = Grid(*sizes)
    matrices = (query_weight, key_weight, value_weight, out_weight, up_weight, down_weight)
    vectors = [query_bias, value_bias, out_bias, first_gain, first_shift, mask_vector,
               second_gain, second_shift, down_bias]
    placed = sizes == (4, 8) and query_weight.shape[0] % 32 == 0
    program = four_by_eight if placed else any_grid
    output, frames_grad, sums, small = program(
        grid, frames, cotangent, span_starts, matrices, vectors, up_bias
    )
    return (
        output, frames_grad, *sums[:4], small["qb"], small["vb"], small["ob"], small["g1"], small["s1"],
        sums[4], small["b1"], sums[5], small["b2"], small["g2"], small["s2"], small["m"],
    )


def solution(mesh):
    sizes = (mesh.shape["dp"], mesh.shape["fsdp"])
    tokens = P(("dp", "fsdp"), None)
    matrix, vector = P("fsdp", None), P("fsdp")
    return jax.shard_map(
        functools.partial(on_device, sizes),
        mesh=mesh,
        in_specs=(tokens,) * 3 + (matrix,) * 4 + (vector,) * 5 + (matrix, vector, matrix) + (vector,) * 4,
        out_specs=(tokens,) * 2 + (matrix,) * 4 + (vector,) * 5 + (matrix, vector, matrix) + (vector,) * 4,
        check_vma=False,
    )
```

time: 455 us -> 376 us (0.83)
  waiting for transfers between devices: 170 us -> 61.4 us
  Pallas kernels: 160 us -> 209 us
  starting transfers between devices: 49.4 us -> 68 us
  between operations: 30.6 us -> 15.1 us
  other arithmetic: 16 us -> 3.46 us
  local copies, waits for them, and re-layouts: 22.5 us -> 15.7 us
    all_gather x1 -> x0, waiting for transfers between devices: 58.6 us -> none  [on_device(): ffn_mine = lax.all_gather(ffn_half, 'fsdp', axis=0, tiled=False)]
    pallas_call x5 -> x20, Pallas kernels: 160 us -> 209 us  [the longest x7 172 us: call(): pl.pallas_call(kernel, grid=(steps,), in_specs=[SCALARS] + [WHOLE] * (len...]
    ppermute x21 -> x31, waiting for transfers between devices: 85.1 us -> 36.2 us  [swap(): lax.ppermute(value, 'fsdp', [(i, i ^ fsdp_mask) for i in range(self.fsdp)])]
    ppermute x21 -> x31, starting transfers between devices: 33.8 us -> 50.2 us  [swap(): lax.ppermute(value, 'fsdp', [(i, i ^ fsdp_mask) for i in range(self.fsdp)])]
    unnamed x51 -> x98, local copies, waits for them, and re-layouts: 1.21 us -> 11.1 us
    dynamic_slice x11 -> x1, local copies, waits for them, and re-layouts: 10.4 us -> 0.66 us  [vector_grads(): grads['b1'] = lax.dynamic_slice(b1, (me * wide,), (wide,))]
    convert_element_type x11 -> x1, other arithmetic: 8.74 us -> 0.12 us  [four_by_eight(): low = down_sum.astype(BF16)]
    slice x12 -> x2, local copies, waits for them, and re-layouts: 6.07 us -> 0.05 us  [the longest x1 0.04 us: in_columns(): return [weight[:, j * D:(j + 1) * D] for j in range(FF // D)]]
  transfers between devices with their start and end apart: 41 -> 62, of which waited for: 20 -> 18; matrix products, arithmetic and copies ran while one was open for 7% -> 2% of each run, Pallas kernels for 8% -> 49%
where the time goes in v2:
time: 376 us; the launch traced here: 373 us
  Pallas kernels  209 us (56%)
  starting transfers between devices  68 us (18%)
  waiting for transfers between devices  61.4 us (16%)
  local copies, waits for them, and re-layouts  15.7 us (4%)
  between operations  15.1 us (4%)
    pallas_call x7, Pallas kernels, call(): pl.pallas_call(kernel, grid=(steps,), in_specs=[SCALARS] + [WHOLE] * (len...  172 us
    ppermute x31, starting transfers between devices, swap(): lax.ppermute(value, 'fsdp', [(i, i ^ fsdp_mask) for i in range(self.fsdp)])  50.2 us
    pallas_call x13, Pallas kernels, local(): pl.pallas_call(body, in_specs=[SCALARS] + [WHOLE] * count, out_specs=[vme...  37.1 us
    ppermute x31, waiting for transfers between devices, swap(): lax.ppermute(value, 'fsdp', [(i, i ^ fsdp_mask) for i in range(self.fsdp)])  36.2 us
    ppermute x27, waiting for transfers between devices, swap(): return lax.ppermute(value, 'dp', [(i, i ^ dp_mask) for i in range(self.dp)])  25.1 us
    unnamed x98, local copies, waits for them, and re-layouts  11.1 us
    ppermute x27, starting transfers between devices, swap(): return lax.ppermute(value, 'dp', [(i, i ^ dp_mask) for i in range(self.dp)])  10.8 us
  transfers between devices with their start and end apart: 62, of which 18 were waited for; matrix products, arithmetic and copies ran while one was open for 2% of the time, Pallas kernels for 49%

profile of v2, /device:TPU:0, one launch (start us, length us, event | category | flops | bytes accessed | tf_op | source)
XLA Modules:
  0.0 372.7 jit_solution(16086204009759000928)
XLA Ops:
  8.2 3.1 collective-permute-start
  11.3 2.6 collective-permute-start.1
  14.6 1.5 stack.115
  17.1 6.5 %collective-permute-done.1 = bf16[96,640]{1,0:T(8,128)(2,1)S(1)} collective-permute-done((bf16[96,640]{1,0:T(8,128)(2,1)S(1)}, bf16[96,640]{1,0:T(8,128)(2,1)S(1)}, u32[]{:S(2)}, u32[]{:S(2)}) %collective-permute-start.1) | collective-permute-done | bytes 122912 | tf_op jit(solution)/shard_map/ppermute | solution.py:614
  23.7 1.6 collective-permute-start.10
  25.4 1.9 collective-permute-start.3
  27.3 1.1 collective-permute-start.4
  28.4 1.4 collective-permute-start.5
  29.8 1.9 collective-permute-done.3
  31.7 7.9 %collective-permute-done.4 = bf16[112,640]{1,0:T(8,128)(2,1)S(1)} collective-permute-done((bf16[112,640]{1,0:T(8,128)(2,1)S(1)}, bf16[112,640]{1,0:T(8,128)(2,1)S(1)}, u32[]{:S(2)}, u32[]{:S(2)}) %collective-permute-start.4) | collective-permute-done | bytes 143392 | tf_op jit(solution)/shard_map/ppermute | solution.py:614
  40.4 2.2 collective-permute-start.6
  42.6 1.1 collective-permute-start.7
  43.7 6.9 %collective-permute-done.13.refs_1_.refs_6_ = bf16[4,112,640]{2,1,0:T(8,128)(2,1)S(1)} collective-permute-done((bf16[4,112,640]{2,1,0:T(8,128)(2,1)S(1)}, bf16[4,112,640]{2,1,0:T(8,128)(2,1)S(1)}, u32[]{:S(2)}, u32[]{:S(2)}) %collective-permute-start.13) | collective-permute-done | bytes 573472 | tf_op jit(solution)/shard_map/ppermute | solution.py:614
  52.1 5.7 %collective-permute-start.8 = (bf16[192,640]{1,0:T(8,128)(2,1)S(1)}, bf16[192,640]{1,0:T(8,128)(2,1)S(1)}, u32[]{:S(2)}, u32[]{:S(2)}) collective-permute-start(bf16[192,640]{1,0:T(8,128)(2,1)S(1)} %maximum_select_fusion), channel_id=1, source_target_pairs={{0,6},{1,7},{2,4},{3,5},{4,2},{5,3},{6,0},{7,1},{8,14},{9,15},{10,... | collective-permute-start | bytes 737288 | tf_op jit(solution)/shard_map/ppermute | solution.py:614
  58.5 4.4 %collective-permute-done.8 = bf16[192,640]{1,0:T(8,128)(2,1)S(1)} collective-permute-done((bf16[192,640]{1,0:T(8,128)(2,1)S(1)}, bf16[192,640]{1,0:T(8,128)(2,1)S(1)}, u32[]{:S(2)}, u32[]{:S(2)}) %collective-permute-start.8) | collective-permute-done | bytes 245792 | tf_op jit(solution)/shard_map/ppermute | solution.py:614
  63.1 6.0 %collective-permute-start.9 = (bf16[192,640]{1,0:T(8,128)(2,1)S(1)}, bf16[192,640]{1,0:T(8,128)(2,1)S(1)}, u32[]{:S(2)}, u32[]{:S(2)}) collective-permute-start(bf16[192,640]{1,0:T(8,128)(2,1)S(1)} %slice_select_fusion), channel_id=1, source_target_pairs={{0,2},{1,3},{2,0},{3,1},{4,6},{5,7},{6,4},{7,5},{8,10},{9,11},{10,... | collective-permute-start | bytes 737288 | tf_op jit(solution)/shard_map/ppermute | solution.py:614
  69.1 2.6 shard_map.322
  71.8 2.0 collective-permute-start.16
  73.7 1.5 collective-permute-start.17
  75.3 1.1 collective-permute-start.18
  76.3 26.0 %shard_map.323 = (bf16[1600,640]{1,0:T(8,128)(2,1)}, bf16[1600,640]{1,0:T(8,128)(2,1)}, bf16[1600,640]{1,0:T(8,128)(2,1)}, bf16[1600,640]{1,0:T(8,128)(2,1)}, f3...) custom-call(s32[3]{0:T(128)} %pad_add_fusion.place_ref, bf16[4,192,640]{2,1,0:T(8,128)(2,1)} %copy-done.2, ...), custom_call_target="tpu_custom_call" | custom-call | flops 11796480000 | bytes 14336000 | tf_op jit(solution)/shard_map/pallas_call | solution.py:363
  104.1 1.3 collective-permute-done.20.refs_2_.refs_6_
  105.4 1.4 collective-permute-done.21.refs_3_.refs_7_
  107.8 23.1 %shard_map.324 = (bf16[1600,2560]{1,0:T(8,128)(2,1)}, bf16[1600,2560]{1,0:T(8,128)(2,1)}) custom-call(s32[3]{0:T(128)} %pad_add_fusion.place_ref, bf16[4,192,640]{2,1,0:T(8,128)(2,1)} %copy-done.2, bf16[4,192,640]{2,1,0:T(8,128)(2,1)} %collective-permute-done.18.refs_1_.refs_5_, bf16[4,192,640]{2,1,0:T(8,128)(2,1)} %copy-done.39, ...), custom_call_target="tpu_custom_call" | custom-call | flops 10485760000 | bytes 24576000 | tf_op jit(solution)/shard_map/pallas_call | solution.py:363
  131.5 2.3 collective-permute-done.23.refs_3_.refs_11_
  133.8 1.2 collective-permute-done.22.refs_2_.refs_10_
  135.9 26.0 %shard_map.325 = (bf16[1600,640]{1,0:T(8,128)(2,1)}, bf16[1600,640]{1,0:T(8,128)(2,1)}, f32[1600,640]{1,0:T(8,128)}, f32[8,640]{1,0:T(8,128)}, bf16[3072,640]{1,0:T(8,128)(2,1)}) custom-call(s32[3]{0:T(128)} %pad_add_fusion.place_ref, bf16[4,192,640]{2,1,0:T(8,128)(2,1)} %copy-done.3, bf16[4,192,640]{2,1,0:T(8,128)(2,1)} %collective-permute-done.19.refs_1_.refs_9_, ...), custom_call_target="tpu_custom_call" | custom-call | flops 15728640000 | bytes 32768000 | tf_op jit(solution)/shard_map/pallas_call | solution.py:363
  161.9 42.5 %shard_map.326 = (f32[1600,640]{1,0:T(8,128)}, bf16[1600,640]{1,0:T(8,128)(2,1)}, f32[8,640]{1,0:T(8,128)}, f32[8,2560]{1,0:T(8,128)}, bf16[8,2,120,640]{3,2,1,0...) custom-call(s32[3]{0:T(128)} %pad_add_fusion.place_ref, bf16[4,112,640]{2,1,0:T(8,128)(2,1)} %copy-done.1, ...), custom_call_target="tpu_custom_call" | custom-call | flops 23592960000 | bytes 32768000 | tf_op jit(solution)/shard_map/pallas_call | solution.py:363
  205.2 4.5 %collective-permute-done.24.refs_1_ = bf16[8,2,120,640]{3,2,1,0:T(8,128)(2,1)S(1)} collective-permute-done((bf16[8,2,120,640]{3,2,1,0:T(8,128)(2,1)}, bf16[8,2,120,640]{3,2,1,0:T(8,128)(2,1)S(1)}, u32[]{:S(2)}, u32[]{:S(2)}) %collective-permute-start.24) | collective-permute-done | bytes 2457632 | tf_op jit(solution)/shard_map/ppermute | solution.py:616
  209.7 1.4 copy-done
  211.1 4.8 %shard_map.327 = (bf16[4,120,640]{2,1,0:T(8,128)(2,1)}, bf16[4,120,640]{2,1,0:T(8,128)(2,1)}, bf16[4,120,640]{2,1,0:T(8,128)(2,1)}, bf16[4,120,640]{2,1,0:T(8,128)(2,1)}) custom-call(s32[3]{0:T(128)} %pad_add_fusion.place_ref, bf16[8,2,120,640]{3,2,1,0:T(8,128)(2,1)} %get-tuple-element.125.refs_0_, bf16[8,2,120,640]{3,2,1,0:T(8,128)(2,1)} %copy-done), custom_call_target="tpu_custom_call" | custom-call | flops 1000 | bytes 9830400 | tf_op jit(solution)/shard_map/pallas_call | solution.py:499
  216.0 1.5 collective-permute-start.25
  218.2 1.4 collective-permute-start.27
  219.5 24.8 %shard_map.328 = (bf16[1600,384]{1,0:T(8,128)(2,1)}, bf16[1600,384]{1,0:T(8,128)(2,1)}, bf16[1600,384]{1,0:T(8,128)(2,1)}, f32[8,384]{1,0:T(8,128)}, bf16[8,2,72...) custom-call(s32[3]{0:T(128)} %pad_add_fusion.place_ref, bf16[4,120,640]{2,1,0:T(8,128)(2,1)} %get-tuple-element.127.refs_0_, ...), custom_call_target="tpu_custom_call" | custom-call | flops 12189696000 | bytes 10240000 | tf_op jit(solution)/shard_map/pallas_call | solution.py:363
  244.3 7.6 %collective-permute-done.26.refs_2_ = bf16[4,120,640]{2,1,0:T(8,128)(2,1)S(1)} collective-permute-done((bf16[4,120,640]{2,1,0:T(8,128)(2,1)}, bf16[4,120,640]{2,1,0:T(8,128)(2,1)S(1)}, u32[]{:S(2)}, u32[]{:S(2)}) %collective-permute-start.26) | collective-permute-done | bytes 614432 | tf_op jit(solution)/shard_map/ppermute | solution.py:614
  253.6 3.3 shard_map.329
  257.1 1.5 collective-permute-start.33
  260.3 3.1 shard_map.330
  264.3 2.8 collective-permute-start.31
  267.0 18.0 %shard_map.331 = (bf16[1600,256]{1,0:T(8,128)(2,1)}, bf16[1600,256]{1,0:T(8,128)(2,1)}, bf16[1600,256]{1,0:T(8,128)(2,1)}, f32[8,256]{1,0:T(8,128)}, bf16[8,2,72...) custom-call(s32[3]{0:T(128)} %pad_add_fusion.place_ref, bf16[120,640]{1,0:T(8,128)(2,1)} %get-tuple-element.174.refs_0_, ...), custom_call_target="tpu_custom_call" | custom-call | flops 8126464000 | bytes 10240000 | tf_op jit(solution)/shard_map/pallas_call | solution.py:363
  285.2 2.1 collective-permute-start.50
  288.2 2.8 shard_map.332
  291.8 2.8 collective-permute-start.37
  294.6 2.7 shard_map.333
  297.5 11.5 %shard_map.334 = (bf16[1600,640]{1,0:T(8,128)(2,1)}, f32[8,640]{1,0:T(8,128)}) custom-call(s32[3]{0:T(128)} %pad_add_fusion.place_ref, bf16[72,384]{1,0:T(8,128)(2,1)} %get-tuple-element.164.refs_0_, bf16[4,96,640]{2,1,0:T(8,128)(2,1)} %copy-done.10, bf16[4,96,640]{2,1,0:T(8,128)(2,1)} %collective-permute-done.10.refs_2_, ...), custom_call_target="tpu_custom_call" | custom-call | flops 5242880000 | bytes 12288000 | tf_op jit(solution)/shard_map/pallas_call | solution.py:363
  309.1 2.5 shard_map.341
  312.9 2.5 shard_map.335
  317.1 1.2 collective-permute-start.55
  319.1 1.7 collective-permute-start.39
  320.9 9.3 %collective-permute-done.55 = f32[16,640]{1,0:T(8,128)S(1)} collective-permute-done((f32[16,640]{1,0:T(8,128)S(1)}, f32[16,640]{1,0:T(8,128)S(1)}, u32[]{:S(2)}, u32[]{:S(2)}) %collective-permute-start.55) | collective-permute-done | bytes 40992 | tf_op jit(solution)/shard_map/ppermute | solution.py:616
  330.2 2.0 collective-permute-start.40
  333.3 2.0 collective-permute-start.45
  335.3 2.6 shard_map.339.refs_0_
  338.3 2.1 collective-permute-start.46
  340.4 2.2 shard_map.336.refs_0_
  342.7 1.8 collective-permute-start.41
  345.2 2.2 shard_map.337.refs_4_
  347.3 1.5 collective-permute-start.47
  349.4 2.2 collective-permute-done.47.refs_5_
  351.6 1.8 collective-permute-start.58
  353.4 1.2 collective-permute-done.49.refs_7_
  355.8 2.6 shard_map.338
  361.3 3.1 shard_map.340
  364.5 1.1 pad.29
  (206 shorter events, 28.4 us)
Async XLA Ops:
  7.2 290.2 %reduce-scatter.2.cloned.1.call-start = ((), (), s32[]{:S(2)}) async-start(), calls=%async_computation.1 | async-start | bytes 4423680 | tf_op jit(solution)/shard_map/reduce_scatter | solution.py:822
  8.2 8.9 %collective-permute-start = (bf16[96,640]{1,0:T(8,128)(2,1)S(1)}, bf16[96,640]{1,0:T(8,128)(2,1)S(1)}, u32[]{:S(2)}, u32[]{:S(2)}) collective-permute-start(bf16[96,640]{1,0:T(8,128)(2,1)S(1)} %slice_select_fusion.1), channel_id=1, source_target_pairs={{0,2},{1,3},{2,0},{3,1},{4,6},{5,7},{6,4},{7,5},{8,10},{9,11},{10,... | collective-permute-start | bytes 368648 | tf_op jit(solution)/shard_map/ppermute | solution.py:614
  11.3 12.3 %collective-permute-start.1 = (bf16[96,640]{1,0:T(8,128)(2,1)S(1)}, bf16[96,640]{1,0:T(8,128)(2,1)S(1)}, u32[]{:S(2)}, u32[]{:S(2)}) collective-permute-start(bf16[96,640]{1,0:T(8,128)(2,1)S(1)} %slice_select_fusion.1), channel_id=1, source_target_pairs={{0,4},{1,5},{2,6},{3,7},{4,0},{5,1},{6,2},{7,3},{8,12},{9,13},{10,... | collective-permute-start | bytes 368648 | tf_op jit(solution)/shard_map/ppermute | solution.py:614
  13.9 9.7 %collective-permute-start.2 = (bf16[96,640]{1,0:T(8,128)(2,1)S(1)}, bf16[96,640]{1,0:T(8,128)(2,1)S(1)}, u32[]{:S(2)}, u32[]{:S(2)}) collective-permute-start(bf16[96,640]{1,0:T(8,128)(2,1)S(1)} %slice_select_fusion.1), channel_id=1, source_target_pairs={{0,6},{1,7},{2,4},{3,5},{4,2},{5,3},{6,0},{7,1},{8,14},{9,15},{10,... | collective-permute-start | bytes 368648 | tf_op jit(solution)/shard_map/ppermute | solution.py:614
  23.6 34.8 %copy-start.12 = (bf16[384,768]{1,0:T(8,128)(2,1)S(1)}, bf16[384,768]{1,0:T(8,128)(2,1)}, u32[]{:S(2)}) copy-start(bf16[384,768]{1,0:T(8,128)(2,1)} %param.33) | copy-start | bytes 1769476
  23.7 39.4 %copy-start.10 = (bf16[4,96,640]{2,1,0:T(8,128)(2,1)}, bf16[4,96,640]{2,1,0:T(8,128)(2,1)S(1)}, u32[]{:S(2)}) copy-start(bf16[4,96,640]{2,1,0:T(8,128)(2,1)S(1)} %pad_maximum_fusion.3.refs_1_) | copy-start | bytes 1474564
  23.7 16.0 %collective-permute-start.10 = (bf16[4,96,640]{2,1,0:T(8,128)(2,1)S(1)}, bf16[4,96,640]{2,1,0:T(8,128)(2,1)}, u32[]{:S(2)}, u32[]{:S(2)}) collective-permute-start(bf16[4,96,640]{2,1,0:T(8,128)(2,1)S(1)} %pad_maximum_fusion.3.refs_1_), channel_id=1, source_target_pairs={{0,1},{1,0},{2,3},{3,2},{4,5},{5,4},{6,7},{7,6},{8,9},{9,8},{10,11... | collective-permute-start | bytes 1474568 | tf_op jit(solution)/shard_map/ppermute | solution.py:614
  25.4 6.4 %collective-permute-start.3 = (bf16[112,640]{1,0:T(8,128)(2,1)S(1)}, bf16[112,640]{1,0:T(8,128)(2,1)S(1)}, u32[]{:S(2)}, u32[]{:S(2)}) collective-permute-start(bf16[112,640]{1,0:T(8,128)(2,1)S(1)} %fusion.1), channel_id=1, source_target_pairs={{0,2},{1,3},{2,0},{3,1},{4,6},{5,7},{6,4},{7,5},{8,10},{9,11},{10,... | collective-permute-start | bytes 430088 | tf_op jit(solution)/shard_map/ppermute | solution.py:614
  27.3 12.3 %collective-permute-start.4 = (bf16[112,640]{1,0:T(8,128)(2,1)S(1)}, bf16[112,640]{1,0:T(8,128)(2,1)S(1)}, u32[]{:S(2)}, u32[]{:S(2)}) collective-permute-start(bf16[112,640]{1,0:T(8,128)(2,1)S(1)} %fusion.1), channel_id=1, source_target_pairs={{0,4},{1,5},{2,6},{3,7},{4,0},{5,1},{6,2},{7,3},{8,12},{9,13},{10,... | collective-permute-start | bytes 430088 | tf_op jit(solution)/shard_map/ppermute | solution.py:614
  28.4 11.2 %collective-permute-start.5 = (bf16[112,640]{1,0:T(8,128)(2,1)S(1)}, bf16[112,640]{1,0:T(8,128)(2,1)S(1)}, u32[]{:S(2)}, u32[]{:S(2)}) collective-permute-start(bf16[112,640]{1,0:T(8,128)(2,1)S(1)} %fusion.1), channel_id=1, source_target_pairs={{0,6},{1,7},{2,4},{3,5},{4,2},{5,3},{6,0},{7,1},{8,14},{9,15},{10,... | collective-permute-start | bytes 430088 | tf_op jit(solution)/shard_map/ppermute | solution.py:614
  39.7 10.9 %collective-permute-start.13 = (bf16[4,112,640]{2,1,0:T(8,128)(2,1)S(1)}, bf16[4,112,640]{2,1,0:T(8,128)(2,1)S(1)}, u32[]{:S(2)}, u32[]{:S(2)}) collective-permute-start(bf16[4,112,640]{2,1,0:T(8,128)(2,1)S(1)} %pad_maximum_fusion.2.refs_0_.refs_5_), channel_id=1, source_target_pairs={{0,1},{1,0},{2,3},{3,2},{4,5},{5,4},{6,7},{7,6},{8,9},{9,8},{10,11... | collective-permute-start | bytes 1720328 | tf_op jit(solution)/shard_map/ppermute | solution.py:614
  40.4 11.7 %collective-permute-start.6 = (bf16[192,640]{1,0:T(8,128)(2,1)S(1)}, bf16[192,640]{1,0:T(8,128)(2,1)S(1)}, u32[]{:S(2)}, u32[]{:S(2)}) collective-permute-start(bf16[192,640]{1,0:T(8,128)(2,1)S(1)} %maximum_select_fusion), channel_id=1, source_target_pairs={{0,2},{1,3},{2,0},{3,1},{4,6},{5,7},{6,4},{7,5},{8,10},{9,11},{10,... | collective-permute-start | bytes 737288 | tf_op jit(solution)/shard_map/ppermute | solution.py:614
  42.6 9.5 %collective-permute-start.7 = (bf16[192,640]{1,0:T(8,128)(2,1)S(1)}, bf16[192,640]{1,0:T(8,128)(2,1)S(1)}, u32[]{:S(2)}, u32[]{:S(2)}) collective-permute-start(bf16[192,640]{1,0:T(8,128)(2,1)S(1)} %maximum_select_fusion), channel_id=1, source_target_pairs={{0,4},{1,5},{2,6},{3,7},{4,0},{5,1},{6,2},{7,3},{8,12},{9,13},{10,... | collective-permute-start | bytes 737288 | tf_op jit(solution)/shard_map/ppermute | solution.py:614
  43.7 30.0 %collective-permute-start.14 = (bf16[4,112,640]{2,1,0:T(8,128)(2,1)S(1)}, bf16[4,112,640]{2,1,0:T(8,128)(2,1)}, u32[]{:S(2)}, u32[]{:S(2)}) collective-permute-start(bf16[4,112,640]{2,1,0:T(8,128)(2,1)S(1)} %pad_maximum_fusion.2.refs_0_.refs_5_), channel_id=1, source_target_pairs={{0,8},{8,0},{16,24},{24,16},{1,9},{9,1},{17,25},{25,17},{2,10},{10... | collective-permute-start | bytes 1720328 | tf_op jit(solution)/shard_map/ppermute | solution.py:616
  50.6 25.7 %collective-permute-start.15 = (bf16[4,112,640]{2,1,0:T(8,128)(2,1)S(1)}, bf16[4,112,640]{2,1,0:T(8,128)(2,1)}, u32[]{:S(2)}, u32[]{:S(2)}) collective-permute-start(bf16[4,112,640]{2,1,0:T(8,128)(2,1)S(1)} %collective-permute-done.13.refs_1_.refs_6_), channel_id=1, source_target_pairs={{0,8},{8,0},{16,24},{24,16},{1,9},{9,1},{17,25},{25,17},{2,10},{10... | collective-permute-start | bytes 1720328 | tf_op jit(solution)/shard_map/ppermute | solution.py:616
  50.6 21.1 %collective-permute-start.11 = (bf16[4,96,640]{2,1,0:T(8,128)(2,1)S(1)}, bf16[4,96,640]{2,1,0:T(8,128)(2,1)}, u32[]{:S(2)}, u32[]{:S(2)}) collective-permute-start(bf16[4,96,640]{2,1,0:T(8,128)(2,1)S(1)} %pad_maximum_fusion.3.refs_1_), channel_id=1, source_target_pairs={{0,8},{8,0},{16,24},{24,16},{1,9},{9,1},{17,25},{25,17},{2,10},{10... | collective-permute-start | bytes 1474568 | tf_op jit(solution)/shard_map/ppermute | solution.py:616
  52.1 23.1 %collective-permute-start.12 = (bf16[4,96,640]{2,1,0:T(8,128)(2,1)}, bf16[4,96,640]{2,1,0:T(8,128)(2,1)}, u32[]{:S(2)}, u32[]{:S(2)}) collective-permute-start(bf16[4,96,640]{2,1,0:T(8,128)(2,1)} %collective-permute-done.10.refs_2_), channel_id=1, source_target_pairs={{0,8},{8,0},{16,24},{24,16},{1,9},{9,1},{17,25},{25,17},{2,10},{10... | collective-permute-start | bytes 1474568 | tf_op jit(solution)/shard_map/ppermute | solution.py:616
  52.1 10.8 %collective-permute-start.8 = (bf16[192,640]{1,0:T(8,128)(2,1)S(1)}, bf16[192,640]{1,0:T(8,128)(2,1)S(1)}, u32[]{:S(2)}, u32[]{:S(2)}) collective-permute-start(bf16[192,640]{1,0:T(8,128)(2,1)S(1)} %maximum_select_fusion), channel_id=1, source_target_pairs={{0,6},{1,7},{2,4},{3,5},{4,2},{5,3},{6,0},{7,1},{8,14},{9,15},{10,... | collective-permute-start | bytes 737288 | tf_op jit(solution)/shard_map/ppermute | solution.py:614
  63.1 39.3 %collective-permute-start.9 = (bf16[192,640]{1,0:T(8,128)(2,1)S(1)}, bf16[192,640]{1,0:T(8,128)(2,1)S(1)}, u32[]{:S(2)}, u32[]{:S(2)}) collective-permute-start(bf16[192,640]{1,0:T(8,128)(2,1)S(1)} %slice_select_fusion), channel_id=1, source_target_pairs={{0,2},{1,3},{2,0},{3,1},{4,6},{5,7},{6,4},{7,5},{8,10},{9,11},{10,... | collective-permute-start | bytes 737288 | tf_op jit(solution)/shard_map/ppermute | solution.py:614
  71.8 30.6 %collective-permute-start.16 = (bf16[192,640]{1,0:T(8,128)(2,1)S(1)}, bf16[192,640]{1,0:T(8,128)(2,1)S(1)}, u32[]{:S(2)}, u32[]{:S(2)}) collective-permute-start(bf16[192,640]{1,0:T(8,128)(2,1)S(1)} %slice_select_fusion), channel_id=1, source_target_pairs={{0,4},{1,5},{2,6},{3,7},{4,0},{5,1},{6,2},{7,3},{8,12},{9,13},{10,... | collective-permute-start | bytes 737288 | tf_op jit(solution)/shard_map/ppermute | solution.py:614
  73.7 28.7 %collective-permute-start.17 = (bf16[192,640]{1,0:T(8,128)(2,1)S(1)}, bf16[192,640]{1,0:T(8,128)(2,1)S(1)}, u32[]{:S(2)}, u32[]{:S(2)}) collective-permute-start(bf16[192,640]{1,0:T(8,128)(2,1)S(1)} %slice_select_fusion), channel_id=1, source_target_pairs={{0,6},{1,7},{2,4},{3,5},{4,2},{5,3},{6,0},{7,1},{8,14},{9,15},{10,... | collective-permute-start | bytes 737288 | tf_op jit(solution)/shard_map/ppermute | solution.py:614
  75.3 27.4 %collective-permute-start.18 = (bf16[4,192,640]{2,1,0:T(8,128)(2,1)S(1)}, bf16[4,192,640]{2,1,0:T(8,128)(2,1)}, u32[]{:S(2)}, u32[]{:S(2)}) collective-permute-start(bf16[4,192,640]{2,1,0:T(8,128)(2,1)S(1)} %pad_maximum_fusion.refs_0_.refs_4_), channel_id=1, source_target_pairs={{0,1},{1,0},{2,3},{3,2},{4,5},{5,4},{6,7},{7,6},{8,9},{9,8},{10,11... | collective-permute-start | bytes 2949128 | tf_op jit(solution)/shard_map/ppermute | solution.py:614
  102.6 2.8 collective-permute-start.20
  102.7 4.2 %collective-permute-start.21 = (bf16[4,192,640]{2,1,0:T(8,128)(2,1)}, bf16[4,192,640]{2,1,0:T(8,128)(2,1)S(1)}, u32[]{:S(2)}, u32[]{:S(2)}) collective-permute-start(bf16[4,192,640]{2,1,0:T(8,128)(2,1)} %collective-permute-done.18.refs_1_.refs_5_), channel_id=1, source_target_pairs={{0,8},{8,0},{16,24},{24,16},{1,9},{9,1},{17,25},{25,17},{2,10},{10... | collective-permute-start | bytes 2949128 | tf_op jit(solution)/shard_map/ppermute | solution.py:616
  103.2 27.8 %collective-permute-start.19 = (bf16[4,192,640]{2,1,0:T(8,128)(2,1)S(1)}, bf16[4,192,640]{2,1,0:T(8,128)(2,1)}, u32[]{:S(2)}, u32[]{:S(2)}) collective-permute-start(bf16[4,192,640]{2,1,0:T(8,128)(2,1)S(1)} %pad_maximum_fusion.1.refs_0_.refs_8_), channel_id=1, source_target_pairs={{0,1},{1,0},{2,3},{3,2},{4,5},{5,4},{6,7},{7,6},{8,9},{9,8},{10,11... | collective-permute-start | bytes 2949128 | tf_op jit(solution)/shard_map/ppermute | solution.py:614
  130.9 2.8 collective-permute-start.23
  131.1 3.8 %collective-permute-start.22 = (bf16[4,192,640]{2,1,0:T(8,128)(2,1)S(1)}, bf16[4,192,640]{2,1,0:T(8,128)(2,1)S(1)}, u32[]{:S(2)}, u32[]{:S(2)}) collective-permute-start(bf16[4,192,640]{2,1,0:T(8,128)(2,1)S(1)} %pad_maximum_fusion.1.refs_0_.refs_8_), channel_id=1, source_target_pairs={{0,8},{8,0},{16,24},{24,16},{1,9},{9,1},{17,25},{25,17},{2,10},{10... | collective-permute-start | bytes 2949128 | tf_op jit(solution)/shard_map/ppermute | solution.py:616
  204.5 5.3 %collective-permute-start.24 = (bf16[8,2,120,640]{3,2,1,0:T(8,128)(2,1)}, bf16[8,2,120,640]{3,2,1,0:T(8,128)(2,1)S(1)}, u32[]{:S(2)}, u32[]{:S(2)}) collective-permute-start(bf16[8,2,120,640]{3,2,1,0:T(8,128)(2,1)} %get-tuple-element.126), channel_id=1, source_target_pairs={{0,8},{8,0},{16,24},{24,16},{1,9},{9,1},{17,25},{25,17},{2,10},{10... | collective-permute-start | bytes 7372808 | tf_op jit(solution)/shard_map/ppermute | solution.py:616
  216.0 28.3 %collective-permute-start.25 = (bf16[4,120,640]{2,1,0:T(8,128)(2,1)}, bf16[4,120,640]{2,1,0:T(8,128)(2,1)S(1)}, u32[]{:S(2)}, u32[]{:S(2)}) collective-permute-start(bf16[4,120,640]{2,1,0:T(8,128)(2,1)} %get-tuple-element.135), channel_id=1, source_target_pairs={{0,16},{8,24},{16,0},{24,8},{1,17},{9,25},{17,1},{25,9},{2,18},{10... | collective-permute-start | bytes 1843208 | tf_op jit(solution)/shard_map/ppermute | solution.py:616
  217.5 34.4 %collective-permute-start.26 = (bf16[4,120,640]{2,1,0:T(8,128)(2,1)}, bf16[4,120,640]{2,1,0:T(8,128)(2,1)S(1)}, u32[]{:S(2)}, u32[]{:S(2)}) collective-permute-start(bf16[4,120,640]{2,1,0:T(8,128)(2,1)} %get-tuple-element.136), channel_id=1, source_target_pairs={{0,1},{1,0},{2,3},{3,2},{4,5},{5,4},{6,7},{7,6},{8,9},{9,8},{10,11... | collective-permute-start | bytes 1843208 | tf_op jit(solution)/shard_map/ppermute | solution.py:614
  218.2 33.8 %collective-permute-start.27 = (bf16[4,120,640]{2,1,0:T(8,128)(2,1)}, bf16[4,120,640]{2,1,0:T(8,128)(2,1)S(1)}, u32[]{:S(2)}, u32[]{:S(2)}) collective-permute-start(bf16[4,120,640]{2,1,0:T(8,128)(2,1)} %get-tuple-element.137), channel_id=1, source_target_pairs={{0,17},{1,16},{2,19},{3,18},{4,21},{5,20},{6,23},{7,22},{8,25},{9,... | collective-permute-start | bytes 1843208 | tf_op jit(solution)/shard_map/ppermute | solution.py:622
  256.9 2.5 collective-permute-start.28
  257.0 28.0 %collective-permute-start.32 = (bf16[120,640]{1,0:T(8,128)(2,1)}, bf16[120,640]{1,0:T(8,128)(2,1)S(1)}, u32[]{:S(2)}, u32[]{:S(2)}) collective-permute-start(bf16[120,640]{1,0:T(8,128)(2,1)} %get-tuple-element.146), channel_id=1, source_target_pairs={{0,2},{1,3},{2,0},{3,1},{4,6},{5,7},{6,4},{7,5},{8,10},{9,11},{10,... | collective-permute-start | bytes 460808 | tf_op jit(solution)/shard_map/ppermute | solution.py:614
  257.1 28.0 %collective-permute-start.33 = (bf16[120,640]{1,0:T(8,128)(2,1)}, bf16[120,640]{1,0:T(8,128)(2,1)S(1)}, u32[]{:S(2)}, u32[]{:S(2)}) collective-permute-start(bf16[120,640]{1,0:T(8,128)(2,1)} %get-tuple-element.147), channel_id=1, source_target_pairs={{0,4},{1,5},{2,6},{3,7},{4,0},{5,1},{6,2},{7,3},{8,12},{9,13},{10,... | collective-permute-start | bytes 460808 | tf_op jit(solution)/shard_map/ppermute | solution.py:614
  263.5 21.6 %collective-permute-start.29 = (bf16[4,72,384]{2,1,0:T(8,128)(2,1)}, bf16[4,72,384]{2,1,0:T(8,128)(2,1)S(1)}, u32[]{:S(2)}, u32[]{:S(2)}) collective-permute-start(bf16[4,72,384]{2,1,0:T(8,128)(2,1)} %get-tuple-element.143), channel_id=1, source_target_pairs={{0,16},{8,24},{16,0},{24,8},{1,17},{9,25},{17,1},{25,9},{2,18},{10... | collective-permute-start | bytes 663560 | tf_op jit(solution)/shard_map/ppermute | solution.py:616
  263.5 21.5 %collective-permute-start.30 = (bf16[4,72,384]{2,1,0:T(8,128)(2,1)}, bf16[4,72,384]{2,1,0:T(8,128)(2,1)S(1)}, u32[]{:S(2)}, u32[]{:S(2)}) collective-permute-start(bf16[4,72,384]{2,1,0:T(8,128)(2,1)} %get-tuple-element.144), channel_id=1, source_target_pairs={{0,1},{1,0},{2,3},{3,2},{4,5},{5,4},{6,7},{7,6},{8,9},{9,8},{10,11... | collective-permute-start | bytes 663560 | tf_op jit(solution)/shard_map/ppermute | solution.py:614
  264.3 20.8 %collective-permute-start.31 = (bf16[4,72,384]{2,1,0:T(8,128)(2,1)}, bf16[4,72,384]{2,1,0:T(8,128)(2,1)S(1)}, u32[]{:S(2)}, u32[]{:S(2)}) collective-permute-start(bf16[4,72,384]{2,1,0:T(8,128)(2,1)} %get-tuple-element.145), channel_id=1, source_target_pairs={{0,17},{1,16},{2,19},{3,18},{4,21},{5,20},{6,23},{7,22},{8,25},{9,... | collective-permute-start | bytes 663560 | tf_op jit(solution)/shard_map/ppermute | solution.py:622
  285.1 2.3 collective-permute-start.34
  285.2 47.0 %collective-permute-start.50 = (bf16[120,640]{1,0:T(8,128)(2,1)S(1)}, bf16[120,640]{1,0:T(8,128)(2,1)S(1)}, u32[]{:S(2)}, u32[]{:S(2)}) collective-permute-start(bf16[120,640]{1,0:T(8,128)(2,1)S(1)} %copy-done.44), channel_id=1, source_target_pairs={{0,6},{1,7},{2,4},{3,5},{4,2},{5,3},{6,0},{7,1},{8,14},{9,15},{10,... | collective-permute-start | bytes 460808 | tf_op jit(solution)/shard_map/ppermute | solution.py:614
  291.1 20.5 %collective-permute-start.35 = (bf16[4,72,256]{2,1,0:T(8,128)(2,1)}, bf16[4,72,256]{2,1,0:T(8,128)(2,1)S(1)}, u32[]{:S(2)}, u32[]{:S(2)}) collective-permute-start(bf16[4,72,256]{2,1,0:T(8,128)(2,1)} %get-tuple-element.160), channel_id=1, source_target_pairs={{0,16},{8,24},{16,0},{24,8},{1,17},{9,25},{17,1},{25,9},{2,18},{10... | collective-permute-start | bytes 442376 | tf_op jit(solution)/shard_map/ppermute | solution.py:616
  291.2 20.4 %collective-permute-start.36 = (bf16[4,72,256]{2,1,0:T(8,128)(2,1)}, bf16[4,72,256]{2,1,0:T(8,128)(2,1)S(1)}, u32[]{:S(2)}, u32[]{:S(2)}) collective-permute-start(bf16[4,72,256]{2,1,0:T(8,128)(2,1)} %get-tuple-element.161), channel_id=1, source_target_pairs={{0,1},{1,0},{2,3},{3,2},{4,5},{5,4},{6,7},{7,6},{8,9},{9,8},{10,11... | collective-permute-start | bytes 442376 | tf_op jit(solution)/shard_map/ppermute | solution.py:614
  291.8 19.7 %collective-permute-start.37 = (bf16[4,72,256]{2,1,0:T(8,128)(2,1)}, bf16[4,72,256]{2,1,0:T(8,128)(2,1)S(1)}, u32[]{:S(2)}, u32[]{:S(2)}) collective-permute-start(bf16[4,72,256]{2,1,0:T(8,128)(2,1)} %get-tuple-element.162), channel_id=1, source_target_pairs={{0,17},{1,16},{2,19},{3,18},{4,21},{5,20},{6,23},{7,22},{8,25},{9,... | collective-permute-start | bytes 442376 | tf_op jit(solution)/shard_map/ppermute | solution.py:622
  297.4 18.6 %collective-permute-start.59 = (bf16[384,640]{1,0:T(8,128)(2,1)}, bf16[384,640]{1,0:T(8,128)(2,1)S(1)}, u32[]{:S(2)}, u32[]{:S(2)}) collective-permute-start(bf16[384,640]{1,0:T(8,128)(2,1)} %bitcast.57), channel_id=1, source_target_pairs={{0,8},{8,0},{16,24},{24,16},{1,9},{9,1},{17,25},{25,17},{2,10},{10... | collective-permute-start | bytes 1474568 | tf_op jit(solution)/shard_map/ppermute | solution.py:616
  315.4 1.6 collective-permute-start.54
  316.1 48.3 %collective-permute-start.60 = (bf16[384,640]{1,0:T(8,128)(2,1)S(1)}, bf16[384,640]{1,0:T(8,128)(2,1)S(1)}, u32[]{:S(2)}, u32[]{:S(2)}) collective-permute-start(bf16[384,640]{1,0:T(8,128)(2,1)S(1)} %add_convert_fusion), channel_id=1, source_target_pairs={{0,16},{8,24},{16,0},{24,8},{1,17},{9,25},{17,1},{25,9},{2,18},{10... | collective-permute-start | bytes 1474568 | tf_op jit(solution)/shard_map/ppermute | solution.py:616
  317.1 13.1 %collective-permute-start.55 = (f32[16,640]{1,0:T(8,128)S(1)}, f32[16,640]{1,0:T(8,128)S(1)}, u32[]{:S(2)}, u32[]{:S(2)}) collective-permute-start(f32[16,640]{1,0:T(8,128)S(1)} %add.47), channel_id=1, source_target_pairs={{0,16},{8,24},{16,0},{24,8},{1,17},{9,25},{17,1},{25,9},{2,18},{10... | collective-permute-start | bytes 122888 | tf_op jit(solution)/shard_map/ppermute | solution.py:616
  318.3 14.7 %collective-permute-start.38 = (bf16[72,384]{1,0:T(8,128)(2,1)S(1)}, bf16[72,384]{1,0:T(8,128)(2,1)S(1)}, u32[]{:S(2)}, u32[]{:S(2)}) collective-permute-start(bf16[72,384]{1,0:T(8,128)(2,1)S(1)} %copy-done.47), channel_id=1, source_target_pairs={{0,2},{1,3},{2,0},{3,1},{4,6},{5,7},{6,4},{7,5},{8,10},{9,11},{10,... | collective-permute-start | bytes 165896 | tf_op jit(solution)/shard_map/ppermute | solution.py:614
  319.1 14.2 %collective-permute-start.39 = (bf16[72,384]{1,0:T(8,128)(2,1)S(1)}, bf16[72,384]{1,0:T(8,128)(2,1)S(1)}, u32[]{:S(2)}, u32[]{:S(2)}) collective-permute-start(bf16[72,384]{1,0:T(8,128)(2,1)S(1)} %copy-done.46), channel_id=1, source_target_pairs={{0,4},{1,5},{2,6},{3,7},{4,0},{5,1},{6,2},{7,3},{8,12},{9,13},{10,... | collective-permute-start | bytes 165896 | tf_op jit(solution)/shard_map/ppermute | solution.py:614
  330.2 7.7 %collective-permute-start.40 = (bf16[72,384]{1,0:T(8,128)(2,1)S(1)}, bf16[72,384]{1,0:T(8,128)(2,1)S(1)}, u32[]{:S(2)}, u32[]{:S(2)}) collective-permute-start(bf16[72,384]{1,0:T(8,128)(2,1)S(1)} %copy-done.45), channel_id=1, source_target_pairs={{0,6},{1,7},{2,4},{3,5},{4,2},{5,3},{6,0},{7,1},{8,14},{9,15},{10,... | collective-permute-start | bytes 165896 | tf_op jit(solution)/shard_map/ppermute | solution.py:614
  332.3 12.2 %collective-permute-start.56 = (f32[16,640]{1,0:T(8,128)S(1)}, f32[16,640]{1,0:T(8,128)S(1)}, u32[]{:S(2)}, u32[]{:S(2)}) collective-permute-start(f32[16,640]{1,0:T(8,128)S(1)} %add.48), channel_id=1, source_target_pairs={{0,1},{1,0},{2,3},{3,2},{4,5},{5,4},{6,7},{7,6},{8,9},{9,8},{10,11... | collective-permute-start | bytes 122888 | tf_op jit(solution)/shard_map/ppermute | solution.py:614
  333.0 5.3 %collective-permute-start.44 = (bf16[72,256]{1,0:T(8,128)(2,1)}, bf16[72,256]{1,0:T(8,128)(2,1)S(1)}, u32[]{:S(2)}, u32[]{:S(2)}) collective-permute-start(bf16[72,256]{1,0:T(8,128)(2,1)} %get-tuple-element.168), channel_id=1, source_target_pairs={{0,2},{1,3},{2,0},{3,1},{4,6},{5,7},{6,4},{7,5},{8,10},{9,11},{10,... | collective-permute-start | bytes 110600 | tf_op jit(solution)/shard_map/ppermute | solution.py:614
  333.3 9.3 %collective-permute-start.45 = (bf16[72,256]{1,0:T(8,128)(2,1)}, bf16[72,256]{1,0:T(8,128)(2,1)S(1)}, u32[]{:S(2)}, u32[]{:S(2)}) collective-permute-start(bf16[72,256]{1,0:T(8,128)(2,1)} %get-tuple-element.169), channel_id=1, source_target_pairs={{0,4},{1,5},{2,6},{3,7},{4,0},{5,1},{6,2},{7,3},{8,12},{9,13},{10,... | collective-permute-start | bytes 110600 | tf_op jit(solution)/shard_map/ppermute | solution.py:614
  337.9 20.5 %collective-permute-start.51 = (bf16[120,640]{1,0:T(8,128)(2,1)}, bf16[120,640]{1,0:T(8,128)(2,1)S(1)}, u32[]{:S(2)}, u32[]{:S(2)}) collective-permute-start(bf16[120,640]{1,0:T(8,128)(2,1)} %shard_map.339.refs_0_), channel_id=1, source_target_pairs={{0,16},{8,24},{16,0},{24,8},{1,17},{9,25},{17,1},{25,9},{2,18},{10... | collective-permute-start | bytes 460808 | tf_op jit(solution)/shard_map/ppermute | solution.py:616
  338.3 6.2 %collective-permute-start.46 = (bf16[72,256]{1,0:T(8,128)(2,1)S(1)}, bf16[72,256]{1,0:T(8,128)(2,1)S(1)}, u32[]{:S(2)}, u32[]{:S(2)}) collective-permute-start(bf16[72,256]{1,0:T(8,128)(2,1)S(1)} %copy-done.48), channel_id=1, source_target_pairs={{0,6},{1,7},{2,4},{3,5},{4,2},{5,3},{6,0},{7,1},{8,14},{9,15},{10,... | collective-permute-start | bytes 110600 | tf_op jit(solution)/shard_map/ppermute | solution.py:614
  342.7 4.6 %collective-permute-start.41 = (bf16[72,384]{1,0:T(8,128)(2,1)}, bf16[72,384]{1,0:T(8,128)(2,1)S(1)}, u32[]{:S(2)}, u32[]{:S(2)}) collective-permute-start(bf16[72,384]{1,0:T(8,128)(2,1)} %shard_map.336.refs_0_), channel_id=1, source_target_pairs={{0,16},{8,24},{16,0},{24,8},{1,17},{9,25},{17,1},{25,9},{2,18},{10... | collective-permute-start | bytes 165896 | tf_op jit(solution)/shard_map/ppermute | solution.py:616
  344.5 4.4 %collective-permute-start.42 = (bf16[72,384]{1,0:T(8,128)(2,1)}, bf16[72,384]{1,0:T(8,128)(2,1)S(1)}, u32[]{:S(2)}, u32[]{:S(2)}) collective-permute-start(bf16[72,384]{1,0:T(8,128)(2,1)} %shard_map.336.refs_0_), channel_id=1, source_target_pairs={{0,8},{8,0},{16,24},{24,16},{1,9},{9,1},{17,25},{25,17},{2,10},{10... | collective-permute-start | bytes 165896 | tf_op jit(solution)/shard_map/ppermute | solution.py:616
  344.5 4.3 %collective-permute-start.57 = (f32[16,640]{1,0:T(8,128)S(1)}, f32[16,640]{1,0:T(8,128)S(1)}, u32[]{:S(2)}, u32[]{:S(2)}) collective-permute-start(f32[16,640]{1,0:T(8,128)S(1)} %add.49), channel_id=1, source_target_pairs={{0,2},{1,3},{2,0},{3,1},{4,6},{5,7},{6,4},{7,5},{8,10},{9,11},{10,... | collective-permute-start | bytes 122888 | tf_op jit(solution)/shard_map/ppermute | solution.py:614
  347.3 4.2 %collective-permute-start.47 = (bf16[72,256]{1,0:T(8,128)(2,1)}, bf16[72,256]{1,0:T(8,128)(2,1)S(1)}, u32[]{:S(2)}, u32[]{:S(2)}) collective-permute-start(bf16[72,256]{1,0:T(8,128)(2,1)} %shard_map.337.refs_4_), channel_id=1, source_target_pairs={{0,16},{8,24},{16,0},{24,8},{1,17},{9,25},{17,1},{25,9},{2,18},{10... | collective-permute-start | bytes 110600 | tf_op jit(solution)/shard_map/ppermute | solution.py:616
  348.9 4.5 %collective-permute-start.48 = (bf16[72,256]{1,0:T(8,128)(2,1)}, bf16[72,256]{1,0:T(8,128)(2,1)S(1)}, u32[]{:S(2)}, u32[]{:S(2)}) collective-permute-start(bf16[72,256]{1,0:T(8,128)(2,1)} %shard_map.337.refs_4_), channel_id=1, source_target_pairs={{0,8},{8,0},{16,24},{24,16},{1,9},{9,1},{17,25},{25,17},{2,10},{10... | collective-permute-start | bytes 110600 | tf_op jit(solution)/shard_map/ppermute | solution.py:616
  348.9 5.9 %collective-permute-start.43 = (bf16[72,384]{1,0:T(8,128)(2,1)S(1)}, bf16[72,384]{1,0:T(8,128)(2,1)S(1)}, u32[]{:S(2)}, u32[]{:S(2)}) collective-permute-start(bf16[72,384]{1,0:T(8,128)(2,1)S(1)} %collective-permute-done.41.refs_1_), channel_id=1, source_target_pairs={{0,8},{8,0},{16,24},{24,16},{1,9},{9,1},{17,25},{25,17},{2,10},{10... | collective-permute-start | bytes 165896 | tf_op jit(solution)/shard_map/ppermute | solution.py:616
  351.6 7.1 %collective-permute-start.58 = (f32[16,640]{1,0:T(8,128)S(1)}, f32[16,640]{1,0:T(8,128)S(1)}, u32[]{:S(2)}, u32[]{:S(2)}) collective-permute-start(f32[16,640]{1,0:T(8,128)S(1)} %add.50), channel_id=1, source_target_pairs={{0,4},{1,5},{2,6},{3,7},{4,0},{5,1},{6,2},{7,3},{8,12},{9,13},{10,... | collective-permute-start | bytes 122888 | tf_op jit(solution)/shard_map/ppermute | solution.py:614
  353.4 1.2 collective-permute-start.49
  354.6 5.4 %collective-permute-start.52 = (bf16[120,640]{1,0:T(8,128)(2,1)}, bf16[120,640]{1,0:T(8,128)(2,1)S(1)}, u32[]{:S(2)}, u32[]{:S(2)}) collective-permute-start(bf16[120,640]{1,0:T(8,128)(2,1)} %shard_map.339.refs_0_), channel_id=1, source_target_pairs={{0,8},{8,0},{16,24},{24,16},{1,9},{9,1},{17,25},{25,17},{2,10},{10... | collective-permute-start | bytes 460808 | tf_op jit(solution)/shard_map/ppermute | solution.py:616
  358.5 1.6 collective-permute-start.53
  (47 other events, 372.7 us)
Sparse Core Ops, SparseCore 0:
  162.0 100.4 reduce-scatter.1
